TPU v7x, 512 devices: a whole 4x4x16 slice. The times are simulated.
512 devices in a mesh: frames: 64 (over z, y_hi, core), rows: 8 (over x, y_lo).
Axes of the slice: x: 4, y: 4 (y_hi: 2, y_lo: 2; y = y_hi * 2 + y_lo), z: 16, core: 2. Of those that a mesh axis runs over, the one named last changes fastest.
Arguments:
- coarse_features: bfloat16 [64, 16, 24, 256], P('frames', 'rows'), may hold values from -64 to 64
- fine_features: bfloat16 [64, 64, 96, 128], P('frames', 'rows'), may hold values from -96 to 96
- coarse_weight: bfloat16 [256, 256], replicated, may hold values from -0.375 to 0.375
- fine_weight: bfloat16 [128, 128], replicated, may hold values from -0.5 to 0.5
- grad_refined: float32 [64, 2, 6144], P('frames', None, 'rows'), may hold values from -24 to 24
- grad_back: float32 [64, 2, 384], P('frames', None, 'rows'), may hold values from -192 to 192
Outputs:
- coarse_grad: bfloat16 [64, 16, 24, 256], P('frames', 'rows')
- fine_grad: bfloat16 [64, 64, 96, 128], P('frames', 'rows')
- coarse_weight_grad: float32 [256, 256], replicated
- fine_weight_grad: float32 [128, 128], replicated
All inputs are finite; a program needn't handle non-finite values.
Results may differ from a plain program's by a relative error of at most 0.007.
The roundings to bfloat16 on the way count: a program that leaves them out, or rounds other values in their place, can miss the bound.
Values may be sent and summed in bfloat16 or wider, within the bound.
No kernel may reach another device: no remote copies, remote signals or barrier semaphores. Data moves between devices by JAX's collectives and lax.ppermute only.
A program may use at most 64 MiB of HBM per device.

v0:
```python
import math

import jax
import jax.numpy as jnp
from jax import lax
from jax.sharding import PartitionSpec as P


def padded_2(x, sides, width):
    for axis, dim in sides:
        count, length = (lax.axis_size(axis), x.shape[dim])
        up = [(i, (i + 1) % count) for i in range(count - 1)]
        down = [(j, i) for i, j in up]
        last = lax.slice_in_dim(x, length - width, length, axis=dim)
        leading = lax.slice_in_dim(x, 0, width, axis=dim)
        before = lax.ppermute(last, axis, up)
        after = lax.ppermute(leading, axis, down)
        x = jnp.concatenate([before, x, after], axis=dim)
    return x


def from_behind(value, axis, steps):
    count = lax.axis_size(axis)
    leading, last = (max(0, -steps), min(count, count - steps))
    return lax.ppermute(value, axis, [(source, source + steps) for source in range(leading, last)])


def attend(queries, key_rows, coord_x, coord_y):
    channels = queries.shape[1]
    scores = jnp.einsum(
        "nc,mc->nm", queries, key_rows, preferred_element_type=jnp.float32
    ) / math.sqrt(channels)
    row_top = jnp.max(scores, axis=1)
    exponent = jnp.exp(scores - row_top[:, None])
    totals = jnp.sum(exponent, axis=1)
    chances = exponent / totals[:, None]
    mean_x = jnp.dot(chances, coord_x, precision=lax.Precision.HIGHEST)
    mean_y = jnp.dot(chances, coord_y, precision=lax.Precision.HIGHEST)
    return (chances, row_top, totals, mean_x, mean_y)


def weigh(chances, cot_x, cot_y, mean_x, mean_y, coord_x, coord_y, channels):
    spread = cot_x[:, None] * coord_x[None, :] + cot_y[:, None] * coord_y[None, :]
    centre = cot_x * mean_x + cot_y * mean_y
    return (chances * (spread - centre[:, None]) / math.sqrt(channels)).astype(jnp.bfloat16)


def band_take(square):
    leading = square.shape[:-2]
    flattened = square.reshape(leading + (384,))
    flattened = jnp.pad(flattened, [(0, 0)] * len(leading) + [(0, 16)])
    return flattened.reshape(leading + (16, 25))[..., :9]


def band_put(band_part):
    leading = band_part.shape[:-2]
    widened = jnp.pad(band_part, [(0, 0)] * len(leading) + [(0, 0), (0, 16)])
    return widened.reshape(leading + (400,))[..., :384].reshape(leading + (16, 24))


def window_grads(local_a, next_rows, grad_x, grad_y):
    height, columns, channels = local_a.shape
    blocks = columns // 16
    root_depth = math.sqrt(channels)
    padded = jnp.pad(next_rows, ((0, 0), (4, 12), (0, 0)))
    leading = padded[:, :columns].reshape(height + 8, blocks, 16, channels)
    trailing = padded[:, 16 : columns + 16].reshape(height + 8, blocks, 16, channels)[:, :, :8]
    key_blocks = jnp.concatenate([leading, trailing], axis=2)
    query_blocks = local_a.reshape(height, blocks, 16, channels)
    scores = (
        jnp.stack(
            [
                band_take(
                    jnp.einsum(
                        "rbqc,rbkc->rbqk",
                        query_blocks,
                        key_blocks[offset : offset + height],
                        preferred_element_type=jnp.float32,
                    )
                )
                for offset in range(9)
            ],
            axis=3,
        )
        / root_depth
    )
    steps_axis = jnp.arange(9, dtype=jnp.float32) - 4.0
    shift_y = steps_axis[:, None]
    shift_x = steps_axis[None, :]
    row_top = jnp.max(scores, axis=(3, 4), keepdims=True)
    exponent = jnp.exp(scores - row_top)
    chances = exponent / jnp.sum(exponent, axis=(3, 4), keepdims=True)
    mean_x = jnp.sum(chances * shift_x, axis=(3, 4))
    mean_y = jnp.sum(chances * shift_y, axis=(3, 4))
    block_x = grad_x.reshape(height, blocks, 16)
    block_y = grad_y.reshape(height, blocks, 16)
    spread = block_x[..., None, None] * shift_x + block_y[..., None, None] * shift_y
    centre = block_x * mean_x + block_y * mean_y
    weights = (chances * (spread - centre[..., None, None]) / root_depth).astype(jnp.bfloat16)
    query_grad = jnp.zeros((height, blocks, 16, channels), jnp.float32)
    key_grad = jnp.zeros((height + 8, blocks, 24, channels), jnp.float32)
    for offset in range(9):
        placed = band_put(weights[:, :, :, offset, :])
        query_grad = query_grad + jnp.einsum(
            "rbqk,rbkc->rbqc",
            placed,
            key_blocks[offset : offset + height],
            preferred_element_type=jnp.float32,
        )
        key_grad = key_grad.at[offset : offset + height].add(
            jnp.einsum("rbqk,rbqc->rbkc", placed, query_blocks, preferred_element_type=jnp.float32)
        )
    first_part = key_grad[:, :, :16].reshape(height + 8, columns, channels)
    second = jnp.pad(key_grad[:, :, 16:], ((0, 0), (0, 0), (0, 8), (0, 0))).reshape(
        height + 8, columns, channels
    )
    padded_grad = jnp.pad(first_part, ((0, 0), (0, 16), (0, 0))) + jnp.pad(
        second, ((0, 0), (16, 0), (0, 0))
    )
    return (query_grad.reshape(height, columns, channels), padded_grad[:, 4 : 4 + columns])


def local(coarse_features, fine_features, coarse_weight, fine_weight, grad_refined, grad_back):
    band_rows, columns, channels = (
        coarse_features.shape[1],
        coarse_features.shape[2],
        coarse_features.shape[3],
    )
    fine_rows, fine_columns, fine_channels = (
        fine_features.shape[1],
        fine_features.shape[2],
        fine_features.shape[3],
    )
    cell_count = band_rows * columns
    coarse_own = coarse_features[0].reshape(cell_count, channels)
    fine_own = fine_features[0].reshape(fine_rows * fine_columns, fine_channels)
    query_a = jnp.dot(coarse_own, coarse_weight, preferred_element_type=jnp.float32).astype(
        jnp.bfloat16
    )
    local_a = jnp.dot(fine_own, fine_weight, preferred_element_type=jnp.float32).astype(
        jnp.bfloat16
    )
    fine_length = 4 * fine_columns * fine_channels
    outgoing = jnp.concatenate(
        [local_a.reshape(band_rows, fine_length), query_a.reshape(band_rows, columns * channels)],
        axis=1,
    )
    rimmed = padded_2(outgoing, (("rows", 0),), 1)
    arrived = from_behind(rimmed, "frames", -1)
    next_rows = arrived[:, :fine_length].reshape(fine_rows + 8, fine_columns, fine_channels)
    query_b = arrived[1 : band_rows + 1, fine_length:].reshape(cell_count, channels)
    keys_a, keys_b = (
        lax.all_gather(query_a, "rows", axis=0, tiled=True),
        lax.all_gather(query_b, "rows", axis=0, tiled=True),
    )
    positions = jnp.arange(keys_a.shape[0], dtype=jnp.int32)
    coord_x = (positions % columns).astype(jnp.float32)
    coord_y = (positions // columns).astype(jnp.float32)
    refined_cot = grad_refined[0]
    pooled = 4.0 * jnp.sum(refined_cot.reshape(2, band_rows, 4, columns, 4), axis=(2, 4)).reshape(
        2, cell_count
    )
    back_cot = grad_back[0]
    chances_f, top_f, total_f, mean_fx, mean_fy = attend(query_a, keys_b, coord_x, coord_y)
    forward_w = weigh(chances_f, pooled[0], pooled[1], mean_fx, mean_fy, coord_x, coord_y, channels)
    chances_b, top_b, total_b, mean_bx, mean_by = attend(query_b, keys_a, coord_x, coord_y)
    backward_w = weigh(
        chances_b, back_cot[0], back_cot[1], mean_bx, mean_by, coord_x, coord_y, channels
    )
    own_a = jnp.dot(forward_w, keys_b, preferred_element_type=jnp.float32)
    own_b = jnp.dot(backward_w, keys_a, preferred_element_type=jnp.float32)
    term_b = jnp.einsum("nm,nc->mc", forward_w, query_a, preferred_element_type=jnp.float32)
    term_a = jnp.einsum("nm,nc->mc", backward_w, query_b, preferred_element_type=jnp.float32)
    summed = lax.psum_scatter(
        jnp.concatenate([term_b, term_a], axis=1), "rows", scatter_dimension=0, tiled=True
    )
    key_b = summed[:, :channels]
    key_a = summed[:, channels:]
    grad_a = own_a + key_a
    grad_b = own_b + key_b
    refined_grid = refined_cot.reshape(2, fine_rows, fine_columns)
    local_grad, rim_grad = window_grads(
        local_a.reshape(fine_rows, fine_columns, fine_channels),
        next_rows,
        refined_grid[0],
        refined_grid[1],
    )
    fine_back = rim_grad.astype(jnp.bfloat16).reshape(band_rows + 2, fine_length)
    coarse_back = jnp.pad(
        grad_b.astype(jnp.bfloat16).reshape(band_rows, columns * channels), ((1, 1), (0, 0))
    )
    widened = padded_2(jnp.concatenate([fine_back, coarse_back], axis=1), (("rows", 0),), 1)
    returned = from_behind(widened, "frames", 1)
    incoming = returned[:, :fine_length].astype(jnp.float32)
    rim_sum = (
        incoming[2 : band_rows + 2]
        + jnp.pad(incoming[0:1], ((0, band_rows - 1), (0, 0)))
        + jnp.pad(incoming[band_rows + 3 : band_rows + 4], ((band_rows - 1, 0), (0, 0)))
    )
    fine_total = (
        local_grad.reshape(fine_rows * fine_columns, fine_channels)
        + rim_sum.reshape(fine_rows * fine_columns, fine_channels)
    ).astype(jnp.bfloat16)
    coarse_in = (
        returned[2 : band_rows + 2, fine_length:].astype(jnp.float32).reshape(cell_count, channels)
    )
    coarse_total = (grad_a + coarse_in).astype(jnp.bfloat16)
    coarse_grad = (
        jnp.einsum("nd,cd->nc", coarse_total, coarse_weight, preferred_element_type=jnp.float32)
        .astype(jnp.bfloat16)
        .reshape(1, band_rows, columns, channels)
    )
    fine_grad = (
        jnp.einsum("nd,cd->nc", fine_total, fine_weight, preferred_element_type=jnp.float32)
        .astype(jnp.bfloat16)
        .reshape(1, fine_rows, fine_columns, fine_channels)
    )
    partial_coarse = jnp.einsum(
        "nc,nd->cd", coarse_own, coarse_total, preferred_element_type=jnp.float32
    )
    partial_fine = jnp.einsum("nc,nd->cd", fine_own, fine_total, preferred_element_type=jnp.float32)
    weight_totals = lax.psum((partial_coarse, partial_fine), ("frames", "rows"))
    frame_count = lax.axis_size("frames")
    return (coarse_grad, fine_grad, weight_totals[0] / frame_count, weight_totals[1] / frame_count)


def solution(mesh):
    in_specs = (
        P("frames", "rows", None, None),
        P("frames", "rows", None, None),
        P(),
        P(),
        P("frames", None, "rows"),
        P("frames", None, "rows"),
    )
    out_specs = (P("frames", "rows", None, None), P("frames", "rows", None, None), P(), P())
    return jax.shard_map(local, mesh=mesh, in_specs=in_specs, out_specs=out_specs, check_vma=False)
```

profile of v0, /device:TPU:1, one launch (start us, length us, event | category | flops | bytes accessed | tf_op | source)
XLA Modules:
  0.0 741.7 jit_solution(13359719974634137960)
XLA Ops:
  9.9 4.0 collective-permute-start
  17.1 3.6 collective-permute-done.1
  21.4 7.2 collective-permute-start.2
  31.2 26.8 %all_gather.7 = bf16[384,256]{1,0:T(8,128)(2,1)} all-gather(bf16[48,256]{1,0:T(8,128)(2,1)S(1)} %convolution_convert_fusion.3), channel_id=1, replica_groups=mesh['frames'=64,'rows'=8] {'rows'}, dimensions={0}, use_global_device_ids=true | all-gather | bytes 221184 | tf_op jit(solution)/shard_map/all_gather | solution.py:153
  75.9 1.9 reshape.575
  77.8 1.9 fusion.29
  79.6 1.8 fusion.28
  81.5 1.8 fusion.27
  83.2 1.8 fusion.26
  88.2 2.6 multiply_reduce_fusion.2
  96.0 3.9 multiply_convert_fusion
  108.7 1.7 reshape.579
  113.8 1.7 reshape.581
  119.0 1.7 reshape.583
  124.1 1.7 reshape.585
  129.2 1.7 reshape.587
  136.7 1.7 pad.121
  140.2 1.7 reshape.593
  142.8 22.8 %all_gather.6 = bf16[384,256]{1,0:T(8,128)(2,1)S(1)} all-gather(bf16[48,256]{1,0:T(8,128)(2,1)S(1)} %reshape.554), channel_id=1, replica_groups=mesh['frames'=64,'rows'=8] {'rows'}, dimensions={0}, use_global_device_ids=true | all-gather | bytes 221184 | tf_op jit(solution)/shard_map/all_gather | solution.py:154
  185.7 43.1 %reduce-scatter.2.cloned.1.call-done = f32[48,512]{1,0:T(8,128)} async-done(((f32[384,512]{1,0:T(8,128)}), f32[48,512]{1,0:T(8,128)}) %reduce-scatter.2.cloned.1.call-update) | async-done | bytes 98320 | tf_op jit(solution)/shard_map/reduce_scatter | solution.py:174
  234.4 3.8 collective-permute-done.4
  239.0 11.3 %collective-permute-start.5 = (bf16[6,55296]{1,0:T(8,128)(2,1)S(1)}, bf16[6,55296]{1,0:T(8,128)(2,1)S(1)}, u32[]{:S(2)}, u32[]{:S(2)}) collective-permute-start(bf16[6,55296]{1,0:T(8,128)(2,1)S(1)} %pad_maximum_fusion), channel_id=1, source_target_pairs={{0,8},{8,16},{16,24},{24,32},{32,40},{40,48},{48,56},{56,64},{64,7... | collective-permute-start | bytes 1990664 | tf_op jit(solution)/shard_map/ppermute | solution.py:25
  251.1 8.9 %collective-permute-done.5 = bf16[6,55296]{1,0:T(8,128)(2,1)S(1)} collective-permute-done((bf16[6,55296]{1,0:T(8,128)(2,1)S(1)}, bf16[6,55296]{1,0:T(8,128)(2,1)S(1)}, u32[]{:S(2)}, u32[]{:S(2)}) %collective-permute-start.5) | collective-permute-done | bytes 663584 | tf_op jit(solution)/shard_map/ppermute | solution.py:25
  267.3 464.1 %all-reduce.28.cloned.1.call-done = (f32[256,256]{0,1:T(8,128)}, f32[128,128]{0,1:T(8,128)}) async-done(((f32[256,256]{0,1:T(8,128)}, f32[128,128]{0,1:T(8,128)}), (f32[256,256]{0,1:T(8,128)}, f32[128,128]{0,1:T(8,128)})) %all-reduce.28.cloned.1.call-update) | async-done | bytes 327696 | tf_op jit(solution)/shard_map/psum | solution.py:222
  (264 shorter events, 103.2 us)
Async XLA Ops:
  7.2 51.4 %copy-start.36 = (f32[1,2,48]{2,1,0:T(2,128)S(1)}, f32[1,2,48]{2,1,0:T(2,128)}, u32[]{:S(2)}) copy-start(f32[1,2,48]{2,1,0:T(2,128)} %param.29) | copy-start | bytes 1156
  7.2 221.6 %reduce-scatter.2.cloned.1.call-start = ((), (), s32[]{:S(2)}) async-start(), calls=%async_computation.1 | async-start | bytes 884736 | tf_op jit(solution)/shard_map/reduce_scatter | solution.py:174
  9.9 7.2 collective-permute-start
  13.9 6.7 collective-permute-start.1
  21.4 37.8 %collective-permute-start.2 = (bf16[4,55296]{1,0:T(4,128)(2,1)S(1)}, bf16[4,55296]{1,0:T(4,128)(2,1)S(1)}, u32[]{:S(2)}, u32[]{:S(2)}) collective-permute-start(bf16[4,55296]{1,0:T(4,128)(2,1)S(1)} %pad_maximum_fusion.2), channel_id=1, source_target_pairs={{8,0},{16,8},{24,16},{32,24},{40,32},{48,40},{56,48},{64,56},{72,6... | collective-permute-start | bytes 1327112 | tf_op jit(solution)/shard_map/ppermute | solution.py:25
  134.5 44.4 %copy-start.6 = (bf16[8,6,16,24]{3,2,0,1:T(8,128)(2,1)}, bf16[8,6,16,24]{3,2,0,1:T(8,128)(2,1)S(1)}, u32[]{:S(2)}) copy-start(bf16[8,6,16,24]{3,2,0,1:T(8,128)(2,1)S(1)} %reshape.589) | copy-start | bytes 110596
  136.7 42.6 %copy-start.8 = (bf16[8,6,16,24]{3,2,0,1:T(8,128)(2,1)}, bf16[8,6,16,24]{3,2,0,1:T(8,128)(2,1)S(1)}, u32[]{:S(2)}) copy-start(bf16[8,6,16,24]{3,2,0,1:T(8,128)(2,1)S(1)} %reshape.591) | copy-start | bytes 110596
  142.7 24.7 %copy-start.30 = (bf16[48,256]{1,0:T(8,128)(2,1)}, bf16[48,256]{1,0:T(8,128)(2,1)S(1)}, u32[]{:S(2)}) copy-start(bf16[48,256]{1,0:T(8,128)(2,1)S(1)} %reshape.554) | copy-start | bytes 73732
  174.3 557.2 %all-reduce.28.cloned.1.call-start = ((), (), s32[]{:S(2)}) async-start(), calls=%async_computation.2 | async-start | bytes 655360 | tf_op jit(solution)/shard_map/psum | solution.py:222
  181.2 47.6 %copy-start.5 = (f32[48,384]{1,0:T(8,128)S(1)}, f32[48,384]{1,0:T(8,128)}, u32[]{:S(2)}) copy-start(f32[48,384]{1,0:T(8,128)} %copy-done.4) | copy-start | bytes 221188
  181.2 47.6 %copy-start.40 = (f32[48]{0:T(128)S(1)}, f32[48]{0:T(128)}, u32[]{:S(2)}) copy-start(f32[48]{0:T(128)} %copy-done.39) | copy-start | bytes 580
  181.2 47.6 %copy-start.41 = (f32[48]{0:T(128)S(1)}, f32[48]{0:T(128)}, u32[]{:S(2)}) copy-start(f32[48]{0:T(128)} %get-tuple-element.159) | copy-start | bytes 580
  181.2 47.6 %copy-start.42 = (f32[48]{0:T(128)S(1)}, f32[48]{0:T(128)}, u32[]{:S(2)}) copy-start(f32[48]{0:T(128)} %get-tuple-element.160) | copy-start | bytes 580
  183.6 49.2 %copy-start.13 = (bf16[8,6,16,24]{3,2,0,1:T(8,128)(2,1)S(1)}, bf16[8,6,16,24]{3,2,0,1:T(8,128)(2,1)}, u32[]{:S(2)}) copy-start(bf16[8,6,16,24]{3,2,0,1:T(8,128)(2,1)} %reshape.587) | copy-start | bytes 110596
  183.9 44.9 %copy-start.22 = (bf16[384,256]{1,0:T(8,128)(2,1)S(1)}, bf16[384,256]{1,0:T(8,128)(2,1)}, u32[]{:S(2)}) copy-start(bf16[384,256]{1,0:T(8,128)(2,1)} %all_gather.7) | copy-start | bytes 589828
  185.1 65.2 %copy-start.7 = (bf16[8,6,16,24]{3,2,0,1:T(8,128)(2,1)S(1)}, bf16[8,6,16,24]{3,2,0,1:T(8,128)(2,1)}, u32[]{:S(2)}) copy-start(bf16[8,6,16,24]{3,2,0,1:T(8,128)(2,1)} %copy-done.6) | copy-start | bytes 110596
  185.4 65.2 %copy-start.9 = (bf16[8,6,16,24]{3,2,0,1:T(8,128)(2,1)S(1)}, bf16[8,6,16,24]{3,2,0,1:T(8,128)(2,1)}, u32[]{:S(2)}) copy-start(bf16[8,6,16,24]{3,2,0,1:T(8,128)(2,1)} %copy-done.8) | copy-start | bytes 110596
  185.7 65.2 %copy-start.11 = (bf16[8,6,16,24]{3,2,0,1:T(8,128)(2,1)S(1)}, bf16[8,6,16,24]{3,2,0,1:T(8,128)(2,1)}, u32[]{:S(2)}) copy-start(bf16[8,6,16,24]{3,2,0,1:T(8,128)(2,1)} %reshape.593) | copy-start | bytes 110596
  230.3 4.2 collective-permute-start.3
  231.6 6.7 collective-permute-start.4
  239.0 22.3 %copy-start.44 = (pred[2]{0:T(512)(128)(4,1)S(1)}, pred[2]{0:T(512)(128)(4,1)}, u32[]{:S(2)}) copy-start(pred[2]{0:T(512)(128)(4,1)} %constant.297.clone.1) | copy-start | bytes 10
  239.0 21.0 %collective-permute-start.5 = (bf16[6,55296]{1,0:T(8,128)(2,1)S(1)}, bf16[6,55296]{1,0:T(8,128)(2,1)S(1)}, u32[]{:S(2)}, u32[]{:S(2)}) collective-permute-start(bf16[6,55296]{1,0:T(8,128)(2,1)S(1)} %pad_maximum_fusion), channel_id=1, source_target_pairs={{0,8},{8,16},{16,24},{24,32},{32,40},{40,48},{48,56},{56,64},{64,7... | collective-permute-start | bytes 1990664 | tf_op jit(solution)/shard_map/ppermute | solution.py:25
  251.1 13.3 %copy-start.3 = (f32[48,384]{1,0:T(8,128)S(1)}, f32[48,384]{1,0:T(8,128)}, u32[]{:S(2)}) copy-start(f32[48,384]{1,0:T(8,128)} %copy-done.2) | copy-start | bytes 221188
  251.1 13.5 %copy-start.35 = (bf16[1,2,24,256]{3,2,1,0:T(8,128)(2,1)S(1)}, bf16[1,2,24,256]{3,2,1,0:T(8,128)(2,1)}, u32[]{:S(2)}) copy-start(bf16[1,2,24,256]{3,2,1,0:T(8,128)(2,1)} %param.24) | copy-start | bytes 73732
  (29 other events, 156.7 us)
Sparse Core Ops, SparseCore 0:
  174.4 54.3 reduce-scatter.1
  266.7 464.7 all-reduce.27
where the time goes:
time: 744 us; the launch traced here: 742 us
  waiting for transfers between devices  525 us (71%)
  local copies, waits for them, and re-layouts  81.1 us (11%)
  blocking collectives  49.6 us (7%)
  starting transfers between devices  26.5 us (4%)
  matrix products  25.8 us (3%)
  other arithmetic  18.6 us (3%)
  between operations  15.2 us (2%)
    psum x1, waiting for transfers between devices, local(): weight_totals = lax.psum((partial_coarse, partial_fine), ('frames', 'rows'))  464 us
    reduce_scatter x1, waiting for transfers between devices, local(): lax.psum_scatter(jnp.concatenate([term_b, term_a], axis=1), 'rows', scatt...  43.1 us
    all_gather x1, blocking collectives, local(): lax.all_gather(query_a, 'rows', axis=0, tiled=True)  26.8 us
    reshape x18, local copies, waits for them, and re-layouts, band_put(): widened.reshape(leading + (400,))[..., :384].reshape(leading + (16, 24))  23.6 us
    all_gather x1, blocking collectives, local(): lax.all_gather(query_b, 'rows', axis=0, tiled=True)  22.8 us
    ppermute x2, starting transfers between devices, from_behind(): lax.ppermute(value, axis, [(source, source + steps) for source in range(l...  18.5 us
  transfers between devices with their start and end apart: 8, of which 6 were waited for; matrix products, arithmetic and copies ran while one was open for 2% of the time, Pallas kernels for 0%

commit v1 on v0

v1 whole, which is shorter than its diff:
```python
import math

import jax
import jax.numpy as jnp
from jax import lax
from jax.experimental import pallas as pl
from jax.experimental.pallas import tpu as pltpu
from jax.sharding import Mesh, PartitionSpec as P

F32 = jnp.float32
BF16 = jnp.bfloat16
FRAMES = ("z", "yh", "core")
ROWS = ("x", "yl")
PLANE = ("yh", "core", "x", "yl")
ALL = FRAMES + ROWS
N_FRAMES, N_ROWS, N_PLANE, N_Z = 64, 8, 32, 16
COLS = 112
SPAN = 9 * COLS
VMEM = pl.BlockSpec(memory_space=pltpu.VMEM)
SMEM = pl.BlockSpec(memory_space=pltpu.SMEM)


def call(body, outs, scratch=(), n_smem=0, n_in=0, flops=0, nbytes=0):
    return pl.pallas_call(
        body,
        out_shape=outs,
        in_specs=[SMEM] * n_smem + [VMEM] * n_in,
        out_specs=jax.tree.map(lambda _: VMEM, outs),
        scratch_shapes=list(scratch),
        compiler_params=pltpu.CompilerParams(vmem_limit_bytes=40 * 1024 * 1024),
        cost_estimate=pl.CostEstimate(flops=flops, bytes_accessed=nbytes, transcendentals=0),
    )


def shape(*dims, dtype=BF16):
    return jax.ShapeDtypeStruct(dims, dtype)


def mm(a, b):
    return lax.dot_general(a, b, (((1,), (0,)), ((), ())), preferred_element_type=F32)


def mm_nt(a, b):
    return lax.dot_general(a, b, (((1,), (1,)), ((), ())), preferred_element_type=F32)


def mm_tn(a, b):
    return lax.dot_general(a, b, (((0,), (0,)), ((), ())), preferred_element_type=F32)


def split3(value):
    hi = value.astype(BF16)
    rest = value - hi.astype(F32)
    mid = rest.astype(BF16)
    low = (rest - mid.astype(F32)).astype(BF16)
    return hi, mid, low


def iota(dims, axis):
    return lax.broadcasted_iota(jnp.int32, dims, axis)


def prepare_body(coarse, refined, back, out, cots):
    cell = iota((768, 128), 0)
    low = (cell >= 384).astype(jnp.int32)
    cell = cell - 384 * low
    line = (cell >= 96).astype(jnp.int32) + (cell >= 192).astype(jnp.int32) + (cell >= 288).astype(jnp.int32)
    column = lax.shift_right_logical(cell - 96 * line, 2)
    pool = (iota((768, 128), 1) == column + 24 * low).astype(F32).astype(BF16)
    hi, mid, rest = split3(refined[...])
    cots[...] = jnp.zeros_like(cots)
    cots[0:2, 0:128] = 4.0 * (mm(hi, pool) + (mm(mid, pool) + mm(rest, pool)))
    cots[2:4, 0:48] = back[...]
    hi, mid, rest = split3(cots[0:4, :])
    cots[0:4, :] = hi.astype(F32)
    cots[4:8, :] = mid.astype(F32)
    cots[8:12, :] = rest.astype(F32)
    packed = cots[...].astype(BF16)
    for band in range(N_ROWS):
        out[band, 0:48, :] = coarse[...]
        out[band, 48:64, :] = packed


def fine_body(own, middle, above, below, weight, refined, first, mid_out, up_out, down_out, partial,
              queries, keys, key_grad, turned):
    scale = 1.0 / math.sqrt(128.0)
    w = weight[...]
    queries[...] = mm(own[...], w).astype(BF16)
    blank = jnp.zeros((COLS - 96, 128), BF16)
    for row in range(16):
        if row < 4:
            source = above[row * 96 : row * 96 + 96, :]
        elif row < 12:
            source = middle[(row - 4) * 96 : (row - 4) * 96 + 96, :]
        else:
            source = below[(row - 12) * 96 : (row - 12) * 96 + 96, :]
        keys[row * COLS : row * COLS + 96, :] = mm(source, w).astype(BF16)
        keys[row * COLS + 96 : row * COLS + COLS, :] = blank
    key_grad[...] = jnp.zeros_like(key_grad)
    turned[...] = jnp.zeros_like(turned)
    turned[0:2, :] = refined[...]
    cot = jnp.transpose(turned[...], (1, 0))
    lane = iota((1, SPAN), 1).astype(F32)
    line = jnp.floor((lane + 0.5) * (1.0 / COLS))
    column = lane - line * COLS
    step_y = line - 4.0
    step_x = column - iota((96, SPAN), 0).astype(F32)
    step_x = jnp.where(step_x > 50.0, step_x - COLS, step_x)
    inside = jnp.abs(step_x) < 4.5
    for row in range(8):
        q = queries[row * 96 : row * 96 + 96, :]
        k = keys[row * COLS : row * COLS + SPAN, :]
        s = jnp.where(inside, mm_nt(q, k) * scale, -1e30)
        e = jnp.exp(s - jnp.max(s, axis=1, keepdims=True))
        inverse = 1.0 / jnp.sum(e, axis=1, keepdims=True)
        mean_x = jnp.sum(e * step_x, axis=1, keepdims=True) * inverse
        mean_y = jnp.sum(e * step_y, axis=1, keepdims=True) * inverse
        gx = cot[row * 96 : row * 96 + 96, 0:1]
        gy = cot[row * 96 : row * 96 + 96, 1:2]
        factor = inverse * scale
        bend = gx * step_x + gy * step_y - (gx * mean_x + gy * mean_y)
        weights = (e * bend * factor).astype(BF16)
        first[row * 96 : row * 96 + 96, :] = mm(weights, k)
        key_grad[row * COLS : row * COLS + SPAN, :] += mm_tn(weights, q)
    for row in range(16):
        rounded = key_grad[row * COLS : row * COLS + 96, :].astype(BF16)
        if row < 4:
            up_out[row * 96 : row * 96 + 96, :] = rounded
        elif row < 12:
            mid_out[(row - 4) * 96 : (row - 4) * 96 + 96, :] = rounded
        else:
            down_out[(row - 12) * 96 : (row - 12) * 96 + 96, :] = rounded
    hi = first[...].astype(BF16)
    low = (first[...] - hi.astype(F32)).astype(BF16)
    total = mm_tn(own[...], hi) + mm_tn(own[...], low)
    total = total + mm_tn(middle[...], mid_out[...])
    partial[...] = total + mm_tn(above[...], up_out[...]) + mm_tn(below[...], down_out[...])


def coarse_body(position, here, there, weight, fine_partial, first, second, send,
                forward, backward, both, packed):
    band = position[0]
    w = weight[...]
    qa = mm(here[:, 0:48, :].reshape(384, 256), w).astype(BF16)
    qb = mm(there[:, 0:48, :].reshape(384, 256), w).astype(BF16)
    flat = jnp.zeros((16, 384), F32)
    upright = jnp.zeros((384, 16), F32)
    for source in range(N_ROWS):
        cots = here[source, 48:64, 0:128]
        place = (iota((128, 384), 1) - iota((128, 384), 0) == 48 * source).astype(F32).astype(BF16)
        turned = (iota((384, 128), 0) - iota((384, 128), 1) == 48 * source).astype(F32).astype(BF16)
        flat = flat + mm(cots, place)
        upright = upright + mm_nt(turned, cots)
    cf_x = upright[:, 0:1] + (upright[:, 4:5] + upright[:, 8:9])
    cf_y = upright[:, 1:2] + (upright[:, 5:6] + upright[:, 9:10])
    cb_x = flat[2:3, :] + (flat[6:7, :] + flat[10:11, :])
    cb_y = flat[3:4, :] + (flat[7:8, :] + flat[11:12, :])
    lane = iota((1, 384), 1).astype(F32)
    lane_y = jnp.floor((lane + 0.5) * (1.0 / 24.0))
    lane_x = lane - 24.0 * lane_y
    line = iota((384, 1), 0).astype(F32)
    line_y = jnp.floor((line + 0.5) * (1.0 / 24.0))
    line_x = line - 24.0 * line_y
    s = mm_nt(qa, qb) * (1.0 / 16.0)
    e = jnp.exp(s - jnp.max(s, axis=1, keepdims=True))
    inverse = 1.0 / jnp.sum(e, axis=1, keepdims=True)
    mean_x = jnp.sum(e * lane_x, axis=1, keepdims=True) * inverse
    mean_y = jnp.sum(e * lane_y, axis=1, keepdims=True) * inverse
    bend = cf_x * lane_x + cf_y * lane_y - (cf_x * mean_x + cf_y * mean_y)
    forward_w = (e * bend * (inverse * (1.0 / 16.0))).astype(BF16)
    forward[...] = forward_w
    e = jnp.exp(s - jnp.max(s, axis=0, keepdims=True))
    inverse = 1.0 / jnp.sum(e, axis=0, keepdims=True)
    mean_x = jnp.sum(e * line_x, axis=0, keepdims=True) * inverse
    mean_y = jnp.sum(e * line_y, axis=0, keepdims=True) * inverse
    bend = cb_x * line_x + cb_y * line_y - (cb_x * mean_x + cb_y * mean_y)
    backward_w = (e * bend * (inverse * (1.0 / 16.0))).astype(BF16)
    backward[...] = backward_w
    both[...] = mm_tn(forward_w, qa) + mm_tn(backward_w, qa)
    mine = pl.ds(pl.multiple_of(band * 48, 16), 48)
    own_first = mm(forward[mine, :], qb) + mm(backward[mine, :], qb)
    own_second = both[mine, :].astype(BF16)
    first[...] = own_first
    second[...] = own_second
    hi = own_first.astype(BF16)
    low = (own_first - hi.astype(F32)).astype(BF16)
    f_here = here[band, 0:48, :]
    total = mm_tn(f_here, hi) + mm_tn(f_here, low) + mm_tn(there[band, 0:48, :], own_second)
    packed[:, 0:8, :] = total[:, 0:128].reshape(N_PLANE, 8, 128)
    packed[:, 8:16, :] = total[:, 128:256].reshape(N_PLANE, 8, 128)
    for chunk in range(N_PLANE):
        packed[chunk, 16:20, :] = fine_partial[4 * chunk : 4 * chunk + 4, :]
    send[...] = packed[...][:, 0:20, :].astype(BF16)


def sum_body(parts, out):
    total = parts[0].astype(F32)
    for source in range(1, parts.shape[0]):
        total = total + parts[source].astype(F32)
    rounded = total.astype(BF16)
    for target in range(out.shape[0]):
        out[target] = rounded


def unpack_body(parts, coarse, fine):
    values = parts[...].astype(F32) * (1.0 / N_FRAMES)
    coarse[:, 0:128] = values[:, 0:8, :].reshape(256, 128)
    coarse[:, 128:256] = values[:, 8:16, :].reshape(256, 128)
    for chunk in range(N_PLANE):
        fine[4 * chunk : 4 * chunk + 4, :] = values[chunk, 16:20, :]


def finish_body(first, middle, from_above, from_below, weight, coarse_first, coarse_second, coarse_weight,
                fine_out, coarse_out):
    total = first[...] + middle[...].astype(F32)
    w = weight[...]
    top = (total[0:384, :] + from_above[...].astype(F32)).astype(BF16)
    bottom = (total[384:768, :] + from_below[...].astype(F32)).astype(BF16)
    fine_out[0:384, :] = mm_nt(top, w).astype(BF16)
    fine_out[384:768, :] = mm_nt(bottom, w).astype(BF16)
    dq = (coarse_first[...] + coarse_second[...].astype(F32)).astype(BF16)
    coarse_out[...] = mm_nt(dq, coarse_weight[...]).astype(BF16)


def shifted(value, frames, rows):
    pairs = [
        (f * N_ROWS + r, (f + frames) * N_ROWS + r + rows)
        for f in range(max(0, -frames), min(N_FRAMES, N_FRAMES - frames))
        for r in range(max(0, -rows), min(N_ROWS, N_ROWS - rows))
    ]
    return lax.ppermute(value, ALL, pairs)


def local(coarse_features, fine_features, coarse_weight, fine_weight, grad_refined, grad_back):
    coarse_own = coarse_features.reshape(48, 256)
    fine_own = fine_features.reshape(768, 128)
    refined = grad_refined.reshape(2, 768)
    band = lax.axis_index(ROWS).astype(jnp.int32).reshape(1)
    middle = shifted(fine_own, -1, 0)
    above = shifted(fine_own[384:768], -1, 1)
    below = shifted(fine_own[0:384], -1, -1)
    outgoing = call(prepare_body, shape(N_ROWS, 64, 256), [pltpu.VMEM((16, 256), F32)], n_in=3,
                    flops=10**8, nbytes=10**6)(coarse_own, refined, grad_back.reshape(2, 48))
    here = lax.all_to_all(outgoing, ROWS, 0, 0, tiled=True)
    there = shifted(here, -1, 0)
    first, mid_out, up_out, down_out, fine_partial = call(
        fine_body,
        (shape(768, 128, dtype=F32), shape(768, 128), shape(384, 128), shape(384, 128), shape(128, 128, dtype=F32)),
        [
            pltpu.VMEM((768, 128), BF16),
            pltpu.VMEM((16 * COLS, 128), BF16),
            pltpu.VMEM((16 * COLS, 128), F32),
            pltpu.VMEM((8, 768), F32),
        ],
        n_in=6, flops=10**9, nbytes=4 * 10**6,
    )(fine_own, middle, above, below, fine_weight, refined)
    back_up = shifted(up_out, 1, -1)
    back_down = shifted(down_out, 1, 1)
    back_mid = shifted(mid_out, 1, 0)
    coarse_first, coarse_second, send = call(
        coarse_body,
        (shape(48, 256, dtype=F32), shape(48, 256), shape(N_PLANE, 20, 128)),
        [
            pltpu.VMEM((384, 384), BF16),
            pltpu.VMEM((384, 384), BF16),
            pltpu.VMEM((384, 256), F32),
            pltpu.VMEM((N_PLANE, 24, 128), F32),
        ],
        n_smem=1, n_in=4, flops=10**9, nbytes=2 * 10**6,
    )(band, here, there, coarse_weight, fine_partial)
    back_coarse = shifted(coarse_second, 1, 0)
    parts = lax.all_to_all(send, PLANE, 0, 0, tiled=True)
    copies = call(sum_body, shape(N_Z, 20, 128), n_in=1, nbytes=10**6)(parts)
    parts = lax.all_to_all(copies, "z", 0, 0, tiled=True)
    copies = call(sum_body, shape(N_PLANE, 20, 128), n_in=1, nbytes=10**6)(parts)
    parts = lax.all_to_all(copies, PLANE, 0, 0, tiled=True)
    coarse_total, fine_total = call(
        unpack_body, (shape(256, 256, dtype=F32), shape(128, 128, dtype=F32)), n_in=1, nbytes=10**6
    )(parts)
    fine_grad, coarse_grad = call(
        finish_body, (shape(768, 128), shape(48, 256)), n_in=8, flops=10**8, nbytes=10**6
    )(first, back_mid, back_down, back_up, fine_weight, coarse_first, back_coarse, coarse_weight)
    return (
        coarse_grad.reshape(coarse_features.shape),
        fine_grad.reshape(fine_features.shape),
        coarse_total,
        fine_total,
    )


def solution(mesh):
    fine_mesh = Mesh(mesh.devices.reshape(16, 2, 2, 4, 2), ALL)
    in_specs = (
        P(FRAMES, ROWS, None, None),
        P(FRAMES, ROWS, None, None),
        P(),
        P(),
        P(FRAMES, None, ROWS),
        P(FRAMES, None, ROWS),
    )
    out_specs = (P(FRAMES, ROWS, None, None), P(FRAMES, ROWS, None, None), P(), P())
    return jax.shard_map(local, mesh=fine_mesh, in_specs=in_specs, out_specs=out_specs, check_vma=False)
```

time: 744 us -> 104 us (0.14)
  the two profiles are of different devices: /device:TPU:1 before, /device:TPU:34 now
where the time goes in v1:
time: 104 us; the launch traced here: 103 us
  starting transfers between devices  51.6 us (50%)
  waiting for transfers between devices  20.5 us (20%)
  blocking collectives  15 us (14%)
  Pallas kernels  13.5 us (13%)
  local copies, waits for them, and re-layouts  2.14 us (2%)
    ppermute x8, starting transfers between devices, shifted(): return lax.ppermute(value, ALL, pairs)  25.3 us
    all_to_all x1, starting transfers between devices, local(): parts = lax.all_to_all(copies, 'z', 0, 0, tiled=True)  15.2 us
    all_to_all x1, blocking collectives, local(): parts = lax.all_to_all(send, PLANE, 0, 0, tiled=True)  15 us
    all_to_all x1, waiting for transfers between devices, local(): parts = lax.all_to_all(copies, 'z', 0, 0, tiled=True)  11.3 us
    pallas_call x1, Pallas kernels, local(): call(fine_body, (shape(768, 128, dtype=F32), shape(768, 128), shape(384,...  7.15 us
    ppermute x8, waiting for transfers between devices, shifted(): return lax.ppermute(value, ALL, pairs)  7.01 us
    all_to_all x1, starting transfers between devices, local(): here = lax.all_to_all(outgoing, ROWS, 0, 0, tiled=True)  5.97 us
    all_to_all x1, starting transfers between devices, local(): parts = lax.all_to_all(copies, PLANE, 0, 0, tiled=True)  5.03 us
  transfers between devices with their start and end apart: 11, of which 5 were waited for; matrix products, arithmetic and copies ran while one was open for 0% of the time, Pallas kernels for 8%

profile of v1, /device:TPU:34, one launch (start us, length us, event | category | flops | bytes accessed | tf_op | source)
XLA Modules:
  0.0 103.4 jit_solution(11841603610570809053)
XLA Ops:
  1.3 0.7 copy-done.3
  2.7 1.0 shard_map.94
  3.7 6.0 %all-to-all-start = ((bf16[8,64,256]{2,1,0:T(8,128)(2,1)}), bf16[8,64,256]{2,1,0:T(8,128)(2,1)S(1)}, u32[]{:S(2)}, u32[]{:S(2)}) async-start(bf16[8,64,256]{2,1,0:T(8,128)(2,1)} %shard_map.94), calls=%async_computation | async-start | bytes 524288 | tf_op jit(solution)/shard_map/all_to_all | solution.py:244
  9.7 3.4 %collective-permute-start = (bf16[768,128]{1,0:T(8,128)(2,1)S(1)}, bf16[768,128]{1,0:T(8,128)(2,1)S(1)}, u32[]{:S(2)}, u32[]{:S(2)}) collective-permute-start(bf16[768,128]{1,0:T(8,128)(2,1)S(1)} %bitcast.9), channel_id=1, source_target_pairs={{8,0},{9,1},{10,2},{11,3},{12,4},{13,5},{14,6},{15,7},{16,8},{17,9... | collective-permute-start | bytes 589832 | tf_op jit(solution)/shard_map/ppermute | solution.py:231
  13.1 2.1 %all-to-all-done.here = bf16[8,64,256]{2,1,0:T(8,128)(2,1)S(1)} async-done(((bf16[8,64,256]{2,1,0:T(8,128)(2,1)}), bf16[8,64,256]{2,1,0:T(8,128)(2,1)S(1)}, u32[]{:S(2)}, u32[]{:S(2)}) %all-to-all-start) | async-done | bytes 262176 | tf_op jit(solution)/shard_map/all_to_all | solution.py:244
  15.2 2.1 %collective-permute-start.6 = (bf16[8,64,256]{2,1,0:T(8,128)(2,1)S(1)}, bf16[8,64,256]{2,1,0:T(8,128)(2,1)S(1)}, u32[]{:S(2)}, u32[]{:S(2)}) collective-permute-start(bf16[8,64,256]{2,1,0:T(8,128)(2,1)S(1)} %all-to-all-done.here), channel_id=1, source_target_pairs={{8,0},{9,1},{10,2},{11,3},{12,4},{13,5},{14,6},{15,7},{16,8},{17,9... | collective-permute-start | bytes 786440 | tf_op jit(solution)/shard_map/ppermute | solution.py:231
  17.4 4.0 %collective-permute-start.1 = (bf16[384,128]{1,0:T(8,128)(2,1)S(1)}, bf16[384,128]{1,0:T(8,128)(2,1)S(1)}, u32[]{:S(2)}, u32[]{:S(2)}) collective-permute-start(bf16[384,128]{1,0:T(8,128)(2,1)S(1)} %bitcast.16), channel_id=1, source_target_pairs={{8,1},{9,2},{10,3},{11,4},{12,5},{13,6},{14,7},{16,9},{17,10},{18,... | collective-permute-start | bytes 294920 | tf_op jit(solution)/shard_map/ppermute | solution.py:231
  21.3 4.0 %collective-permute-start.2 = (bf16[384,128]{1,0:T(8,128)(2,1)S(1)}, bf16[384,128]{1,0:T(8,128)(2,1)S(1)}, u32[]{:S(2)}, u32[]{:S(2)}) collective-permute-start(bf16[384,128]{1,0:T(8,128)(2,1)S(1)} %bitcast.15), channel_id=1, source_target_pairs={{9,0},{10,1},{11,2},{12,3},{13,4},{14,5},{15,6},{17,8},{18,9},{19,... | collective-permute-start | bytes 294920 | tf_op jit(solution)/shard_map/ppermute | solution.py:231
  25.3 2.2 %collective-permute-done.2.below = bf16[384,128]{1,0:T(8,128)(2,1)S(1)} collective-permute-done((bf16[384,128]{1,0:T(8,128)(2,1)S(1)}, bf16[384,128]{1,0:T(8,128)(2,1)S(1)}, u32[]{:S(2)}, u32[]{:S(2)}) %collective-permute-start.2) | collective-permute-done | bytes 98336 | tf_op jit(solution)/shard_map/ppermute | solution.py:231
  27.5 7.1 %shard_map.93 = (f32[768,128]{1,0:T(8,128)S(1)}, bf16[768,128]{1,0:T(8,128)(2,1)S(1)}, bf16[384,128]{1,0:T(8,128)(2,1)S(1)}, bf16[384,128]{1,0:T(8,128)(2,1)S(1)}, f32[128,128]{1,0:T(8,128)S(1)}) custom-call(bf16[768,128]{1,0:T(8,128)(2,1)S(1)} %bitcast.10, bf16[768,128]{1,0:T(8,128)(2,1)S(1)} %collective-permute-done.middle, ...), custom_call_target="tpu_custom_call" | custom-call | flops 1000000000 | bytes 4000000 | tf_op jit(solution)/shard_map/pallas_call | solution.py:246
  34.7 2.3 %shard_map.95 = (f32[48,256]{1,0:T(8,128)S(1)}, bf16[48,256]{1,0:T(8,128)(2,1)S(1)}, bf16[32,20,128]{2,1,0:T(8,128)(2,1)S(1)}) custom-call(s32[1]{0:T(128)} %bitcast.4.position, bf16[8,64,256]{2,1,0:T(8,128)(2,1)S(1)} %all-to-all-done.here, bf16[8,64,256]{2,1,0:T(8,128)(2,1)S(1)} %collective-permute-done.6.there, bf16[256,256]{1,0:T(8,128)(2,1)S(1)} %copy-done.1, ...), custom_call_target="tpu_custom_call" | custom-call | flops 1000000000 | bytes 2000000 | tf_op jit(solution)/shard_map/pallas_call | solution.py:260
  37.0 15.0 %all_to_all.20.parts = bf16[32,20,128]{2,1,0:T(8,128)(2,1)S(1)} all-to-all(bf16[32,20,128]{2,1,0:T(8,128)(2,1)S(1)} %get-tuple-element.25), channel_id=1, replica_groups=mesh['z'=16,'yh'=2,'core'=2,'x'=4,'yl'=2] {'yh','core','x','yl'}, dimensions={0} | all-to-all | bytes 327680 | tf_op jit(solution)/shard_map/all_to_all | solution.py:272
  52.7 15.2 %all-to-all-start.2 = ((bf16[16,20,128]{2,1,0:T(8,128)(2,1)}), bf16[16,20,128]{2,1,0:T(8,128)(2,1)S(1)}, u32[]{:S(2)}, u32[]{:S(2)}) async-start(bf16[16,20,128]{2,1,0:T(8,128)(2,1)} %shard_map.97), calls=%async_computation.2 | async-start | bytes 196608 | tf_op jit(solution)/shard_map/all_to_all | solution.py:274
  67.9 1.9 %collective-permute-start.3 = (bf16[768,128]{1,0:T(8,128)(2,1)S(1)}, bf16[768,128]{1,0:T(8,128)(2,1)S(1)}, u32[]{:S(2)}, u32[]{:S(2)}) collective-permute-start(bf16[768,128]{1,0:T(8,128)(2,1)S(1)} %get-tuple-element.17), channel_id=1, source_target_pairs={{0,8},{1,9},{2,10},{3,11},{4,12},{5,13},{6,14},{7,15},{8,16},{9,17... | collective-permute-start | bytes 589832 | tf_op jit(solution)/shard_map/ppermute | solution.py:231
  69.8 11.3 %all-to-all-done.2.parts = bf16[16,20,128]{2,1,0:T(8,128)(2,1)S(1)} async-done(((bf16[16,20,128]{2,1,0:T(8,128)(2,1)}), bf16[16,20,128]{2,1,0:T(8,128)(2,1)S(1)}, u32[]{:S(2)}, u32[]{:S(2)}) %all-to-all-start.2) | async-done | bytes 81952 | tf_op jit(solution)/shard_map/all_to_all | solution.py:274
  81.1 0.7 shard_map.98
  81.8 5.0 %all-to-all-start.3 = ((bf16[32,20,128]{2,1,0:T(8,128)(2,1)}), bf16[32,20,128]{2,1,0:T(8,128)(2,1)S(1)}, u32[]{:S(2)}, u32[]{:S(2)}) async-start(bf16[32,20,128]{2,1,0:T(8,128)(2,1)} %shard_map.98), calls=%async_computation.3 | async-start | bytes 393216 | tf_op jit(solution)/shard_map/all_to_all | solution.py:276
  86.8 3.1 %collective-permute-start.4 = (bf16[384,128]{1,0:T(8,128)(2,1)S(1)}, bf16[384,128]{1,0:T(8,128)(2,1)S(1)}, u32[]{:S(2)}, u32[]{:S(2)}) collective-permute-start(bf16[384,128]{1,0:T(8,128)(2,1)S(1)} %get-tuple-element.18), channel_id=1, source_target_pairs={{0,9},{1,10},{2,11},{3,12},{4,13},{5,14},{6,15},{8,17},{9,18},{10,... | collective-permute-start | bytes 294920 | tf_op jit(solution)/shard_map/ppermute | solution.py:231
  90.0 4.2 %collective-permute-start.5 = (bf16[384,128]{1,0:T(8,128)(2,1)S(1)}, bf16[384,128]{1,0:T(8,128)(2,1)S(1)}, u32[]{:S(2)}, u32[]{:S(2)}) collective-permute-start(bf16[384,128]{1,0:T(8,128)(2,1)S(1)} %get-tuple-element.19), channel_id=1, source_target_pairs={{1,8},{2,9},{3,10},{4,11},{5,12},{6,13},{7,14},{9,16},{10,17},{11,... | collective-permute-start | bytes 294920 | tf_op jit(solution)/shard_map/ppermute | solution.py:231
  94.2 2.7 %collective-permute-start.7 = (bf16[48,256]{1,0:T(8,128)(2,1)S(1)}, bf16[48,256]{1,0:T(8,128)(2,1)S(1)}, u32[]{:S(2)}, u32[]{:S(2)}) collective-permute-start(bf16[48,256]{1,0:T(8,128)(2,1)S(1)} %get-tuple-element.22), channel_id=1, source_target_pairs={{0,8},{1,9},{2,10},{3,11},{4,12},{5,13},{6,14},{7,15},{8,16},{9,17... | collective-permute-start | bytes 73736 | tf_op jit(solution)/shard_map/ppermute | solution.py:231
  96.9 1.1 %collective-permute-done.5.from_below = bf16[384,128]{1,0:T(8,128)(2,1)S(1)} collective-permute-done((bf16[384,128]{1,0:T(8,128)(2,1)S(1)}, bf16[384,128]{1,0:T(8,128)(2,1)S(1)}, u32[]{:S(2)}, u32[]{:S(2)}) %collective-permute-start.5) | collective-permute-done | bytes 98336 | tf_op jit(solution)/shard_map/ppermute | solution.py:231
  98.0 3.8 %collective-permute-done.7.coarse_second = bf16[48,256]{1,0:T(8,128)(2,1)S(1)} collective-permute-done((bf16[48,256]{1,0:T(8,128)(2,1)S(1)}, bf16[48,256]{1,0:T(8,128)(2,1)S(1)}, u32[]{:S(2)}, u32[]{:S(2)}) %collective-permute-start.7) | collective-permute-done | bytes 24608 | tf_op jit(solution)/shard_map/ppermute | solution.py:231
  101.8 0.9 shard_map.96
  102.7 0.7 shard_map.99
  (21 shorter events, 2.1 us)
Async XLA Ops:
  0.6 0.7 copy-start.6
  1.3 0.7 copy-start.3
  2.0 0.7 copy-start.4
  3.7 6.0 %copy-start = (bf16[1,8,96,128]{3,2,1,0:T(8,128)(2,1)S(1)}, bf16[1,8,96,128]{3,2,1,0:T(8,128)(2,1)}, u32[]{:S(2)}) copy-start(bf16[1,8,96,128]{3,2,1,0:T(8,128)(2,1)} %param.7) | copy-start | bytes 589828
  3.7 11.5 %all-to-all-start = ((bf16[8,64,256]{2,1,0:T(8,128)(2,1)}), bf16[8,64,256]{2,1,0:T(8,128)(2,1)S(1)}, u32[]{:S(2)}, u32[]{:S(2)}) async-start(bf16[8,64,256]{2,1,0:T(8,128)(2,1)} %shard_map.94), calls=%async_computation | async-start | bytes 524288 | tf_op jit(solution)/shard_map/all_to_all | solution.py:244
  9.7 17.8 %copy-start.2 = (bf16[128,128]{1,0:T(8,128)(2,1)S(1)}, bf16[128,128]{1,0:T(8,128)(2,1)}, u32[]{:S(2)}) copy-start(bf16[128,128]{1,0:T(8,128)(2,1)} %weight.5) | copy-start | bytes 98308
  9.7 17.8 %collective-permute-start = (bf16[768,128]{1,0:T(8,128)(2,1)S(1)}, bf16[768,128]{1,0:T(8,128)(2,1)S(1)}, u32[]{:S(2)}, u32[]{:S(2)}) collective-permute-start(bf16[768,128]{1,0:T(8,128)(2,1)S(1)} %bitcast.9), channel_id=1, source_target_pairs={{8,0},{9,1},{10,2},{11,3},{12,4},{13,5},{14,6},{15,7},{16,8},{17,9... | collective-permute-start | bytes 589832 | tf_op jit(solution)/shard_map/ppermute | solution.py:231
  15.2 19.4 %collective-permute-start.6 = (bf16[8,64,256]{2,1,0:T(8,128)(2,1)S(1)}, bf16[8,64,256]{2,1,0:T(8,128)(2,1)S(1)}, u32[]{:S(2)}, u32[]{:S(2)}) collective-permute-start(bf16[8,64,256]{2,1,0:T(8,128)(2,1)S(1)} %all-to-all-done.here), channel_id=1, source_target_pairs={{8,0},{9,1},{10,2},{11,3},{12,4},{13,5},{14,6},{15,7},{16,8},{17,9... | collective-permute-start | bytes 786440 | tf_op jit(solution)/shard_map/ppermute | solution.py:231
  17.4 8.0 %collective-permute-start.1 = (bf16[384,128]{1,0:T(8,128)(2,1)S(1)}, bf16[384,128]{1,0:T(8,128)(2,1)S(1)}, u32[]{:S(2)}, u32[]{:S(2)}) collective-permute-start(bf16[384,128]{1,0:T(8,128)(2,1)S(1)} %bitcast.16), channel_id=1, source_target_pairs={{8,1},{9,2},{10,3},{11,4},{12,5},{13,6},{14,7},{16,9},{17,10},{18,... | collective-permute-start | bytes 294920 | tf_op jit(solution)/shard_map/ppermute | solution.py:231
  21.3 6.2 %collective-permute-start.2 = (bf16[384,128]{1,0:T(8,128)(2,1)S(1)}, bf16[384,128]{1,0:T(8,128)(2,1)S(1)}, u32[]{:S(2)}, u32[]{:S(2)}) collective-permute-start(bf16[384,128]{1,0:T(8,128)(2,1)S(1)} %bitcast.15), channel_id=1, source_target_pairs={{9,0},{10,1},{11,2},{12,3},{13,4},{14,5},{15,6},{17,8},{18,9},{19,... | collective-permute-start | bytes 294920 | tf_op jit(solution)/shard_map/ppermute | solution.py:231
  25.3 2.2 %copy-start.5 = (f32[1,2,768]{2,1,0:T(2,128)S(1)}, f32[1,2,768]{2,1,0:T(2,128)}, u32[]{:S(2)}) copy-start(f32[1,2,768]{2,1,0:T(2,128)} %param.10) | copy-start | bytes 18436
  25.3 9.4 %copy-start.1 = (bf16[256,256]{1,0:T(8,128)(2,1)S(1)}, bf16[256,256]{1,0:T(8,128)(2,1)}, u32[]{:S(2)}) copy-start(bf16[256,256]{1,0:T(8,128)(2,1)} %coarse_weight.1) | copy-start | bytes 393220
  52.7 28.4 %all-to-all-start.2 = ((bf16[16,20,128]{2,1,0:T(8,128)(2,1)}), bf16[16,20,128]{2,1,0:T(8,128)(2,1)S(1)}, u32[]{:S(2)}, u32[]{:S(2)}) async-start(bf16[16,20,128]{2,1,0:T(8,128)(2,1)} %shard_map.97), calls=%async_computation.2 | async-start | bytes 196608 | tf_op jit(solution)/shard_map/all_to_all | solution.py:274
  67.9 30.2 %collective-permute-start.3 = (bf16[768,128]{1,0:T(8,128)(2,1)S(1)}, bf16[768,128]{1,0:T(8,128)(2,1)S(1)}, u32[]{:S(2)}, u32[]{:S(2)}) collective-permute-start(bf16[768,128]{1,0:T(8,128)(2,1)S(1)} %get-tuple-element.17), channel_id=1, source_target_pairs={{0,8},{1,9},{2,10},{3,11},{4,12},{5,13},{6,14},{7,15},{8,16},{9,17... | collective-permute-start | bytes 589832 | tf_op jit(solution)/shard_map/ppermute | solution.py:231
  81.8 20.9 %all-to-all-start.3 = ((bf16[32,20,128]{2,1,0:T(8,128)(2,1)}), bf16[32,20,128]{2,1,0:T(8,128)(2,1)S(1)}, u32[]{:S(2)}, u32[]{:S(2)}) async-start(bf16[32,20,128]{2,1,0:T(8,128)(2,1)} %shard_map.98), calls=%async_computation.3 | async-start | bytes 393216 | tf_op jit(solution)/shard_map/all_to_all | solution.py:276
  86.8 10.1 %collective-permute-start.4 = (bf16[384,128]{1,0:T(8,128)(2,1)S(1)}, bf16[384,128]{1,0:T(8,128)(2,1)S(1)}, u32[]{:S(2)}, u32[]{:S(2)}) collective-permute-start(bf16[384,128]{1,0:T(8,128)(2,1)S(1)} %get-tuple-element.18), channel_id=1, source_target_pairs={{0,9},{1,10},{2,11},{3,12},{4,13},{5,14},{6,15},{8,17},{9,18},{10,... | collective-permute-start | bytes 294920 | tf_op jit(solution)/shard_map/ppermute | solution.py:231
  90.0 8.0 %collective-permute-start.5 = (bf16[384,128]{1,0:T(8,128)(2,1)S(1)}, bf16[384,128]{1,0:T(8,128)(2,1)S(1)}, u32[]{:S(2)}, u32[]{:S(2)}) collective-permute-start(bf16[384,128]{1,0:T(8,128)(2,1)S(1)} %get-tuple-element.19), channel_id=1, source_target_pairs={{1,8},{2,9},{3,10},{4,11},{5,12},{6,13},{7,14},{9,16},{10,17},{11,... | collective-permute-start | bytes 294920 | tf_op jit(solution)/shard_map/ppermute | solution.py:231
  94.2 7.5 %collective-permute-start.7 = (bf16[48,256]{1,0:T(8,128)(2,1)S(1)}, bf16[48,256]{1,0:T(8,128)(2,1)S(1)}, u32[]{:S(2)}, u32[]{:S(2)}) collective-permute-start(bf16[48,256]{1,0:T(8,128)(2,1)S(1)} %get-tuple-element.22), channel_id=1, source_target_pairs={{0,8},{1,9},{2,10},{3,11},{4,12},{5,13},{6,14},{7,15},{8,16},{9,17... | collective-permute-start | bytes 73736 | tf_op jit(solution)/shard_map/ppermute | solution.py:231

commit v2 on v1

--- a/solution.py
+++ b/solution.py
@@ -14,17 +14,16 @@
 PLANE = ("yh", "core", "x", "yl")
 ALL = FRAMES + ROWS
 N_FRAMES, N_ROWS, N_PLANE, N_Z = 64, 8, 32, 16
-COLS = 112
-SPAN = 9 * COLS
 VMEM = pl.BlockSpec(memory_space=pltpu.VMEM)
+HBM = pl.BlockSpec(memory_space=pltpu.HBM)
 SMEM = pl.BlockSpec(memory_space=pltpu.SMEM)
 
 
-def call(body, outs, scratch=(), n_smem=0, n_in=0, flops=0, nbytes=0):
+def call(body, outs, scratch=(), n_smem=0, n_in=0, flops=0, nbytes=0, kind=VMEM):
     return pl.pallas_call(
         body,
         out_shape=outs,
-        in_specs=[SMEM] * n_smem + [VMEM] * n_in,
+        in_specs=[SMEM] * n_smem + [kind] * n_in,
         out_specs=jax.tree.map(lambda _: VMEM, outs),
         scratch_shapes=list(scratch),
         compiler_params=pltpu.CompilerParams(vmem_limit_bytes=40 * 1024 * 1024),
@@ -60,15 +59,25 @@
     return lax.broadcasted_iota(jnp.int32, dims, axis)
 
 
-def prepare_body(coarse, refined, back, out, cots):
+def prepare_body(coarse_hbm, refined_hbm, back_hbm, out, cots, refined, back, sems):
+    copies = [
+        pltpu.make_async_copy(refined_hbm, refined, sems.at[N_ROWS]),
+        pltpu.make_async_copy(back_hbm, back, sems.at[N_ROWS + 1]),
+    ]
+    for band in range(N_ROWS):
+        copies.append(pltpu.make_async_copy(coarse_hbm, out.at[band, pl.ds(0, 48), :], sems.at[band]))
+    for copy in copies:
+        copy.start()
     cell = iota((768, 128), 0)
     low = (cell >= 384).astype(jnp.int32)
     cell = cell - 384 * low
     line = (cell >= 96).astype(jnp.int32) + (cell >= 192).astype(jnp.int32) + (cell >= 288).astype(jnp.int32)
     column = lax.shift_right_logical(cell - 96 * line, 2)
     pool = (iota((768, 128), 1) == column + 24 * low).astype(F32).astype(BF16)
+    cots[...] = jnp.zeros_like(cots)
+    copies[0].wait()
+    copies[1].wait()
     hi, mid, rest = split3(refined[...])
-    cots[...] = jnp.zeros_like(cots)
     cots[0:2, 0:128] = 4.0 * (mm(hi, pool) + (mm(mid, pool) + mm(rest, pool)))
     cots[2:4, 0:48] = back[...]
     hi, mid, rest = split3(cots[0:4, :])
@@ -77,67 +86,70 @@
     cots[8:12, :] = rest.astype(F32)
     packed = cots[...].astype(BF16)
     for band in range(N_ROWS):
-        out[band, 0:48, :] = coarse[...]
         out[band, 48:64, :] = packed
+    for copy in copies[2:]:
+        copy.wait()
 
 
 def fine_body(own, middle, above, below, weight, refined, first, mid_out, up_out, down_out, partial,
-              queries, keys, key_grad, turned):
+              queries, keys, key_grad, turned, window):
     scale = 1.0 / math.sqrt(128.0)
     w = weight[...]
-    queries[...] = mm(own[...], w).astype(BF16)
-    blank = jnp.zeros((COLS - 96, 128), BF16)
-    for row in range(16):
-        if row < 4:
-            source = above[row * 96 : row * 96 + 96, :]
-        elif row < 12:
-            source = middle[(row - 4) * 96 : (row - 4) * 96 + 96, :]
-        else:
-            source = below[(row - 12) * 96 : (row - 12) * 96 + 96, :]
-        keys[row * COLS : row * COLS + 96, :] = mm(source, w).astype(BF16)
-        keys[row * COLS + 96 : row * COLS + COLS, :] = blank
+    queries[...] = mm(own[...], w).astype(BF16).reshape(8, 96, 128)
+    keys[:, 0:16, :] = jnp.zeros((16, 16, 128), BF16)
+    keys[:, 112:128, :] = jnp.zeros((16, 16, 128), BF16)
+    keys[0:4, 16:112, :] = mm(above[...], w).astype(BF16).reshape(4, 96, 128)
+    keys[4:12, 16:112, :] = mm(middle[...], w).astype(BF16).reshape(8, 96, 128)
+    keys[12:16, 16:112, :] = mm(below[...], w).astype(BF16).reshape(4, 96, 128)
     key_grad[...] = jnp.zeros_like(key_grad)
     turned[...] = jnp.zeros_like(turned)
     turned[0:2, :] = refined[...]
-    cot = jnp.transpose(turned[...], (1, 0))
-    lane = iota((1, SPAN), 1).astype(F32)
-    line = jnp.floor((lane + 0.5) * (1.0 / COLS))
-    column = lane - line * COLS
-    step_y = line - 4.0
-    step_x = column - iota((96, SPAN), 0).astype(F32)
-    step_x = jnp.where(step_x > 50.0, step_x - COLS, step_x)
-    inside = jnp.abs(step_x) < 4.5
-    for row in range(8):
-        q = queries[row * 96 : row * 96 + 96, :]
-        k = keys[row * COLS : row * COLS + SPAN, :]
-        s = jnp.where(inside, mm_nt(q, k) * scale, -1e30)
-        e = jnp.exp(s - jnp.max(s, axis=1, keepdims=True))
-        inverse = 1.0 / jnp.sum(e, axis=1, keepdims=True)
-        mean_x = jnp.sum(e * step_x, axis=1, keepdims=True) * inverse
-        mean_y = jnp.sum(e * step_y, axis=1, keepdims=True) * inverse
-        gx = cot[row * 96 : row * 96 + 96, 0:1]
-        gy = cot[row * 96 : row * 96 + 96, 1:2]
-        factor = inverse * scale
-        bend = gx * step_x + gy * step_y - (gx * mean_x + gy * mean_y)
-        weights = (e * bend * factor).astype(BF16)
-        first[row * 96 : row * 96 + 96, :] = mm(weights, k)
-        key_grad[row * COLS : row * COLS + SPAN, :] += mm_tn(weights, q)
-    for row in range(16):
-        rounded = key_grad[row * COLS : row * COLS + 96, :].astype(BF16)
-        if row < 4:
-            up_out[row * 96 : row * 96 + 96, :] = rounded
-        elif row < 12:
-            mid_out[(row - 4) * 96 : (row - 4) * 96 + 96, :] = rounded
-        else:
-            down_out[(row - 12) * 96 : (row - 12) * 96 + 96, :] = rounded
-    hi = first[...].astype(BF16)
-    low = (first[...] - hi.astype(F32)).astype(BF16)
+    upright = jnp.transpose(turned[...], (1, 0))
+    lane = iota((1, 128), 1)
+    query_x = jnp.bitwise_and(lane, 31).astype(F32)
+    query_y = lax.shift_right_logical(lane, 5).astype(F32)
+    key_x = iota((64, 128), 0).astype(F32) - 16.0
+    near_x = jnp.where(jnp.abs(key_x - query_x) < 4.5, 0.0, -1e30)
+    for line in range(12):
+        near_y = jnp.where(jnp.abs(line - 4.0 - query_y) < 4.5, 0.0, -1e30)
+        window[line] = jnp.minimum(near_x, near_y)
+    for part in range(2):
+        for column in range(3):
+            q = queries[4 * part : 4 * part + 4, 32 * column : 32 * column + 32, :].reshape(128, 128)
+            k = keys[4 * part : 4 * part + 12, 32 * column : 32 * column + 64, :].reshape(768, 128)
+            pieces = [(4 * part + line) * 96 + 32 * column for line in range(4)]
+            cot = jnp.transpose(jnp.concatenate([upright[at : at + 32, :] for at in pieces], axis=0), (1, 0))
+            gx, gy = cot[0:1, :], cot[1:2, :]
+            s = mm_nt(k, q).reshape(12, 64, 128) * (scale * math.log2(math.e)) + window[...]
+            top = jnp.max(jnp.max(s, axis=0), axis=0, keepdims=True)
+            e = jnp.exp2(s - top)
+            by_x = jnp.sum(e, axis=0)
+            inverse = 1.0 / jnp.sum(by_x, axis=0, keepdims=True)
+            mean_x = jnp.sum(by_x * key_x, axis=0, keepdims=True) * inverse
+            mean_y = jnp.zeros((1, 128), F32)
+            for line in range(12):
+                mean_y = mean_y + (line - 4.0) * jnp.sum(e[line], axis=0, keepdims=True)
+            mean_y = mean_y * inverse
+            factor = inverse * scale
+            gx, gy = gx * factor, gy * factor
+            bend_x = gx * (key_x - mean_x)
+            weights = jnp.concatenate(
+                [(e[line] * (bend_x + gy * ((line - 4.0) - mean_y))).astype(BF16) for line in range(12)], axis=0
+            )
+            first[4 * part : 4 * part + 4, 32 * column : 32 * column + 32, :] = mm_tn(weights, k).reshape(4, 32, 128)
+            key_grad[4 * part : 4 * part + 12, 32 * column : 32 * column + 64, :] += mm(weights, q).reshape(12, 64, 128)
+    up_out[...] = key_grad[0:4, 16:112, :].astype(BF16).reshape(384, 128)
+    mid_out[...] = key_grad[4:12, 16:112, :].astype(BF16).reshape(768, 128)
+    down_out[...] = key_grad[12:16, 16:112, :].astype(BF16).reshape(384, 128)
+    exact = first[...].reshape(768, 128)
+    hi = exact.astype(BF16)
+    low = (exact - hi.astype(F32)).astype(BF16)
     total = mm_tn(own[...], hi) + mm_tn(own[...], low)
     total = total + mm_tn(middle[...], mid_out[...])
     partial[...] = total + mm_tn(above[...], up_out[...]) + mm_tn(below[...], down_out[...])
 
 
-def coarse_body(position, here, there, weight, fine_partial, first, second, send,
+def coarse_body(position, here, there, weight, fine_partial, fine_middle, first, joined, send,
                 forward, backward, both, packed):
     band = position[0]
     w = weight[...]
@@ -181,7 +193,9 @@
     own_first = mm(forward[mine, :], qb) + mm(backward[mine, :], qb)
     own_second = both[mine, :].astype(BF16)
     first[...] = own_first
-    second[...] = own_second
+    joined[0:768, :] = fine_middle[...]
+    joined[768:816, :] = own_second[:, 0:128]
+    joined[816:864, :] = own_second[:, 128:256]
     hi = own_first.astype(BF16)
     low = (own_first - hi.astype(F32)).astype(BF16)
     f_here = here[band, 0:48, :]
@@ -210,16 +224,17 @@
         fine[4 * chunk : 4 * chunk + 4, :] = values[chunk, 16:20, :]
 
 
-def finish_body(first, middle, from_above, from_below, weight, coarse_first, coarse_second, coarse_weight,
-                fine_out, coarse_out):
-    total = first[...] + middle[...].astype(F32)
+def finish_body(first, joined, from_above, from_below, weight, coarse_first, coarse_weight, fine_out, coarse_out):
+    total = first[...] + joined[0:768, :].astype(F32)
     w = weight[...]
     top = (total[0:384, :] + from_above[...].astype(F32)).astype(BF16)
     bottom = (total[384:768, :] + from_below[...].astype(F32)).astype(BF16)
     fine_out[0:384, :] = mm_nt(top, w).astype(BF16)
     fine_out[384:768, :] = mm_nt(bottom, w).astype(BF16)
-    dq = (coarse_first[...] + coarse_second[...].astype(F32)).astype(BF16)
-    coarse_out[...] = mm_nt(dq, coarse_weight[...]).astype(BF16)
+    w = coarse_weight[...]
+    left = (coarse_first[:, 0:128] + joined[768:816, :].astype(F32)).astype(BF16)
+    right = (coarse_first[:, 128:256] + joined[816:864, :].astype(F32)).astype(BF16)
+    coarse_out[...] = (mm_nt(left, w[:, 0:128]) + mm_nt(right, w[:, 128:256])).astype(BF16)
 
 
 def shifted(value, frames, rows):
@@ -239,47 +254,58 @@
     middle = shifted(fine_own, -1, 0)
     above = shifted(fine_own[384:768], -1, 1)
     below = shifted(fine_own[0:384], -1, -1)
-    outgoing = call(prepare_body, shape(N_ROWS, 64, 256), [pltpu.VMEM((16, 256), F32)], n_in=3,
-                    flops=10**8, nbytes=10**6)(coarse_own, refined, grad_back.reshape(2, 48))
+    outgoing = call(
+        prepare_body,
+        shape(N_ROWS, 64, 256),
+        [
+            pltpu.VMEM((16, 256), F32),
+            pltpu.VMEM((2, 768), F32),
+            pltpu.VMEM((2, 48), F32),
+            pltpu.SemaphoreType.DMA((N_ROWS + 2,)),
+        ],
+        n_in=3, flops=10**9, nbytes=10**6, kind=HBM,
+    )(coarse_own, refined, grad_back.reshape(2, 48))
     here = lax.all_to_all(outgoing, ROWS, 0, 0, tiled=True)
     there = shifted(here, -1, 0)
     first, mid_out, up_out, down_out, fine_partial = call(
         fine_body,
-        (shape(768, 128, dtype=F32), shape(768, 128), shape(384, 128), shape(384, 128), shape(128, 128, dtype=F32)),
+        (shape(8, 96, 128, dtype=F32), shape(768, 128), shape(384, 128), shape(384, 128), shape(128, 128, dtype=F32)),
         [
-            pltpu.VMEM((768, 128), BF16),
-            pltpu.VMEM((16 * COLS, 128), BF16),
-            pltpu.VMEM((16 * COLS, 128), F32),
+            pltpu.VMEM((8, 96, 128), BF16),
+            pltpu.VMEM((16, 128, 128), BF16),
+            pltpu.VMEM((16, 128, 128), F32),
             pltpu.VMEM((8, 768), F32),
+            pltpu.VMEM((12, 64, 128), F32),
         ],
-        n_in=6, flops=10**9, nbytes=4 * 10**6,
+        n_in=6, flops=20 * 10**9, nbytes=4 * 10**6,
     )(fine_own, middle, above, below, fine_weight, refined)
     back_up = shifted(up_out, 1, -1)
     back_down = shifted(down_out, 1, 1)
-    back_mid = shifted(mid_out, 1, 0)
-    coarse_first, coarse_second, send = call(
+    coarse_first, joined, send = call(
         coarse_body,
-        (shape(48, 256, dtype=F32), shape(48, 256), shape(N_PLANE, 20, 128)),
+        (shape(48, 256, dtype=F32), shape(864, 128), shape(N_PLANE, 20, 128)),
         [
             pltpu.VMEM((384, 384), BF16),
             pltpu.VMEM((384, 384), BF16),
             pltpu.VMEM((384, 256), F32),
             pltpu.VMEM((N_PLANE, 24, 128), F32),
         ],
-        n_smem=1, n_in=4, flops=10**9, nbytes=2 * 10**6,
-    )(band, here, there, coarse_weight, fine_partial)
-    back_coarse = shifted(coarse_second, 1, 0)
+        n_smem=1, n_in=5, flops=3 * 10**9, nbytes=2 * 10**6,
+    )(band, here, there, coarse_weight, fine_partial, mid_out)
+    back_joined = shifted(joined, 1, 0)
     parts = lax.all_to_all(send, PLANE, 0, 0, tiled=True)
+    parts, back_up, back_down = lax.optimization_barrier((parts, back_up, back_down))
     copies = call(sum_body, shape(N_Z, 20, 128), n_in=1, nbytes=10**6)(parts)
     parts = lax.all_to_all(copies, "z", 0, 0, tiled=True)
+    parts, back_joined = lax.optimization_barrier((parts, back_joined))
     copies = call(sum_body, shape(N_PLANE, 20, 128), n_in=1, nbytes=10**6)(parts)
     parts = lax.all_to_all(copies, PLANE, 0, 0, tiled=True)
     coarse_total, fine_total = call(
         unpack_body, (shape(256, 256, dtype=F32), shape(128, 128, dtype=F32)), n_in=1, nbytes=10**6
     )(parts)
     fine_grad, coarse_grad = call(
-        finish_body, (shape(768, 128), shape(48, 256)), n_in=8, flops=10**8, nbytes=10**6
-    )(first, back_mid, back_down, back_up, fine_weight, coarse_first, back_coarse, coarse_weight)
+        finish_body, (shape(768, 128), shape(48, 256)), n_in=7, flops=10**8, nbytes=10**6
+    )(first.reshape(768, 128), back_joined, back_down, back_up, fine_weight, coarse_first, coarse_weight)
     return (
         coarse_grad.reshape(coarse_features.shape),
         fine_grad.reshape(fine_features.shape),

time: 104 us -> 96.2 us (0.925)
  the two profiles are of different devices: /device:TPU:34 before, /device:TPU:1 now
where the time goes in v2:
time: 96.2 us; the launch traced here: 95.4 us
  starting transfers between devices  60 us (62%)
  waiting for transfers between devices  22.3 us (23%)
  Pallas kernels  10.8 us (11%)
  local copies, waits for them, and re-layouts  1.44 us (1%)
    ppermute x7, starting transfers between devices, shifted(): return lax.ppermute(value, ALL, pairs)  26.9 us
    all_to_all x1, starting transfers between devices, local(): parts = lax.all_to_all(copies, 'z', 0, 0, tiled=True)  11.2 us
    all_to_all x1, starting transfers between devices, local(): parts = lax.all_to_all(copies, PLANE, 0, 0, tiled=True)  10.8 us
    ppermute x7, waiting for transfers between devices, shifted(): return lax.ppermute(value, ALL, pairs)  7.82 us
    all_to_all x1, starting transfers between devices, local(): parts = lax.all_to_all(send, PLANE, 0, 0, tiled=True)  7.57 us
    all_to_all x1, waiting for transfers between devices, local(): parts = lax.all_to_all(copies, PLANE, 0, 0, tiled=True)  7.13 us
    all_to_all x1, waiting for transfers between devices, local(): parts = lax.all_to_all(copies, 'z', 0, 0, tiled=True)  4.68 us
    all_to_all x1, starting transfers between devices, local(): here = lax.all_to_all(outgoing, ROWS, 0, 0, tiled=True)  3.56 us
  transfers between devices with their start and end apart: 11, of which 7 were waited for; matrix products, arithmetic and copies ran while one was open for 0% of the time, Pallas kernels for 6%

profile of v2, /device:TPU:1, one launch (start us, length us, event | category | flops | bytes accessed | tf_op | source)
XLA Modules:
  0.0 95.4 jit_solution(4478100717029752847)
XLA Ops:
  0.6 8.8 %collective-permute-start = (bf16[768,128]{1,0:T(8,128)(2,1)}, bf16[768,128]{1,0:T(8,128)(2,1)S(1)}, u32[]{:S(2)}, u32[]{:S(2)}) collective-permute-start(bf16[768,128]{1,0:T(8,128)(2,1)} %bitcast.11), channel_id=1, source_target_pairs={{8,0},{9,1},{10,2},{11,3},{12,4},{13,5},{14,6},{15,7},{16,8},{17,9... | collective-permute-start | bytes 589832 | tf_op jit(solution)/shard_map/ppermute | solution.py:246
  10.1 0.7 copy-done.3
  10.9 1.4 %shard_map.94 = bf16[8,64,256]{2,1,0:T(8,128)(2,1)} custom-call(bf16[48,256]{1,0:T(8,128)(2,1)S(1)} %bitcast.13, f32[2,768]{1,0:T(2,128)S(1)} %bitcast.14, f32[2,48]{1,0:T(2,128)S(1)} %bitcast.16), custom_call_target="tpu_custom_call" | custom-call | flops 1000000000 | bytes 1000000 | tf_op jit(solution)/shard_map/pallas_call | solution.py:257
  12.2 3.6 %all-to-all-start = ((bf16[8,64,256]{2,1,0:T(8,128)(2,1)}), bf16[8,64,256]{2,1,0:T(8,128)(2,1)S(1)}, u32[]{:S(2)}, u32[]{:S(2)}) async-start(bf16[8,64,256]{2,1,0:T(8,128)(2,1)} %shard_map.94), calls=%async_computation | async-start | bytes 524288 | tf_op jit(solution)/shard_map/all_to_all | solution.py:268
  15.8 2.8 %collective-permute-start.1 = (bf16[384,128]{1,0:T(8,128)(2,1)S(1)}, bf16[384,128]{1,0:T(8,128)(2,1)S(1)}, u32[]{:S(2)}, u32[]{:S(2)}) collective-permute-start(bf16[384,128]{1,0:T(8,128)(2,1)S(1)} %bitcast.18), channel_id=1, source_target_pairs={{8,1},{9,2},{10,3},{11,4},{12,5},{13,6},{14,7},{16,9},{17,10},{18,... | collective-permute-start | bytes 294920 | tf_op jit(solution)/shard_map/ppermute | solution.py:246
  18.6 1.3 %collective-permute-start.2 = (bf16[384,128]{1,0:T(8,128)(2,1)S(1)}, bf16[384,128]{1,0:T(8,128)(2,1)S(1)}, u32[]{:S(2)}, u32[]{:S(2)}) collective-permute-start(bf16[384,128]{1,0:T(8,128)(2,1)S(1)} %bitcast.17), channel_id=1, source_target_pairs={{9,0},{10,1},{11,2},{12,3},{13,4},{14,5},{15,6},{17,8},{18,9},{19,... | collective-permute-start | bytes 294920 | tf_op jit(solution)/shard_map/ppermute | solution.py:246
  20.0 2.7 %all-to-all-done.here = bf16[8,64,256]{2,1,0:T(8,128)(2,1)S(1)} async-done(((bf16[8,64,256]{2,1,0:T(8,128)(2,1)}), bf16[8,64,256]{2,1,0:T(8,128)(2,1)S(1)}, u32[]{:S(2)}, u32[]{:S(2)}) %all-to-all-start) | async-done | bytes 262176 | tf_op jit(solution)/shard_map/all_to_all | solution.py:268
  22.6 2.4 %collective-permute-start.3 = (bf16[8,64,256]{2,1,0:T(8,128)(2,1)S(1)}, bf16[8,64,256]{2,1,0:T(8,128)(2,1)S(1)}, u32[]{:S(2)}, u32[]{:S(2)}) collective-permute-start(bf16[8,64,256]{2,1,0:T(8,128)(2,1)S(1)} %all-to-all-done.here), channel_id=1, source_target_pairs={{8,0},{9,1},{10,2},{11,3},{12,4},{13,5},{14,6},{15,7},{16,8},{17,9... | collective-permute-start | bytes 786440 | tf_op jit(solution)/shard_map/ppermute | solution.py:246
  25.0 1.0 %collective-permute-done.2.below = bf16[384,128]{1,0:T(8,128)(2,1)S(1)} collective-permute-done((bf16[384,128]{1,0:T(8,128)(2,1)S(1)}, bf16[384,128]{1,0:T(8,128)(2,1)S(1)}, u32[]{:S(2)}, u32[]{:S(2)}) %collective-permute-start.2) | collective-permute-done | bytes 98336 | tf_op jit(solution)/shard_map/ppermute | solution.py:246
  26.0 3.4 %shard_map.93 = (f32[8,96,128]{2,1,0:T(8,128)S(1)}, bf16[768,128]{1,0:T(8,128)(2,1)S(1)}, bf16[384,128]{1,0:T(8,128)(2,1)S(1)}, bf16[384,128]{1,0:T(8,128)(2,1)S(1)}, f32[128,128]{1,0:T(8,128)S(1)}) custom-call(bf16[768,128]{1,0:T(8,128)(2,1)S(1)} %bitcast.12, bf16[768,128]{1,0:T(8,128)(2,1)S(1)} %collective-permute-done.middle, ...), custom_call_target="tpu_custom_call" | custom-call | flops 20000000000 | bytes 4000000 | tf_op jit(solution)/shard_map/pallas_call | solution.py:270
  29.4 2.4 %collective-permute-done.3.there = bf16[8,64,256]{2,1,0:T(8,128)(2,1)S(1)} collective-permute-done((bf16[8,64,256]{2,1,0:T(8,128)(2,1)S(1)}, bf16[8,64,256]{2,1,0:T(8,128)(2,1)S(1)}, u32[]{:S(2)}, u32[]{:S(2)}) %collective-permute-start.3) | collective-permute-done | bytes 262176 | tf_op jit(solution)/shard_map/ppermute | solution.py:246
  31.8 3.0 %shard_map.95 = (f32[48,256]{1,0:T(8,128)S(1)}, bf16[864,128]{1,0:T(8,128)(2,1)S(1)}, bf16[32,20,128]{2,1,0:T(8,128)(2,1)}) custom-call(s32[1]{0:T(128)} %bitcast.5.position, bf16[8,64,256]{2,1,0:T(8,128)(2,1)S(1)} %all-to-all-done.here, bf16[8,64,256]{2,1,0:T(8,128)(2,1)S(1)} %collective-permute-done.3.there, bf16[256,256]{1,0:T(8,128)(2,1)S(1)} %copy-done.1, ...), custom_call_target="tpu_custom_call" | custom-call | flops 3000000000 | bytes 2000000 | tf_op jit(solution)/shard_map/pallas_call | solution.py:284
  34.8 7.6 %all-to-all-start.1 = ((bf16[32,20,128]{2,1,0:T(8,128)(2,1)}), bf16[32,20,128]{2,1,0:T(8,128)(2,1)S(1)}, u32[]{:S(2)}, u32[]{:S(2)}) async-start(bf16[32,20,128]{2,1,0:T(8,128)(2,1)} %get-tuple-element.24), calls=%async_computation.1 | async-start | bytes 393216 | tf_op jit(solution)/shard_map/all_to_all | solution.py:296
  42.4 1.3 %collective-permute-start.4 = (bf16[384,128]{1,0:T(8,128)(2,1)S(1)}, bf16[384,128]{1,0:T(8,128)(2,1)S(1)}, u32[]{:S(2)}, u32[]{:S(2)}) collective-permute-start(bf16[384,128]{1,0:T(8,128)(2,1)S(1)} %get-tuple-element.25), channel_id=1, source_target_pairs={{1,8},{2,9},{3,10},{4,11},{5,12},{6,13},{7,14},{9,16},{10,17},{11,... | collective-permute-start | bytes 294920 | tf_op jit(solution)/shard_map/ppermute | solution.py:246
  43.7 6.0 %collective-permute-start.5 = (bf16[384,128]{1,0:T(8,128)(2,1)S(1)}, bf16[384,128]{1,0:T(8,128)(2,1)S(1)}, u32[]{:S(2)}, u32[]{:S(2)}) collective-permute-start(bf16[384,128]{1,0:T(8,128)(2,1)S(1)} %get-tuple-element.26), channel_id=1, source_target_pairs={{0,9},{1,10},{2,11},{3,12},{4,13},{5,14},{6,15},{8,17},{9,18},{10,... | collective-permute-start | bytes 294920 | tf_op jit(solution)/shard_map/ppermute | solution.py:246
  49.7 1.6 %collective-permute-done.5.from_above = bf16[384,128]{1,0:T(8,128)(2,1)S(1)} collective-permute-done((bf16[384,128]{1,0:T(8,128)(2,1)S(1)}, bf16[384,128]{1,0:T(8,128)(2,1)S(1)}, u32[]{:S(2)}, u32[]{:S(2)}) %collective-permute-start.5) | collective-permute-done | bytes 98336 | tf_op jit(solution)/shard_map/ppermute | solution.py:246
  52.0 11.2 %all-to-all-start.2 = ((bf16[16,20,128]{2,1,0:T(8,128)(2,1)}), bf16[16,20,128]{2,1,0:T(8,128)(2,1)S(1)}, u32[]{:S(2)}, u32[]{:S(2)}) async-start(bf16[16,20,128]{2,1,0:T(8,128)(2,1)} %shard_map.96), calls=%async_computation.2 | async-start | bytes 196608 | tf_op jit(solution)/shard_map/all_to_all | solution.py:299
  63.3 4.3 %collective-permute-start.6 = (bf16[864,128]{1,0:T(8,128)(2,1)S(1)}, bf16[864,128]{1,0:T(8,128)(2,1)S(1)}, u32[]{:S(2)}, u32[]{:S(2)}) collective-permute-start(bf16[864,128]{1,0:T(8,128)(2,1)S(1)} %get-tuple-element.28), channel_id=1, source_target_pairs={{0,8},{1,9},{2,10},{3,11},{4,12},{5,13},{6,14},{7,15},{8,16},{9,17... | collective-permute-start | bytes 663560 | tf_op jit(solution)/shard_map/ppermute | solution.py:246
  67.6 2.9 %collective-permute-done.6.joined = bf16[864,128]{1,0:T(8,128)(2,1)S(1)} collective-permute-done((bf16[864,128]{1,0:T(8,128)(2,1)S(1)}, bf16[864,128]{1,0:T(8,128)(2,1)S(1)}, u32[]{:S(2)}, u32[]{:S(2)}) %collective-permute-start.6) | collective-permute-done | bytes 221216 | tf_op jit(solution)/shard_map/ppermute | solution.py:246
  70.4 4.7 %all-to-all-done.2.parts = bf16[16,20,128]{2,1,0:T(8,128)(2,1)S(1)} async-done(((bf16[16,20,128]{2,1,0:T(8,128)(2,1)}), bf16[16,20,128]{2,1,0:T(8,128)(2,1)S(1)}, u32[]{:S(2)}, u32[]{:S(2)}) %all-to-all-start.2) | async-done | bytes 81952 | tf_op jit(solution)/shard_map/all_to_all | solution.py:299
  75.8 10.8 %all-to-all-start.3 = ((bf16[32,20,128]{2,1,0:T(8,128)(2,1)}), bf16[32,20,128]{2,1,0:T(8,128)(2,1)S(1)}, u32[]{:S(2)}, u32[]{:S(2)}) async-start(bf16[32,20,128]{2,1,0:T(8,128)(2,1)} %shard_map.98), calls=%async_computation.3 | async-start | bytes 393216 | tf_op jit(solution)/shard_map/all_to_all | solution.py:302
  86.6 0.9 shard_map.97
  87.5 7.1 %all-to-all-done.3.parts = bf16[32,20,128]{2,1,0:T(8,128)(2,1)S(1)} async-done(((bf16[32,20,128]{2,1,0:T(8,128)(2,1)}), bf16[32,20,128]{2,1,0:T(8,128)(2,1)S(1)}, u32[]{:S(2)}, u32[]{:S(2)}) %all-to-all-start.3) | async-done | bytes 163872 | tf_op jit(solution)/shard_map/all_to_all | solution.py:302
  94.7 0.7 shard_map.99
  (18 shorter events, 2.1 us)
Async XLA Ops:
  0.6 8.8 %copy-start.4 = (f32[1,2,768]{2,1,0:T(2,128)S(1)}, f32[1,2,768]{2,1,0:T(2,128)}, u32[]{:S(2)}) copy-start(f32[1,2,768]{2,1,0:T(2,128)} %param.10) | copy-start | bytes 18436
  0.6 25.3 %collective-permute-start = (bf16[768,128]{1,0:T(8,128)(2,1)}, bf16[768,128]{1,0:T(8,128)(2,1)S(1)}, u32[]{:S(2)}, u32[]{:S(2)}) collective-permute-start(bf16[768,128]{1,0:T(8,128)(2,1)} %bitcast.11), channel_id=1, source_target_pairs={{8,0},{9,1},{10,2},{11,3},{12,4},{13,5},{14,6},{15,7},{16,8},{17,9... | collective-permute-start | bytes 589832 | tf_op jit(solution)/shard_map/ppermute | solution.py:246
  9.4 0.7 copy-start.5
  10.1 0.7 copy-start.3
  12.2 3.6 %copy-start = (bf16[1,8,96,128]{3,2,1,0:T(8,128)(2,1)S(1)}, bf16[1,8,96,128]{3,2,1,0:T(8,128)(2,1)}, u32[]{:S(2)}) copy-start(bf16[1,8,96,128]{3,2,1,0:T(8,128)(2,1)} %param.7) | copy-start | bytes 589828
  12.2 10.4 %all-to-all-start = ((bf16[8,64,256]{2,1,0:T(8,128)(2,1)}), bf16[8,64,256]{2,1,0:T(8,128)(2,1)S(1)}, u32[]{:S(2)}, u32[]{:S(2)}) async-start(bf16[8,64,256]{2,1,0:T(8,128)(2,1)} %shard_map.94), calls=%async_computation | async-start | bytes 524288 | tf_op jit(solution)/shard_map/all_to_all | solution.py:268
  15.8 10.2 %copy-start.2 = (bf16[128,128]{1,0:T(8,128)(2,1)S(1)}, bf16[128,128]{1,0:T(8,128)(2,1)}, u32[]{:S(2)}) copy-start(bf16[128,128]{1,0:T(8,128)(2,1)} %weight.5) | copy-start | bytes 98308
  15.8 9.2 %collective-permute-start.1 = (bf16[384,128]{1,0:T(8,128)(2,1)S(1)}, bf16[384,128]{1,0:T(8,128)(2,1)S(1)}, u32[]{:S(2)}, u32[]{:S(2)}) collective-permute-start(bf16[384,128]{1,0:T(8,128)(2,1)S(1)} %bitcast.18), channel_id=1, source_target_pairs={{8,1},{9,2},{10,3},{11,4},{12,5},{13,6},{14,7},{16,9},{17,10},{18,... | collective-permute-start | bytes 294920 | tf_op jit(solution)/shard_map/ppermute | solution.py:246
  18.6 7.3 %collective-permute-start.2 = (bf16[384,128]{1,0:T(8,128)(2,1)S(1)}, bf16[384,128]{1,0:T(8,128)(2,1)S(1)}, u32[]{:S(2)}, u32[]{:S(2)}) collective-permute-start(bf16[384,128]{1,0:T(8,128)(2,1)S(1)} %bitcast.17), channel_id=1, source_target_pairs={{9,0},{10,1},{11,2},{12,3},{13,4},{14,5},{15,6},{17,8},{18,9},{19,... | collective-permute-start | bytes 294920 | tf_op jit(solution)/shard_map/ppermute | solution.py:246
  20.0 11.9 %copy-start.1 = (bf16[256,256]{1,0:T(8,128)(2,1)S(1)}, bf16[256,256]{1,0:T(8,128)(2,1)}, u32[]{:S(2)}) copy-start(bf16[256,256]{1,0:T(8,128)(2,1)} %coarse_weight.1) | copy-start | bytes 393220
  22.6 9.2 %collective-permute-start.3 = (bf16[8,64,256]{2,1,0:T(8,128)(2,1)S(1)}, bf16[8,64,256]{2,1,0:T(8,128)(2,1)S(1)}, u32[]{:S(2)}, u32[]{:S(2)}) collective-permute-start(bf16[8,64,256]{2,1,0:T(8,128)(2,1)S(1)} %all-to-all-done.here), channel_id=1, source_target_pairs={{8,0},{9,1},{10,2},{11,3},{12,4},{13,5},{14,6},{15,7},{16,8},{17,9... | collective-permute-start | bytes 786440 | tf_op jit(solution)/shard_map/ppermute | solution.py:246
  34.8 16.5 %all-to-all-start.1 = ((bf16[32,20,128]{2,1,0:T(8,128)(2,1)}), bf16[32,20,128]{2,1,0:T(8,128)(2,1)S(1)}, u32[]{:S(2)}, u32[]{:S(2)}) async-start(bf16[32,20,128]{2,1,0:T(8,128)(2,1)} %get-tuple-element.24), calls=%async_computation.1 | async-start | bytes 393216 | tf_op jit(solution)/shard_map/all_to_all | solution.py:296
  42.4 7.3 %collective-permute-start.4 = (bf16[384,128]{1,0:T(8,128)(2,1)S(1)}, bf16[384,128]{1,0:T(8,128)(2,1)S(1)}, u32[]{:S(2)}, u32[]{:S(2)}) collective-permute-start(bf16[384,128]{1,0:T(8,128)(2,1)S(1)} %get-tuple-element.25), channel_id=1, source_target_pairs={{1,8},{2,9},{3,10},{4,11},{5,12},{6,13},{7,14},{9,16},{10,17},{11,... | collective-permute-start | bytes 294920 | tf_op jit(solution)/shard_map/ppermute | solution.py:246
  43.7 7.6 %collective-permute-start.5 = (bf16[384,128]{1,0:T(8,128)(2,1)S(1)}, bf16[384,128]{1,0:T(8,128)(2,1)S(1)}, u32[]{:S(2)}, u32[]{:S(2)}) collective-permute-start(bf16[384,128]{1,0:T(8,128)(2,1)S(1)} %get-tuple-element.26), channel_id=1, source_target_pairs={{0,9},{1,10},{2,11},{3,12},{4,13},{5,14},{6,15},{8,17},{9,18},{10,... | collective-permute-start | bytes 294920 | tf_op jit(solution)/shard_map/ppermute | solution.py:246
  52.0 23.1 %all-to-all-start.2 = ((bf16[16,20,128]{2,1,0:T(8,128)(2,1)}), bf16[16,20,128]{2,1,0:T(8,128)(2,1)S(1)}, u32[]{:S(2)}, u32[]{:S(2)}) async-start(bf16[16,20,128]{2,1,0:T(8,128)(2,1)} %shard_map.96), calls=%async_computation.2 | async-start | bytes 196608 | tf_op jit(solution)/shard_map/all_to_all | solution.py:299
  63.3 7.2 %collective-permute-start.6 = (bf16[864,128]{1,0:T(8,128)(2,1)S(1)}, bf16[864,128]{1,0:T(8,128)(2,1)S(1)}, u32[]{:S(2)}, u32[]{:S(2)}) collective-permute-start(bf16[864,128]{1,0:T(8,128)(2,1)S(1)} %get-tuple-element.28), channel_id=1, source_target_pairs={{0,8},{1,9},{2,10},{3,11},{4,12},{5,13},{6,14},{7,15},{8,16},{9,17... | collective-permute-start | bytes 663560 | tf_op jit(solution)/shard_map/ppermute | solution.py:246
  75.8 18.8 %all-to-all-start.3 = ((bf16[32,20,128]{2,1,0:T(8,128)(2,1)}), bf16[32,20,128]{2,1,0:T(8,128)(2,1)S(1)}, u32[]{:S(2)}, u32[]{:S(2)}) async-start(bf16[32,20,128]{2,1,0:T(8,128)(2,1)} %shard_map.98), calls=%async_computation.3 | async-start | bytes 393216 | tf_op jit(solution)/shard_map/all_to_all | solution.py:302

commit v3 on v2

--- a/solution.py
+++ b/solution.py
@@ -19,14 +19,14 @@
 SMEM = pl.BlockSpec(memory_space=pltpu.SMEM)
 
 
-def call(body, outs, scratch=(), n_smem=0, n_in=0, flops=0, nbytes=0, kind=VMEM):
+def call(body, outs, scratch=(), n_smem=0, n_in=0, flops=0, nbytes=0, kind=VMEM, room=40):
     return pl.pallas_call(
         body,
         out_shape=outs,
         in_specs=[SMEM] * n_smem + [kind] * n_in,
         out_specs=jax.tree.map(lambda _: VMEM, outs),
         scratch_shapes=list(scratch),
-        compiler_params=pltpu.CompilerParams(vmem_limit_bytes=40 * 1024 * 1024),
+        compiler_params=pltpu.CompilerParams(vmem_limit_bytes=room * 1024 * 1024),
         cost_estimate=pl.CostEstimate(flops=flops, bytes_accessed=nbytes, transcendentals=0),
     )
 
@@ -149,49 +149,43 @@
     partial[...] = total + mm_tn(above[...], up_out[...]) + mm_tn(below[...], down_out[...])
 
 
+def match(scores, cot_x, cot_y):
+    s = scores * (math.log2(math.e) / 16.0)
+    e = jnp.exp2(s - jnp.max(s, axis=0, keepdims=True)).reshape(16, 24, 384)
+    by_x = jnp.sum(e, axis=0)
+    inverse = 1.0 / jnp.sum(by_x, axis=0, keepdims=True)
+    key_x = iota((24, 384), 0).astype(F32)
+    mean_x = jnp.sum(by_x * key_x, axis=0, keepdims=True) * inverse
+    mean_y = jnp.zeros((1, 384), F32)
+    for line in range(1, 16):
+        mean_y = mean_y + float(line) * jnp.sum(e[line], axis=0, keepdims=True)
+    mean_y = mean_y * inverse
+    factor = inverse * (1.0 / 16.0)
+    cot_x, cot_y = cot_x * factor, cot_y * factor
+    bend_x = cot_x * (key_x - mean_x)
+    lines = [e[line] * (bend_x + cot_y * (float(line) - mean_y)) for line in range(16)]
+    return jnp.concatenate(lines, axis=0).astype(BF16)
+
+
 def coarse_body(position, here, there, weight, fine_partial, fine_middle, first, joined, send,
-                forward, backward, both, packed):
+                sums_first, sums_second, packed):
     band = position[0]
     w = weight[...]
     qa = mm(here[:, 0:48, :].reshape(384, 256), w).astype(BF16)
     qb = mm(there[:, 0:48, :].reshape(384, 256), w).astype(BF16)
     flat = jnp.zeros((16, 384), F32)
-    upright = jnp.zeros((384, 16), F32)
+    ahead = iota((128, 384), 1) - iota((128, 384), 0)
     for source in range(N_ROWS):
-        cots = here[source, 48:64, 0:128]
-        place = (iota((128, 384), 1) - iota((128, 384), 0) == 48 * source).astype(F32).astype(BF16)
-        turned = (iota((384, 128), 0) - iota((384, 128), 1) == 48 * source).astype(F32).astype(BF16)
-        flat = flat + mm(cots, place)
-        upright = upright + mm_nt(turned, cots)
-    cf_x = upright[:, 0:1] + (upright[:, 4:5] + upright[:, 8:9])
-    cf_y = upright[:, 1:2] + (upright[:, 5:6] + upright[:, 9:10])
-    cb_x = flat[2:3, :] + (flat[6:7, :] + flat[10:11, :])
-    cb_y = flat[3:4, :] + (flat[7:8, :] + flat[11:12, :])
-    lane = iota((1, 384), 1).astype(F32)
-    lane_y = jnp.floor((lane + 0.5) * (1.0 / 24.0))
-    lane_x = lane - 24.0 * lane_y
-    line = iota((384, 1), 0).astype(F32)
-    line_y = jnp.floor((line + 0.5) * (1.0 / 24.0))
-    line_x = line - 24.0 * line_y
-    s = mm_nt(qa, qb) * (1.0 / 16.0)
-    e = jnp.exp(s - jnp.max(s, axis=1, keepdims=True))
-    inverse = 1.0 / jnp.sum(e, axis=1, keepdims=True)
-    mean_x = jnp.sum(e * lane_x, axis=1, keepdims=True) * inverse
-    mean_y = jnp.sum(e * lane_y, axis=1, keepdims=True) * inverse
-    bend = cf_x * lane_x + cf_y * lane_y - (cf_x * mean_x + cf_y * mean_y)
-    forward_w = (e * bend * (inverse * (1.0 / 16.0))).astype(BF16)
-    forward[...] = forward_w
-    e = jnp.exp(s - jnp.max(s, axis=0, keepdims=True))
-    inverse = 1.0 / jnp.sum(e, axis=0, keepdims=True)
-    mean_x = jnp.sum(e * line_x, axis=0, keepdims=True) * inverse
-    mean_y = jnp.sum(e * line_y, axis=0, keepdims=True) * inverse
-    bend = cb_x * line_x + cb_y * line_y - (cb_x * mean_x + cb_y * mean_y)
-    backward_w = (e * bend * (inverse * (1.0 / 16.0))).astype(BF16)
-    backward[...] = backward_w
-    both[...] = mm_tn(forward_w, qa) + mm_tn(backward_w, qa)
+        place = (ahead == 48 * source).astype(F32).astype(BF16)
+        flat = flat + mm(here[source, 48:64, 0:128], place)
+    cots = flat[0:4, :] + (flat[4:8, :] + flat[8:12, :])
+    forward_t = match(mm_nt(qb, qa), cots[0:1, :], cots[1:2, :])
+    backward_t = match(mm_nt(qa, qb), cots[2:3, :], cots[3:4, :])
+    sums_first[...] = mm_tn(forward_t, qb) + mm(backward_t, qb)
+    sums_second[...] = mm(forward_t, qa) + mm_tn(backward_t, qa)
     mine = pl.ds(pl.multiple_of(band * 48, 16), 48)
-    own_first = mm(forward[mine, :], qb) + mm(backward[mine, :], qb)
-    own_second = both[mine, :].astype(BF16)
+    own_first = sums_first[mine, :]
+    own_second = sums_second[mine, :].astype(BF16)
     first[...] = own_first
     joined[0:768, :] = fine_middle[...]
     joined[768:816, :] = own_second[:, 0:128]
@@ -263,7 +257,7 @@
             pltpu.VMEM((2, 48), F32),
             pltpu.SemaphoreType.DMA((N_ROWS + 2,)),
         ],
-        n_in=3, flops=10**9, nbytes=10**6, kind=HBM,
+        n_in=3, flops=10**9, nbytes=10**6, kind=HBM, room=60,
     )(coarse_own, refined, grad_back.reshape(2, 48))
     here = lax.all_to_all(outgoing, ROWS, 0, 0, tiled=True)
     there = shifted(here, -1, 0)
@@ -285,8 +279,7 @@
         coarse_body,
         (shape(48, 256, dtype=F32), shape(864, 128), shape(N_PLANE, 20, 128)),
         [
-            pltpu.VMEM((384, 384), BF16),
-            pltpu.VMEM((384, 384), BF16),
+            pltpu.VMEM((384, 256), F32),
             pltpu.VMEM((384, 256), F32),
             pltpu.VMEM((N_PLANE, 24, 128), F32),
         ],
@@ -294,10 +287,9 @@
     )(band, here, there, coarse_weight, fine_partial, mid_out)
     back_joined = shifted(joined, 1, 0)
     parts = lax.all_to_all(send, PLANE, 0, 0, tiled=True)
-    parts, back_up, back_down = lax.optimization_barrier((parts, back_up, back_down))
     copies = call(sum_body, shape(N_Z, 20, 128), n_in=1, nbytes=10**6)(parts)
     parts = lax.all_to_all(copies, "z", 0, 0, tiled=True)
-    parts, back_joined = lax.optimization_barrier((parts, back_joined))
+    parts, back_up, back_joined = lax.optimization_barrier((parts, back_up, back_joined))
     copies = call(sum_body, shape(N_PLANE, 20, 128), n_in=1, nbytes=10**6)(parts)
     parts = lax.all_to_all(copies, PLANE, 0, 0, tiled=True)
     coarse_total, fine_total = call(

time: 96.2 us -> 88.5 us (0.920)
  blocking collectives: 0 us -> 15.4 us
  starting transfers between devices: 60 us -> 45.6 us
  waiting for transfers between devices: 22.3 us -> 15.8 us
  local copies, waits for them, and re-layouts: 1.44 us -> 0.04 us
    all_to_all x0 -> x1, blocking collectives: none -> 15.4 us  [local(): parts = lax.all_to_all(send, PLANE, 0, 0, tiled=True)]
    all_to_all x1 -> x0, starting transfers between devices: 7.57 us -> none  [local(): parts = lax.all_to_all(send, PLANE, 0, 0, tiled=True)]
    all_to_all x1, waiting for transfers between devices: 7.13 us -> 0.56 us  [local(): parts = lax.all_to_all(copies, PLANE, 0, 0, tiled=True)]
    all_to_all x1, starting transfers between devices: 10.8 us -> 6.3 us  [local(): parts = lax.all_to_all(copies, PLANE, 0, 0, tiled=True)]
    ppermute x7, starting transfers between devices: 26.9 us -> 24.5 us  [shifted(): return lax.ppermute(value, ALL, pairs)]
    ppermute x7, waiting for transfers between devices: 7.82 us -> 10.1 us  [shifted(): return lax.ppermute(value, ALL, pairs)]
    all_to_all x1, waiting for transfers between devices: 4.68 us -> 2.46 us  [local(): parts = lax.all_to_all(copies, 'z', 0, 0, tiled=True)]
    unnamed x12 -> x8, local copies, waits for them, and re-layouts: 1.42 us -> 0.03 us
  transfers between devices with their start and end apart: 11 -> 10, of which waited for: 7 -> 7; matrix products, arithmetic and copies ran while one was open for 0% -> 0% of each run, Pallas kernels for 6% -> 7%
where the time goes in v3:
time: 88.5 us; the launch traced here: 87.6 us
  starting transfers between devices  45.6 us (52%)
  waiting for transfers between devices  15.8 us (18%)
  blocking collectives  15.4 us (17%)
  Pallas kernels  9.97 us (11%)
    ppermute x7, starting transfers between devices, shifted(): return lax.ppermute(value, ALL, pairs)  24.5 us
    all_to_all x1, blocking collectives, local(): parts = lax.all_to_all(send, PLANE, 0, 0, tiled=True)  15.4 us
    all_to_all x1, starting transfers between devices, local(): parts = lax.all_to_all(copies, 'z', 0, 0, tiled=True)  11.2 us
    ppermute x7, waiting for transfers between devices, shifted(): return lax.ppermute(value, ALL, pairs)  10.1 us
    all_to_all x1, starting transfers between devices, local(): parts = lax.all_to_all(copies, PLANE, 0, 0, tiled=True)  6.3 us
    all_to_all x1, starting transfers between devices, local(): here = lax.all_to_all(outgoing, ROWS, 0, 0, tiled=True)  3.56 us
    pallas_call x1, Pallas kernels, local(): call(fine_body, (shape(8, 96, 128, dtype=F32), shape(768, 128), shape(384...  3.43 us
    all_to_all x1, waiting for transfers between devices, local(): here = lax.all_to_all(outgoing, ROWS, 0, 0, tiled=True)  2.65 us
  transfers between devices with their start and end apart: 10, of which 7 were waited for; matrix products, arithmetic and copies ran while one was open for 0% of the time, Pallas kernels for 7%

profile of v3, /device:TPU:1, one launch (start us, length us, event | category | flops | bytes accessed | tf_op | source)
XLA Modules:
  0.0 87.6 jit_solution(11859130690523788050)
XLA Ops:
  0.6 8.8 %collective-permute-start = (bf16[768,128]{1,0:T(8,128)(2,1)}, bf16[768,128]{1,0:T(8,128)(2,1)S(1)}, u32[]{:S(2)}, u32[]{:S(2)}) collective-permute-start(bf16[768,128]{1,0:T(8,128)(2,1)} %bitcast.11), channel_id=1, source_target_pairs={{8,0},{9,1},{10,2},{11,3},{12,4},{13,5},{14,6},{15,7},{16,8},{17,9... | collective-permute-start | bytes 589832 | tf_op jit(solution)/shard_map/ppermute | solution.py:240
  9.4 1.8 %shard_map.94 = bf16[8,64,256]{2,1,0:T(8,128)(2,1)} custom-call(bf16[48,256]{1,0:T(8,128)(2,1)} %bitcast.18, f32[2,768]{1,0:T(2,128)} %bitcast.13, f32[2,48]{1,0:T(2,128)} %bitcast.20), custom_call_target="tpu_custom_call" | custom-call | flops 1000000000 | bytes 1000000 | tf_op jit(solution)/shard_map/pallas_call | solution.py:251
  11.3 3.6 %all-to-all-start = ((bf16[8,64,256]{2,1,0:T(8,128)(2,1)}), bf16[8,64,256]{2,1,0:T(8,128)(2,1)S(1)}, u32[]{:S(2)}, u32[]{:S(2)}) async-start(bf16[8,64,256]{2,1,0:T(8,128)(2,1)} %shard_map.94), calls=%async_computation | async-start | bytes 524288 | tf_op jit(solution)/shard_map/all_to_all | solution.py:262
  14.9 2.8 %collective-permute-start.1 = (bf16[384,128]{1,0:T(8,128)(2,1)S(1)}, bf16[384,128]{1,0:T(8,128)(2,1)S(1)}, u32[]{:S(2)}, u32[]{:S(2)}) collective-permute-start(bf16[384,128]{1,0:T(8,128)(2,1)S(1)} %bitcast.16), channel_id=1, source_target_pairs={{8,1},{9,2},{10,3},{11,4},{12,5},{13,6},{14,7},{16,9},{17,10},{18,... | collective-permute-start | bytes 294920 | tf_op jit(solution)/shard_map/ppermute | solution.py:240
  17.7 1.3 %collective-permute-start.2 = (bf16[384,128]{1,0:T(8,128)(2,1)S(1)}, bf16[384,128]{1,0:T(8,128)(2,1)S(1)}, u32[]{:S(2)}, u32[]{:S(2)}) collective-permute-start(bf16[384,128]{1,0:T(8,128)(2,1)S(1)} %bitcast.15), channel_id=1, source_target_pairs={{9,0},{10,1},{11,2},{12,3},{13,4},{14,5},{15,6},{17,8},{18,9},{19,... | collective-permute-start | bytes 294920 | tf_op jit(solution)/shard_map/ppermute | solution.py:240
  19.0 2.6 %all-to-all-done.here = bf16[8,64,256]{2,1,0:T(8,128)(2,1)S(1)} async-done(((bf16[8,64,256]{2,1,0:T(8,128)(2,1)}), bf16[8,64,256]{2,1,0:T(8,128)(2,1)S(1)}, u32[]{:S(2)}, u32[]{:S(2)}) %all-to-all-start) | async-done | bytes 262176 | tf_op jit(solution)/shard_map/all_to_all | solution.py:262
  21.7 2.4 %collective-permute-start.3 = (bf16[8,64,256]{2,1,0:T(8,128)(2,1)S(1)}, bf16[8,64,256]{2,1,0:T(8,128)(2,1)S(1)}, u32[]{:S(2)}, u32[]{:S(2)}) collective-permute-start(bf16[8,64,256]{2,1,0:T(8,128)(2,1)S(1)} %all-to-all-done.here), channel_id=1, source_target_pairs={{8,0},{9,1},{10,2},{11,3},{12,4},{13,5},{14,6},{15,7},{16,8},{17,9... | collective-permute-start | bytes 786440 | tf_op jit(solution)/shard_map/ppermute | solution.py:240
  24.0 1.0 %collective-permute-done.2.below = bf16[384,128]{1,0:T(8,128)(2,1)S(1)} collective-permute-done((bf16[384,128]{1,0:T(8,128)(2,1)S(1)}, bf16[384,128]{1,0:T(8,128)(2,1)S(1)}, u32[]{:S(2)}, u32[]{:S(2)}) %collective-permute-start.2) | collective-permute-done | bytes 98336 | tf_op jit(solution)/shard_map/ppermute | solution.py:240
  25.0 3.4 %shard_map.93 = (f32[8,96,128]{2,1,0:T(8,128)S(1)}, bf16[768,128]{1,0:T(8,128)(2,1)S(1)}, bf16[384,128]{1,0:T(8,128)(2,1)S(1)}, bf16[384,128]{1,0:T(8,128)(2,1)S(1)}, f32[128,128]{1,0:T(8,128)S(1)}) custom-call(bf16[768,128]{1,0:T(8,128)(2,1)S(1)} %bitcast.12, bf16[768,128]{1,0:T(8,128)(2,1)S(1)} %collective-permute-done.middle, ...), custom_call_target="tpu_custom_call" | custom-call | flops 20000000000 | bytes 4000000 | tf_op jit(solution)/shard_map/pallas_call | solution.py:264
  28.5 2.4 %collective-permute-done.3.there = bf16[8,64,256]{2,1,0:T(8,128)(2,1)S(1)} collective-permute-done((bf16[8,64,256]{2,1,0:T(8,128)(2,1)S(1)}, bf16[8,64,256]{2,1,0:T(8,128)(2,1)S(1)}, u32[]{:S(2)}, u32[]{:S(2)}) %collective-permute-start.3) | collective-permute-done | bytes 262176 | tf_op jit(solution)/shard_map/ppermute | solution.py:240
  30.8 1.7 %shard_map.95 = (f32[48,256]{1,0:T(8,128)S(1)}, bf16[864,128]{1,0:T(8,128)(2,1)S(1)}, bf16[32,20,128]{2,1,0:T(8,128)(2,1)S(1)}) custom-call(s32[1]{0:T(128)} %bitcast.5.position, bf16[8,64,256]{2,1,0:T(8,128)(2,1)S(1)} %all-to-all-done.here, bf16[8,64,256]{2,1,0:T(8,128)(2,1)S(1)} %collective-permute-done.3.there, bf16[256,256]{1,0:T(8,128)(2,1)S(1)} %copy-done.1, ...), custom_call_target="tpu_custom_call" | custom-call | flops 3000000000 | bytes 2000000 | tf_op jit(solution)/shard_map/pallas_call | solution.py:278
  32.5 15.4 %all_to_all.20.parts = bf16[32,20,128]{2,1,0:T(8,128)(2,1)S(1)} all-to-all(bf16[32,20,128]{2,1,0:T(8,128)(2,1)S(1)} %get-tuple-element.22), channel_id=1, replica_groups=mesh['z'=16,'yh'=2,'core'=2,'x'=4,'yl'=2] {'yh','core','x','yl'}, dimensions={0} | all-to-all | bytes 327680 | tf_op jit(solution)/shard_map/all_to_all | solution.py:289
  47.9 0.7 shard_map.96
  48.6 11.2 %all-to-all-start.2 = ((bf16[16,20,128]{2,1,0:T(8,128)(2,1)}), bf16[16,20,128]{2,1,0:T(8,128)(2,1)S(1)}, u32[]{:S(2)}, u32[]{:S(2)}) async-start(bf16[16,20,128]{2,1,0:T(8,128)(2,1)} %shard_map.96), calls=%async_computation.2 | async-start | bytes 196608 | tf_op jit(solution)/shard_map/all_to_all | solution.py:291
  59.9 3.2 %collective-permute-start.5 = (bf16[864,128]{1,0:T(8,128)(2,1)S(1)}, bf16[864,128]{1,0:T(8,128)(2,1)S(1)}, u32[]{:S(2)}, u32[]{:S(2)}) collective-permute-start(bf16[864,128]{1,0:T(8,128)(2,1)S(1)} %get-tuple-element.24), channel_id=1, source_target_pairs={{0,8},{1,9},{2,10},{3,11},{4,12},{5,13},{6,14},{7,15},{8,16},{9,17... | collective-permute-start | bytes 663560 | tf_op jit(solution)/shard_map/ppermute | solution.py:240
  63.1 1.3 %collective-permute-start.4 = (bf16[384,128]{1,0:T(8,128)(2,1)S(1)}, bf16[384,128]{1,0:T(8,128)(2,1)S(1)}, u32[]{:S(2)}, u32[]{:S(2)}) collective-permute-start(bf16[384,128]{1,0:T(8,128)(2,1)S(1)} %get-tuple-element.23), channel_id=1, source_target_pairs={{1,8},{2,9},{3,10},{4,11},{5,12},{6,13},{7,14},{9,16},{10,17},{11,... | collective-permute-start | bytes 294920 | tf_op jit(solution)/shard_map/ppermute | solution.py:240
  64.4 4.9 %collective-permute-done.4.from_below = bf16[384,128]{1,0:T(8,128)(2,1)S(1)} collective-permute-done((bf16[384,128]{1,0:T(8,128)(2,1)S(1)}, bf16[384,128]{1,0:T(8,128)(2,1)S(1)}, u32[]{:S(2)}, u32[]{:S(2)}) %collective-permute-start.4) | collective-permute-done | bytes 98336 | tf_op jit(solution)/shard_map/ppermute | solution.py:240
  69.4 2.5 %all-to-all-done.2.parts = bf16[16,20,128]{2,1,0:T(8,128)(2,1)S(1)} async-done(((bf16[16,20,128]{2,1,0:T(8,128)(2,1)}), bf16[16,20,128]{2,1,0:T(8,128)(2,1)S(1)}, u32[]{:S(2)}, u32[]{:S(2)}) %all-to-all-start.2) | async-done | bytes 81952 | tf_op jit(solution)/shard_map/all_to_all | solution.py:291
  71.8 0.7 shard_map.98
  72.5 6.3 %all-to-all-start.3 = ((bf16[32,20,128]{2,1,0:T(8,128)(2,1)}), bf16[32,20,128]{2,1,0:T(8,128)(2,1)S(1)}, u32[]{:S(2)}, u32[]{:S(2)}) async-start(bf16[32,20,128]{2,1,0:T(8,128)(2,1)} %shard_map.98), calls=%async_computation.3 | async-start | bytes 393216 | tf_op jit(solution)/shard_map/all_to_all | solution.py:294
  78.8 4.8 %collective-permute-start.6 = (bf16[384,128]{1,0:T(8,128)(2,1)S(1)}, bf16[384,128]{1,0:T(8,128)(2,1)S(1)}, u32[]{:S(2)}, u32[]{:S(2)}) collective-permute-start(bf16[384,128]{1,0:T(8,128)(2,1)S(1)} %get-tuple-element.26), channel_id=1, source_target_pairs={{0,9},{1,10},{2,11},{3,12},{4,13},{5,14},{6,15},{8,17},{9,18},{10,... | collective-permute-start | bytes 294920 | tf_op jit(solution)/shard_map/ppermute | solution.py:240
  83.6 1.8 %collective-permute-done.6.from_above = bf16[384,128]{1,0:T(8,128)(2,1)S(1)} collective-permute-done((bf16[384,128]{1,0:T(8,128)(2,1)S(1)}, bf16[384,128]{1,0:T(8,128)(2,1)S(1)}, u32[]{:S(2)}, u32[]{:S(2)}) %collective-permute-start.6) | collective-permute-done | bytes 98336 | tf_op jit(solution)/shard_map/ppermute | solution.py:240
  85.4 0.9 %shard_map.97 = (bf16[768,128]{1,0:T(8,128)(2,1)}, bf16[48,256]{1,0:T(8,128)(2,1)}) custom-call(f32[768,128]{1,0:T(8,128)S(1)} %bitcast.10, bf16[864,128]{1,0:T(8,128)(2,1)S(1)} %collective-permute-done.5.joined, bf16[384,128]{1,0:T(8,128)(2,1)S(1)} %collective-permute-done.6.from_above, bf16[384,128]{1,0:T(8,128)(2,1)S(1)} %collective-permute-done.4.from_below, ...), custom_call_target="tpu_custom_call" | custom-call | flops 100000000 | bytes 1000000 | tf_op jit(solution)/shard_map/pallas_call | solution.py:298
  86.9 0.7 shard_map.99
  (13 shorter events, 0.6 us)
Async XLA Ops:
  0.6 24.4 %collective-permute-start = (bf16[768,128]{1,0:T(8,128)(2,1)}, bf16[768,128]{1,0:T(8,128)(2,1)S(1)}, u32[]{:S(2)}, u32[]{:S(2)}) collective-permute-start(bf16[768,128]{1,0:T(8,128)(2,1)} %bitcast.11), channel_id=1, source_target_pairs={{8,0},{9,1},{10,2},{11,3},{12,4},{13,5},{14,6},{15,7},{16,8},{17,9... | collective-permute-start | bytes 589832 | tf_op jit(solution)/shard_map/ppermute | solution.py:240
  11.3 3.6 %copy-start = (bf16[1,8,96,128]{3,2,1,0:T(8,128)(2,1)S(1)}, bf16[1,8,96,128]{3,2,1,0:T(8,128)(2,1)}, u32[]{:S(2)}) copy-start(bf16[1,8,96,128]{3,2,1,0:T(8,128)(2,1)} %param.7) | copy-start | bytes 589828
  11.3 10.4 %all-to-all-start = ((bf16[8,64,256]{2,1,0:T(8,128)(2,1)}), bf16[8,64,256]{2,1,0:T(8,128)(2,1)S(1)}, u32[]{:S(2)}, u32[]{:S(2)}) async-start(bf16[8,64,256]{2,1,0:T(8,128)(2,1)} %shard_map.94), calls=%async_computation | async-start | bytes 524288 | tf_op jit(solution)/shard_map/all_to_all | solution.py:262
  14.8 10.2 %copy-start.2 = (bf16[128,128]{1,0:T(8,128)(2,1)S(1)}, bf16[128,128]{1,0:T(8,128)(2,1)}, u32[]{:S(2)}) copy-start(bf16[128,128]{1,0:T(8,128)(2,1)} %weight.5) | copy-start | bytes 98308
  14.9 9.2 %collective-permute-start.1 = (bf16[384,128]{1,0:T(8,128)(2,1)S(1)}, bf16[384,128]{1,0:T(8,128)(2,1)S(1)}, u32[]{:S(2)}, u32[]{:S(2)}) collective-permute-start(bf16[384,128]{1,0:T(8,128)(2,1)S(1)} %bitcast.16), channel_id=1, source_target_pairs={{8,1},{9,2},{10,3},{11,4},{12,5},{13,6},{14,7},{16,9},{17,10},{18,... | collective-permute-start | bytes 294920 | tf_op jit(solution)/shard_map/ppermute | solution.py:240
  17.7 7.3 %collective-permute-start.2 = (bf16[384,128]{1,0:T(8,128)(2,1)S(1)}, bf16[384,128]{1,0:T(8,128)(2,1)S(1)}, u32[]{:S(2)}, u32[]{:S(2)}) collective-permute-start(bf16[384,128]{1,0:T(8,128)(2,1)S(1)} %bitcast.15), channel_id=1, source_target_pairs={{9,0},{10,1},{11,2},{12,3},{13,4},{14,5},{15,6},{17,8},{18,9},{19,... | collective-permute-start | bytes 294920 | tf_op jit(solution)/shard_map/ppermute | solution.py:240
  19.0 6.0 %copy-start.3 = (f32[1,2,768]{2,1,0:T(2,128)S(1)}, f32[1,2,768]{2,1,0:T(2,128)}, u32[]{:S(2)}) copy-start(f32[1,2,768]{2,1,0:T(2,128)} %param.10) | copy-start | bytes 18436
  19.0 11.8 %copy-start.1 = (bf16[256,256]{1,0:T(8,128)(2,1)S(1)}, bf16[256,256]{1,0:T(8,128)(2,1)}, u32[]{:S(2)}) copy-start(bf16[256,256]{1,0:T(8,128)(2,1)} %coarse_weight.1) | copy-start | bytes 393220
  21.7 9.2 %collective-permute-start.3 = (bf16[8,64,256]{2,1,0:T(8,128)(2,1)S(1)}, bf16[8,64,256]{2,1,0:T(8,128)(2,1)S(1)}, u32[]{:S(2)}, u32[]{:S(2)}) collective-permute-start(bf16[8,64,256]{2,1,0:T(8,128)(2,1)S(1)} %all-to-all-done.here), channel_id=1, source_target_pairs={{8,0},{9,1},{10,2},{11,3},{12,4},{13,5},{14,6},{15,7},{16,8},{17,9... | collective-permute-start | bytes 786440 | tf_op jit(solution)/shard_map/ppermute | solution.py:240
  48.6 23.2 %all-to-all-start.2 = ((bf16[16,20,128]{2,1,0:T(8,128)(2,1)}), bf16[16,20,128]{2,1,0:T(8,128)(2,1)S(1)}, u32[]{:S(2)}, u32[]{:S(2)}) async-start(bf16[16,20,128]{2,1,0:T(8,128)(2,1)} %shard_map.96), calls=%async_computation.2 | async-start | bytes 196608 | tf_op jit(solution)/shard_map/all_to_all | solution.py:291
  59.9 9.5 %collective-permute-start.5 = (bf16[864,128]{1,0:T(8,128)(2,1)S(1)}, bf16[864,128]{1,0:T(8,128)(2,1)S(1)}, u32[]{:S(2)}, u32[]{:S(2)}) collective-permute-start(bf16[864,128]{1,0:T(8,128)(2,1)S(1)} %get-tuple-element.24), channel_id=1, source_target_pairs={{0,8},{1,9},{2,10},{3,11},{4,12},{5,13},{6,14},{7,15},{8,16},{9,17... | collective-permute-start | bytes 663560 | tf_op jit(solution)/shard_map/ppermute | solution.py:240
  63.1 6.2 %collective-permute-start.4 = (bf16[384,128]{1,0:T(8,128)(2,1)S(1)}, bf16[384,128]{1,0:T(8,128)(2,1)S(1)}, u32[]{:S(2)}, u32[]{:S(2)}) collective-permute-start(bf16[384,128]{1,0:T(8,128)(2,1)S(1)} %get-tuple-element.23), channel_id=1, source_target_pairs={{1,8},{2,9},{3,10},{4,11},{5,12},{6,13},{7,14},{9,16},{10,17},{11,... | collective-permute-start | bytes 294920 | tf_op jit(solution)/shard_map/ppermute | solution.py:240
  72.5 14.3 %all-to-all-start.3 = ((bf16[32,20,128]{2,1,0:T(8,128)(2,1)}), bf16[32,20,128]{2,1,0:T(8,128)(2,1)S(1)}, u32[]{:S(2)}, u32[]{:S(2)}) async-start(bf16[32,20,128]{2,1,0:T(8,128)(2,1)} %shard_map.98), calls=%async_computation.3 | async-start | bytes 393216 | tf_op jit(solution)/shard_map/all_to_all | solution.py:294
  78.8 6.6 %collective-permute-start.6 = (bf16[384,128]{1,0:T(8,128)(2,1)S(1)}, bf16[384,128]{1,0:T(8,128)(2,1)S(1)}, u32[]{:S(2)}, u32[]{:S(2)}) collective-permute-start(bf16[384,128]{1,0:T(8,128)(2,1)S(1)} %get-tuple-element.26), channel_id=1, source_target_pairs={{0,9},{1,10},{2,11},{3,12},{4,13},{5,14},{6,15},{8,17},{9,18},{10,... | collective-permute-start | bytes 294920 | tf_op jit(solution)/shard_map/ppermute | solution.py:240

commit v4 on v3

--- a/solution.py
+++ b/solution.py
@@ -14,6 +14,7 @@
 PLANE = ("yh", "core", "x", "yl")
 ALL = FRAMES + ROWS
 N_FRAMES, N_ROWS, N_PLANE, N_Z = 64, 8, 32, 16
+SOON = 12
 VMEM = pl.BlockSpec(memory_space=pltpu.VMEM)
 HBM = pl.BlockSpec(memory_space=pltpu.HBM)
 SMEM = pl.BlockSpec(memory_space=pltpu.SMEM)
@@ -218,11 +219,11 @@
         fine[4 * chunk : 4 * chunk + 4, :] = values[chunk, 16:20, :]
 
 
-def finish_body(first, joined, from_above, from_below, weight, coarse_first, coarse_weight, fine_out, coarse_out):
+def finish_body(first, joined, above_soon, above_late, below_soon, below_late, weight, coarse_first, coarse_weight, fine_out, coarse_out):
     total = first[...] + joined[0:768, :].astype(F32)
     w = weight[...]
-    top = (total[0:384, :] + from_above[...].astype(F32)).astype(BF16)
-    bottom = (total[384:768, :] + from_below[...].astype(F32)).astype(BF16)
+    top = (total[0:384, :] + (above_soon[...].astype(F32) + above_late[...].astype(F32))).astype(BF16)
+    bottom = (total[384:768, :] + (below_soon[...].astype(F32) + below_late[...].astype(F32))).astype(BF16)
     fine_out[0:384, :] = mm_nt(top, w).astype(BF16)
     fine_out[384:768, :] = mm_nt(bottom, w).astype(BF16)
     w = coarse_weight[...]
@@ -231,10 +232,10 @@
     coarse_out[...] = (mm_nt(left, w[:, 0:128]) + mm_nt(right, w[:, 128:256])).astype(BF16)
 
 
-def shifted(value, frames, rows):
+def shifted(value, frames, rows, sources=(0, N_FRAMES)):
     pairs = [
         (f * N_ROWS + r, (f + frames) * N_ROWS + r + rows)
-        for f in range(max(0, -frames), min(N_FRAMES, N_FRAMES - frames))
+        for f in range(max(sources[0], -frames), min(sources[1], N_FRAMES - frames))
         for r in range(max(0, -rows), min(N_ROWS, N_ROWS - rows))
     ]
     return lax.ppermute(value, ALL, pairs)
@@ -273,8 +274,8 @@
         ],
         n_in=6, flops=20 * 10**9, nbytes=4 * 10**6,
     )(fine_own, middle, above, below, fine_weight, refined)
-    back_up = shifted(up_out, 1, -1)
-    back_down = shifted(down_out, 1, 1)
+    back_up_soon, back_up = (shifted(up_out, 1, -1, part) for part in ((0, SOON), (SOON, N_FRAMES)))
+    back_down_soon, back_down = (shifted(down_out, 1, 1, part) for part in ((0, SOON), (SOON, N_FRAMES)))
     coarse_first, joined, send = call(
         coarse_body,
         (shape(48, 256, dtype=F32), shape(864, 128), shape(N_PLANE, 20, 128)),
@@ -287,17 +288,17 @@
     )(band, here, there, coarse_weight, fine_partial, mid_out)
     back_joined = shifted(joined, 1, 0)
     parts = lax.all_to_all(send, PLANE, 0, 0, tiled=True)
+    parts, back_up_soon, back_down_soon = lax.optimization_barrier((parts, back_up_soon, back_down_soon))
     copies = call(sum_body, shape(N_Z, 20, 128), n_in=1, nbytes=10**6)(parts)
-    parts = lax.all_to_all(copies, "z", 0, 0, tiled=True)
-    parts, back_up, back_joined = lax.optimization_barrier((parts, back_up, back_joined))
+    parts = lax.all_to_all(copies, "z", 0, 0, axis_index_groups=[[(9 + i) % N_Z for i in range(N_Z)]], tiled=True)
     copies = call(sum_body, shape(N_PLANE, 20, 128), n_in=1, nbytes=10**6)(parts)
     parts = lax.all_to_all(copies, PLANE, 0, 0, tiled=True)
     coarse_total, fine_total = call(
         unpack_body, (shape(256, 256, dtype=F32), shape(128, 128, dtype=F32)), n_in=1, nbytes=10**6
     )(parts)
     fine_grad, coarse_grad = call(
-        finish_body, (shape(768, 128), shape(48, 256)), n_in=7, flops=10**8, nbytes=10**6
-    )(first.reshape(768, 128), back_joined, back_down, back_up, fine_weight, coarse_first, coarse_weight)
+        finish_body, (shape(768, 128), shape(48, 256)), n_in=9, flops=20 * 10**9, nbytes=10**6
+    )(first.reshape(768, 128), back_joined, back_down_soon, back_down, back_up_soon, back_up, fine_weight, coarse_first, coarse_weight)
     return (
         coarse_grad.reshape(coarse_features.shape),
         fine_grad.reshape(fine_features.shape),

time: 88.5 us -> 86.5 us (0.977)
  blocking collectives: 15.4 us -> 0 us
  starting transfers between devices: 45.6 us -> 58.1 us
    all_to_all x1 -> x0, blocking collectives: 15.4 us -> none  [local(): parts = lax.all_to_all(send, PLANE, 0, 0, tiled=True)]
    all_to_all x1 -> x2, starting transfers between devices: 11.2 us -> 19.9 us  [the longest x1 12.4 us: local(): lax.all_to_all(copies, 'z', 0, 0, axis_index_groups=[[(9 + i) % N_Z for i...]
    all_to_all x1, waiting for transfers between devices: 0.56 us -> 7.07 us  [local(): parts = lax.all_to_all(copies, PLANE, 0, 0, tiled=True)]
    ppermute x7 -> x9, waiting for transfers between devices: 10.1 us -> 4.96 us  [shifted(): return lax.ppermute(value, ALL, pairs)]
    ppermute x7 -> x9, starting transfers between devices: 24.5 us -> 27.4 us  [shifted(): return lax.ppermute(value, ALL, pairs)]
    all_to_all x1 -> x2, waiting for transfers between devices: 2.46 us -> 1.38 us  [the longest x1 1.37 us: local(): lax.all_to_all(copies, 'z', 0, 0, axis_index_groups=[[(9 + i) % N_Z for i...]
    all_to_all x1, starting transfers between devices: 6.3 us -> 7.27 us  [local(): parts = lax.all_to_all(copies, PLANE, 0, 0, tiled=True)]
  transfers between devices with their start and end apart: 10 -> 13, of which waited for: 7 -> 6; matrix products, arithmetic and copies ran while one was open for 0% -> 0% of each run, Pallas kernels for 7% -> 8%
where the time goes in v4:
time: 86.5 us; the launch traced here: 85.8 us
  starting transfers between devices  58.1 us (67%)
  waiting for transfers between devices  16.1 us (19%)
  Pallas kernels  10.7 us (12%)
    ppermute x9, starting transfers between devices, shifted(): return lax.ppermute(value, ALL, pairs)  27.4 us
    all_to_all x1, starting transfers between devices, local(): lax.all_to_all(copies, 'z', 0, 0, axis_index_groups=[[(9 + i) % N_Z for i...  12.4 us
    all_to_all x1, starting transfers between devices, local(): parts = lax.all_to_all(send, PLANE, 0, 0, tiled=True)  7.58 us
    all_to_all x1, starting transfers between devices, local(): parts = lax.all_to_all(copies, PLANE, 0, 0, tiled=True)  7.27 us
    all_to_all x1, waiting for transfers between devices, local(): parts = lax.all_to_all(copies, PLANE, 0, 0, tiled=True)  7.07 us
    ppermute x9, waiting for transfers between devices, shifted(): return lax.ppermute(value, ALL, pairs)  4.96 us
    all_to_all x1, starting transfers between devices, local(): here = lax.all_to_all(outgoing, ROWS, 0, 0, tiled=True)  3.56 us
    pallas_call x1, Pallas kernels, local(): call(fine_body, (shape(8, 96, 128, dtype=F32), shape(768, 128), shape(384...  3.44 us
  transfers between devices with their start and end apart: 13, of which 6 were waited for; matrix products, arithmetic and copies ran while one was open for 0% of the time, Pallas kernels for 8%

profile of v4, /device:TPU:1, one launch (start us, length us, event | category | flops | bytes accessed | tf_op | source)
XLA Modules:
  0.0 85.8 jit_solution(2180843380230663235)
XLA Ops:
  0.6 8.8 %collective-permute-start = (bf16[768,128]{1,0:T(8,128)(2,1)}, bf16[768,128]{1,0:T(8,128)(2,1)S(1)}, u32[]{:S(2)}, u32[]{:S(2)}) collective-permute-start(bf16[768,128]{1,0:T(8,128)(2,1)} %bitcast.10), channel_id=1, source_target_pairs={{8,0},{9,1},{10,2},{11,3},{12,4},{13,5},{14,6},{15,7},{16,8},{17,9... | collective-permute-start | bytes 589832 | tf_op jit(solution)/shard_map/ppermute | solution.py:241
  9.4 1.8 %shard_map.94 = bf16[8,64,256]{2,1,0:T(8,128)(2,1)} custom-call(bf16[48,256]{1,0:T(8,128)(2,1)} %bitcast.17, f32[2,768]{1,0:T(2,128)} %bitcast.12, f32[2,48]{1,0:T(2,128)} %bitcast.18), custom_call_target="tpu_custom_call" | custom-call | flops 1000000000 | bytes 1000000 | tf_op jit(solution)/shard_map/pallas_call | solution.py:252
  11.3 3.6 %all-to-all-start = ((bf16[8,64,256]{2,1,0:T(8,128)(2,1)}), bf16[8,64,256]{2,1,0:T(8,128)(2,1)S(1)}, u32[]{:S(2)}, u32[]{:S(2)}) async-start(bf16[8,64,256]{2,1,0:T(8,128)(2,1)} %shard_map.94), calls=%async_computation | async-start | bytes 524288 | tf_op jit(solution)/shard_map/all_to_all | solution.py:263
  14.9 2.8 %collective-permute-start.1 = (bf16[384,128]{1,0:T(8,128)(2,1)S(1)}, bf16[384,128]{1,0:T(8,128)(2,1)S(1)}, u32[]{:S(2)}, u32[]{:S(2)}) collective-permute-start(bf16[384,128]{1,0:T(8,128)(2,1)S(1)} %bitcast.16), channel_id=1, source_target_pairs={{8,1},{9,2},{10,3},{11,4},{12,5},{13,6},{14,7},{16,9},{17,10},{18,... | collective-permute-start | bytes 294920 | tf_op jit(solution)/shard_map/ppermute | solution.py:241
  17.7 1.3 %collective-permute-start.2 = (bf16[384,128]{1,0:T(8,128)(2,1)S(1)}, bf16[384,128]{1,0:T(8,128)(2,1)S(1)}, u32[]{:S(2)}, u32[]{:S(2)}) collective-permute-start(bf16[384,128]{1,0:T(8,128)(2,1)S(1)} %bitcast.15), channel_id=1, source_target_pairs={{9,0},{10,1},{11,2},{12,3},{13,4},{14,5},{15,6},{17,8},{18,9},{19,... | collective-permute-start | bytes 294920 | tf_op jit(solution)/shard_map/ppermute | solution.py:241
  19.0 2.6 %all-to-all-done.here = bf16[8,64,256]{2,1,0:T(8,128)(2,1)S(1)} async-done(((bf16[8,64,256]{2,1,0:T(8,128)(2,1)}), bf16[8,64,256]{2,1,0:T(8,128)(2,1)S(1)}, u32[]{:S(2)}, u32[]{:S(2)}) %all-to-all-start) | async-done | bytes 262176 | tf_op jit(solution)/shard_map/all_to_all | solution.py:263
  21.7 2.4 %collective-permute-start.3 = (bf16[8,64,256]{2,1,0:T(8,128)(2,1)S(1)}, bf16[8,64,256]{2,1,0:T(8,128)(2,1)S(1)}, u32[]{:S(2)}, u32[]{:S(2)}) collective-permute-start(bf16[8,64,256]{2,1,0:T(8,128)(2,1)S(1)} %all-to-all-done.here), channel_id=1, source_target_pairs={{8,0},{9,1},{10,2},{11,3},{12,4},{13,5},{14,6},{15,7},{16,8},{17,9... | collective-permute-start | bytes 786440 | tf_op jit(solution)/shard_map/ppermute | solution.py:241
  24.0 1.0 %collective-permute-done.2.below = bf16[384,128]{1,0:T(8,128)(2,1)S(1)} collective-permute-done((bf16[384,128]{1,0:T(8,128)(2,1)S(1)}, bf16[384,128]{1,0:T(8,128)(2,1)S(1)}, u32[]{:S(2)}, u32[]{:S(2)}) %collective-permute-start.2) | collective-permute-done | bytes 98336 | tf_op jit(solution)/shard_map/ppermute | solution.py:241
  25.0 3.4 %shard_map.93 = (f32[8,96,128]{2,1,0:T(8,128)S(1)}, bf16[768,128]{1,0:T(8,128)(2,1)S(1)}, bf16[384,128]{1,0:T(8,128)(2,1)S(1)}, bf16[384,128]{1,0:T(8,128)(2,1)S(1)}, f32[128,128]{1,0:T(8,128)S(1)}) custom-call(bf16[768,128]{1,0:T(8,128)(2,1)S(1)} %bitcast.11, bf16[768,128]{1,0:T(8,128)(2,1)S(1)} %collective-permute-done.middle, ...), custom_call_target="tpu_custom_call" | custom-call | flops 20000000000 | bytes 4000000 | tf_op jit(solution)/shard_map/pallas_call | solution.py:265
  28.5 2.4 %collective-permute-done.3.there = bf16[8,64,256]{2,1,0:T(8,128)(2,1)S(1)} collective-permute-done((bf16[8,64,256]{2,1,0:T(8,128)(2,1)S(1)}, bf16[8,64,256]{2,1,0:T(8,128)(2,1)S(1)}, u32[]{:S(2)}, u32[]{:S(2)}) %collective-permute-start.3) | collective-permute-done | bytes 262176 | tf_op jit(solution)/shard_map/ppermute | solution.py:241
  30.8 2.4 %shard_map.95 = (f32[48,256]{1,0:T(8,128)S(1)}, bf16[864,128]{1,0:T(8,128)(2,1)S(1)}, bf16[32,20,128]{2,1,0:T(8,128)(2,1)}) custom-call(s32[1]{0:T(128)} %bitcast.5.position, bf16[8,64,256]{2,1,0:T(8,128)(2,1)S(1)} %all-to-all-done.here, bf16[8,64,256]{2,1,0:T(8,128)(2,1)S(1)} %collective-permute-done.3.there, bf16[256,256]{1,0:T(8,128)(2,1)S(1)} %copy-done.1, ...), custom_call_target="tpu_custom_call" | custom-call | flops 3000000000 | bytes 2000000 | tf_op jit(solution)/shard_map/pallas_call | solution.py:279
  33.2 7.6 %all-to-all-start.1 = ((bf16[32,20,128]{2,1,0:T(8,128)(2,1)}), bf16[32,20,128]{2,1,0:T(8,128)(2,1)S(1)}, u32[]{:S(2)}, u32[]{:S(2)}) async-start(bf16[32,20,128]{2,1,0:T(8,128)(2,1)} %get-tuple-element.23), calls=%async_computation.1 | async-start | bytes 393216 | tf_op jit(solution)/shard_map/all_to_all | solution.py:290
  40.8 1.3 %collective-permute-start.5 = (bf16[384,128]{1,0:T(8,128)(2,1)S(1)}, bf16[384,128]{1,0:T(8,128)(2,1)S(1)}, u32[]{:S(2)}, u32[]{:S(2)}) collective-permute-start(bf16[384,128]{1,0:T(8,128)(2,1)S(1)} %get-tuple-element.24), channel_id=1, source_target_pairs={{1,8},{2,9},{3,10},{4,11},{5,12},{6,13},{7,14},{9,16},{10,17},{11,... | collective-permute-start | bytes 294920 | tf_op jit(solution)/shard_map/ppermute | solution.py:241
  42.1 6.0 %collective-permute-start.6 = (bf16[384,128]{1,0:T(8,128)(2,1)S(1)}, bf16[384,128]{1,0:T(8,128)(2,1)S(1)}, u32[]{:S(2)}, u32[]{:S(2)}) collective-permute-start(bf16[384,128]{1,0:T(8,128)(2,1)S(1)} %get-tuple-element.25), channel_id=1, source_target_pairs={{0,9},{1,10},{2,11},{3,12},{4,13},{5,14},{6,15},{8,17},{9,18},{10,... | collective-permute-start | bytes 294920 | tf_op jit(solution)/shard_map/ppermute | solution.py:241
  48.1 1.6 %collective-permute-done.6.above_soon = bf16[384,128]{1,0:T(8,128)(2,1)S(1)} collective-permute-done((bf16[384,128]{1,0:T(8,128)(2,1)S(1)}, bf16[384,128]{1,0:T(8,128)(2,1)S(1)}, u32[]{:S(2)}, u32[]{:S(2)}) %collective-permute-start.6) | collective-permute-done | bytes 98336 | tf_op jit(solution)/shard_map/ppermute | solution.py:241
  49.7 0.7 shard_map.97
  50.4 12.4 %all-to-all-start.2 = ((bf16[16,20,128]{2,1,0:T(8,128)(2,1)}), bf16[16,20,128]{2,1,0:T(8,128)(2,1)S(1)}, u32[]{:S(2)}, u32[]{:S(2)}) async-start(bf16[16,20,128]{2,1,0:T(8,128)(2,1)} %shard_map.97), calls=%async_computation.2 | async-start | bytes 196608 | tf_op jit(solution)/shard_map/all_to_all | solution.py:293
  62.8 3.5 %collective-permute-start.4 = (bf16[864,128]{1,0:T(8,128)(2,1)S(1)}, bf16[864,128]{1,0:T(8,128)(2,1)S(1)}, u32[]{:S(2)}, u32[]{:S(2)}) collective-permute-start(bf16[864,128]{1,0:T(8,128)(2,1)S(1)} %get-tuple-element.22), channel_id=1, source_target_pairs={{0,8},{1,9},{2,10},{3,11},{4,12},{5,13},{6,14},{7,15},{8,16},{9,17... | collective-permute-start | bytes 663560 | tf_op jit(solution)/shard_map/ppermute | solution.py:241
  67.6 1.4 %all-to-all-done.2.parts = bf16[16,20,128]{2,1,0:T(8,128)(2,1)S(1)} async-done(((bf16[16,20,128]{2,1,0:T(8,128)(2,1)}), bf16[16,20,128]{2,1,0:T(8,128)(2,1)S(1)}, u32[]{:S(2)}, u32[]{:S(2)}) %all-to-all-start.2) | async-done | bytes 81952 | tf_op jit(solution)/shard_map/all_to_all | solution.py:293
  69.0 0.7 shard_map.98
  69.7 7.3 %all-to-all-start.3 = ((bf16[32,20,128]{2,1,0:T(8,128)(2,1)}), bf16[32,20,128]{2,1,0:T(8,128)(2,1)S(1)}, u32[]{:S(2)}, u32[]{:S(2)}) async-start(bf16[32,20,128]{2,1,0:T(8,128)(2,1)} %shard_map.98), calls=%async_computation.3 | async-start | bytes 393216 | tf_op jit(solution)/shard_map/all_to_all | solution.py:295
  77.0 0.9 %shard_map.96 = (bf16[768,128]{1,0:T(8,128)(2,1)}, bf16[48,256]{1,0:T(8,128)(2,1)}) custom-call(f32[768,128]{1,0:T(8,128)S(1)} %bitcast.14, bf16[864,128]{1,0:T(8,128)(2,1)S(1)} %collective-permute-done.4.joined, bf16[384,128]{1,0:T(8,128)(2,1)S(1)} %collective-permute-done.6.above_soon, bf16[384,128]{1,0:T(8,128)(2,1)S(1)} %collective-permute-done.7.above_late, ...), custom_call_target="tpu_custom_call" | custom-call | flops 20000000000 | bytes 1000000 | tf_op jit(solution)/shard_map/pallas_call | solution.py:299
  78.0 7.1 %all-to-all-done.3.parts = bf16[32,20,128]{2,1,0:T(8,128)(2,1)S(1)} async-done(((bf16[32,20,128]{2,1,0:T(8,128)(2,1)}), bf16[32,20,128]{2,1,0:T(8,128)(2,1)S(1)}, u32[]{:S(2)}, u32[]{:S(2)}) %all-to-all-start.3) | async-done | bytes 163872 | tf_op jit(solution)/shard_map/all_to_all | solution.py:295
  85.0 0.7 shard_map.99
  (18 shorter events, 1.4 us)
Async XLA Ops:
  0.6 24.4 %collective-permute-start = (bf16[768,128]{1,0:T(8,128)(2,1)}, bf16[768,128]{1,0:T(8,128)(2,1)S(1)}, u32[]{:S(2)}, u32[]{:S(2)}) collective-permute-start(bf16[768,128]{1,0:T(8,128)(2,1)} %bitcast.10), channel_id=1, source_target_pairs={{8,0},{9,1},{10,2},{11,3},{12,4},{13,5},{14,6},{15,7},{16,8},{17,9... | collective-permute-start | bytes 589832 | tf_op jit(solution)/shard_map/ppermute | solution.py:241
  11.3 3.6 %copy-start = (bf16[1,8,96,128]{3,2,1,0:T(8,128)(2,1)S(1)}, bf16[1,8,96,128]{3,2,1,0:T(8,128)(2,1)}, u32[]{:S(2)}) copy-start(bf16[1,8,96,128]{3,2,1,0:T(8,128)(2,1)} %param.7) | copy-start | bytes 589828
  11.3 10.4 %all-to-all-start = ((bf16[8,64,256]{2,1,0:T(8,128)(2,1)}), bf16[8,64,256]{2,1,0:T(8,128)(2,1)S(1)}, u32[]{:S(2)}, u32[]{:S(2)}) async-start(bf16[8,64,256]{2,1,0:T(8,128)(2,1)} %shard_map.94), calls=%async_computation | async-start | bytes 524288 | tf_op jit(solution)/shard_map/all_to_all | solution.py:263
  14.8 10.2 %copy-start.2 = (bf16[128,128]{1,0:T(8,128)(2,1)S(1)}, bf16[128,128]{1,0:T(8,128)(2,1)}, u32[]{:S(2)}) copy-start(bf16[128,128]{1,0:T(8,128)(2,1)} %weight.5) | copy-start | bytes 98308
  14.9 9.2 %collective-permute-start.1 = (bf16[384,128]{1,0:T(8,128)(2,1)S(1)}, bf16[384,128]{1,0:T(8,128)(2,1)S(1)}, u32[]{:S(2)}, u32[]{:S(2)}) collective-permute-start(bf16[384,128]{1,0:T(8,128)(2,1)S(1)} %bitcast.16), channel_id=1, source_target_pairs={{8,1},{9,2},{10,3},{11,4},{12,5},{13,6},{14,7},{16,9},{17,10},{18,... | collective-permute-start | bytes 294920 | tf_op jit(solution)/shard_map/ppermute | solution.py:241
  17.7 7.3 %collective-permute-start.2 = (bf16[384,128]{1,0:T(8,128)(2,1)S(1)}, bf16[384,128]{1,0:T(8,128)(2,1)S(1)}, u32[]{:S(2)}, u32[]{:S(2)}) collective-permute-start(bf16[384,128]{1,0:T(8,128)(2,1)S(1)} %bitcast.15), channel_id=1, source_target_pairs={{9,0},{10,1},{11,2},{12,3},{13,4},{14,5},{15,6},{17,8},{18,9},{19,... | collective-permute-start | bytes 294920 | tf_op jit(solution)/shard_map/ppermute | solution.py:241
  19.0 6.0 %copy-start.3 = (f32[1,2,768]{2,1,0:T(2,128)S(1)}, f32[1,2,768]{2,1,0:T(2,128)}, u32[]{:S(2)}) copy-start(f32[1,2,768]{2,1,0:T(2,128)} %param.10) | copy-start | bytes 18436
  19.0 11.8 %copy-start.1 = (bf16[256,256]{1,0:T(8,128)(2,1)S(1)}, bf16[256,256]{1,0:T(8,128)(2,1)}, u32[]{:S(2)}) copy-start(bf16[256,256]{1,0:T(8,128)(2,1)} %coarse_weight.1) | copy-start | bytes 393220
  21.7 9.2 %collective-permute-start.3 = (bf16[8,64,256]{2,1,0:T(8,128)(2,1)S(1)}, bf16[8,64,256]{2,1,0:T(8,128)(2,1)S(1)}, u32[]{:S(2)}, u32[]{:S(2)}) collective-permute-start(bf16[8,64,256]{2,1,0:T(8,128)(2,1)S(1)} %all-to-all-done.here), channel_id=1, source_target_pairs={{8,0},{9,1},{10,2},{11,3},{12,4},{13,5},{14,6},{15,7},{16,8},{17,9... | collective-permute-start | bytes 786440 | tf_op jit(solution)/shard_map/ppermute | solution.py:241
  33.2 16.5 %all-to-all-start.1 = ((bf16[32,20,128]{2,1,0:T(8,128)(2,1)}), bf16[32,20,128]{2,1,0:T(8,128)(2,1)S(1)}, u32[]{:S(2)}, u32[]{:S(2)}) async-start(bf16[32,20,128]{2,1,0:T(8,128)(2,1)} %get-tuple-element.23), calls=%async_computation.1 | async-start | bytes 393216 | tf_op jit(solution)/shard_map/all_to_all | solution.py:290
  40.8 7.3 %collective-permute-start.5 = (bf16[384,128]{1,0:T(8,128)(2,1)S(1)}, bf16[384,128]{1,0:T(8,128)(2,1)S(1)}, u32[]{:S(2)}, u32[]{:S(2)}) collective-permute-start(bf16[384,128]{1,0:T(8,128)(2,1)S(1)} %get-tuple-element.24), channel_id=1, source_target_pairs={{1,8},{2,9},{3,10},{4,11},{5,12},{6,13},{7,14},{9,16},{10,17},{11,... | collective-permute-start | bytes 294920 | tf_op jit(solution)/shard_map/ppermute | solution.py:241
  42.1 7.6 %collective-permute-start.6 = (bf16[384,128]{1,0:T(8,128)(2,1)S(1)}, bf16[384,128]{1,0:T(8,128)(2,1)S(1)}, u32[]{:S(2)}, u32[]{:S(2)}) collective-permute-start(bf16[384,128]{1,0:T(8,128)(2,1)S(1)} %get-tuple-element.25), channel_id=1, source_target_pairs={{0,9},{1,10},{2,11},{3,12},{4,13},{5,14},{6,15},{8,17},{9,18},{10,... | collective-permute-start | bytes 294920 | tf_op jit(solution)/shard_map/ppermute | solution.py:241
  50.4 18.6 %all-to-all-start.2 = ((bf16[16,20,128]{2,1,0:T(8,128)(2,1)}), bf16[16,20,128]{2,1,0:T(8,128)(2,1)S(1)}, u32[]{:S(2)}, u32[]{:S(2)}) async-start(bf16[16,20,128]{2,1,0:T(8,128)(2,1)} %shard_map.97), calls=%async_computation.2 | async-start | bytes 196608 | tf_op jit(solution)/shard_map/all_to_all | solution.py:293
  62.8 14.2 %collective-permute-start.4 = (bf16[864,128]{1,0:T(8,128)(2,1)S(1)}, bf16[864,128]{1,0:T(8,128)(2,1)S(1)}, u32[]{:S(2)}, u32[]{:S(2)}) collective-permute-start(bf16[864,128]{1,0:T(8,128)(2,1)S(1)} %get-tuple-element.22), channel_id=1, source_target_pairs={{0,8},{1,9},{2,10},{3,11},{4,12},{5,13},{6,14},{7,15},{8,16},{9,17... | collective-permute-start | bytes 663560 | tf_op jit(solution)/shard_map/ppermute | solution.py:241
  66.3 10.7 %collective-permute-start.8 = (bf16[384,128]{1,0:T(8,128)(2,1)S(1)}, bf16[384,128]{1,0:T(8,128)(2,1)S(1)}, u32[]{:S(2)}, u32[]{:S(2)}) collective-permute-start(bf16[384,128]{1,0:T(8,128)(2,1)S(1)} %get-tuple-element.24), channel_id=1, source_target_pairs={{97,104},{98,105},{99,106},{100,107},{101,108},{102,109},{103,110}... | collective-permute-start | bytes 294920 | tf_op jit(solution)/shard_map/ppermute | solution.py:241
  67.0 10.1 %collective-permute-start.7 = (bf16[384,128]{1,0:T(8,128)(2,1)S(1)}, bf16[384,128]{1,0:T(8,128)(2,1)S(1)}, u32[]{:S(2)}, u32[]{:S(2)}) collective-permute-start(bf16[384,128]{1,0:T(8,128)(2,1)S(1)} %get-tuple-element.25), channel_id=1, source_target_pairs={{96,105},{97,106},{98,107},{99,108},{100,109},{101,110},{102,111},... | collective-permute-start | bytes 294920 | tf_op jit(solution)/shard_map/ppermute | solution.py:241
  69.7 15.3 %all-to-all-start.3 = ((bf16[32,20,128]{2,1,0:T(8,128)(2,1)}), bf16[32,20,128]{2,1,0:T(8,128)(2,1)S(1)}, u32[]{:S(2)}, u32[]{:S(2)}) async-start(bf16[32,20,128]{2,1,0:T(8,128)(2,1)} %shard_map.98), calls=%async_computation.3 | async-start | bytes 393216 | tf_op jit(solution)/shard_map/all_to_all | solution.py:295

commit v5 on v3

--- a/solution.py
+++ b/solution.py
@@ -16,14 +16,13 @@
 N_FRAMES, N_ROWS, N_PLANE, N_Z = 64, 8, 32, 16
 VMEM = pl.BlockSpec(memory_space=pltpu.VMEM)
 HBM = pl.BlockSpec(memory_space=pltpu.HBM)
-SMEM = pl.BlockSpec(memory_space=pltpu.SMEM)
-
-
-def call(body, outs, scratch=(), n_smem=0, n_in=0, flops=0, nbytes=0, kind=VMEM, room=40):
+
+
+def call(body, outs, scratch=(), n_in=0, flops=0, nbytes=0, kind=VMEM, room=40):
     return pl.pallas_call(
         body,
         out_shape=outs,
-        in_specs=[SMEM] * n_smem + [kind] * n_in,
+        in_specs=[kind] * n_in,
         out_specs=jax.tree.map(lambda _: VMEM, outs),
         scratch_shapes=list(scratch),
         compiler_params=pltpu.CompilerParams(vmem_limit_bytes=room * 1024 * 1024),
@@ -59,10 +58,16 @@
     return lax.broadcasted_iota(jnp.int32, dims, axis)
 
 
-def prepare_body(coarse_hbm, refined_hbm, back_hbm, out, cots, refined, back, sems):
+def key_frame_present():
+    frame = (lax.axis_index("z") * 2 + lax.axis_index("yh")) * 2 + lax.axis_index("core")
+    return jnp.minimum(frame, 1).astype(F32)
+
+
+def prepare_body(coarse_hbm, fine_hbm, refined_hbm, back_hbm, out, taken, cots, refined, back, sems):
     copies = [
         pltpu.make_async_copy(refined_hbm, refined, sems.at[N_ROWS]),
         pltpu.make_async_copy(back_hbm, back, sems.at[N_ROWS + 1]),
+        pltpu.make_async_copy(fine_hbm, taken.at[pl.ds(0, 768), :], sems.at[N_ROWS + 2]),
     ]
     for band in range(N_ROWS):
         copies.append(pltpu.make_async_copy(coarse_hbm, out.at[band, pl.ds(0, 48), :], sems.at[band]))
@@ -77,33 +82,43 @@
     cots[...] = jnp.zeros_like(cots)
     copies[0].wait()
     copies[1].wait()
-    hi, mid, rest = split3(refined[...])
-    cots[0:2, 0:128] = 4.0 * (mm(hi, pool) + (mm(mid, pool) + mm(rest, pool)))
+    terms = split3(refined[...])
+    for term in range(3):
+        wide = terms[term].astype(F32)
+        for k in range(6):
+            at = 16 + 16 * term + 2 * k
+            cots[at : at + 2, 0:128] = wide[:, 128 * k : 128 * k + 128]
+    cots[0:2, 0:128] = 4.0 * (mm(terms[0], pool) + (mm(terms[1], pool) + mm(terms[2], pool)))
     cots[2:4, 0:48] = back[...]
     hi, mid, rest = split3(cots[0:4, :])
     cots[0:4, :] = hi.astype(F32)
     cots[4:8, :] = mid.astype(F32)
     cots[8:12, :] = rest.astype(F32)
-    packed = cots[...].astype(BF16)
+    packed = cots[0:16, :].astype(BF16)
+    taken[768:816, :] = cots[16:64, 0:128].astype(BF16)
     for band in range(N_ROWS):
         out[band, 48:64, :] = packed
     for copy in copies[2:]:
         copy.wait()
 
 
-def fine_body(own, middle, above, below, weight, refined, first, mid_out, up_out, down_out, partial,
-              queries, keys, key_grad, turned, window):
+def fine_body(taken, own, above, below, weight, first_out, mid_out, up_out, down_out, partial,
+              first, queries, keys, key_grad, turned, window):
     scale = 1.0 / math.sqrt(128.0)
     w = weight[...]
-    queries[...] = mm(own[...], w).astype(BF16).reshape(8, 96, 128)
+    present = key_frame_present()
+    queries[...] = mm(taken[0:768, :], w).astype(BF16).reshape(8, 96, 128)
     keys[:, 0:16, :] = jnp.zeros((16, 16, 128), BF16)
     keys[:, 112:128, :] = jnp.zeros((16, 16, 128), BF16)
-    keys[0:4, 16:112, :] = mm(above[...], w).astype(BF16).reshape(4, 96, 128)
-    keys[4:12, 16:112, :] = mm(middle[...], w).astype(BF16).reshape(8, 96, 128)
-    keys[12:16, 16:112, :] = mm(below[...], w).astype(BF16).reshape(4, 96, 128)
+    keys[0:4, 16:112, :] = (mm(above[...], w) * present).astype(BF16).reshape(4, 96, 128)
+    keys[4:12, 16:112, :] = (mm(own[...], w) * present).astype(BF16).reshape(8, 96, 128)
+    keys[12:16, 16:112, :] = (mm(below[...], w) * present).astype(BF16).reshape(4, 96, 128)
     key_grad[...] = jnp.zeros_like(key_grad)
     turned[...] = jnp.zeros_like(turned)
-    turned[0:2, :] = refined[...]
+    terms = taken[768:816, :].astype(F32)
+    refined = terms[0:16, :] + (terms[16:32, :] + terms[32:48, :])
+    for k in range(6):
+        turned[0:2, 128 * k : 128 * k + 128] = refined[2 * k : 2 * k + 2, :]
     upright = jnp.transpose(turned[...], (1, 0))
     lane = iota((1, 128), 1)
     query_x = jnp.bitwise_and(lane, 31).astype(F32)
@@ -138,14 +153,15 @@
             )
             first[4 * part : 4 * part + 4, 32 * column : 32 * column + 32, :] = mm_tn(weights, k).reshape(4, 32, 128)
             key_grad[4 * part : 4 * part + 12, 32 * column : 32 * column + 64, :] += mm(weights, q).reshape(12, 64, 128)
-    up_out[...] = key_grad[0:4, 16:112, :].astype(BF16).reshape(384, 128)
-    mid_out[...] = key_grad[4:12, 16:112, :].astype(BF16).reshape(768, 128)
-    down_out[...] = key_grad[12:16, 16:112, :].astype(BF16).reshape(384, 128)
+    up_out[...] = (key_grad[0:4, 16:112, :] * present).astype(BF16).reshape(384, 128)
+    mid_out[...] = (key_grad[4:12, 16:112, :] * present).astype(BF16).reshape(768, 128)
+    down_out[...] = (key_grad[12:16, 16:112, :] * present).astype(BF16).reshape(384, 128)
     exact = first[...].reshape(768, 128)
     hi = exact.astype(BF16)
     low = (exact - hi.astype(F32)).astype(BF16)
-    total = mm_tn(own[...], hi) + mm_tn(own[...], low)
-    total = total + mm_tn(middle[...], mid_out[...])
+    first_out[...] = exact
+    total = mm_tn(taken[0:768, :], hi) + mm_tn(taken[0:768, :], low)
+    total = total + mm_tn(own[...], mid_out[...])
     partial[...] = total + mm_tn(above[...], up_out[...]) + mm_tn(below[...], down_out[...])
 
 
@@ -167,17 +183,17 @@
     return jnp.concatenate(lines, axis=0).astype(BF16)
 
 
-def coarse_body(position, here, there, weight, fine_partial, fine_middle, first, joined, send,
+def coarse_body(before, own, weight, fine_partial, fine_first, second, joined, send,
                 sums_first, sums_second, packed):
-    band = position[0]
+    band, present = lax.axis_index("x") * 2 + lax.axis_index("yl"), key_frame_present()
     w = weight[...]
-    qa = mm(here[:, 0:48, :].reshape(384, 256), w).astype(BF16)
-    qb = mm(there[:, 0:48, :].reshape(384, 256), w).astype(BF16)
+    qa = mm(before[:, 0:48, :].reshape(384, 256), w).astype(BF16)
+    qb = (mm(own[:, 0:48, :].reshape(384, 256), w) * present).astype(BF16)
     flat = jnp.zeros((16, 384), F32)
     ahead = iota((128, 384), 1) - iota((128, 384), 0)
     for source in range(N_ROWS):
         place = (ahead == 48 * source).astype(F32).astype(BF16)
-        flat = flat + mm(here[source, 48:64, 0:128], place)
+        flat = flat + mm(before[source, 48:64, 0:128], place)
     cots = flat[0:4, :] + (flat[4:8, :] + flat[8:12, :])
     forward_t = match(mm_nt(qb, qa), cots[0:1, :], cots[1:2, :])
     backward_t = match(mm_nt(qa, qb), cots[2:3, :], cots[3:4, :])
@@ -185,15 +201,15 @@
     sums_second[...] = mm(forward_t, qa) + mm_tn(backward_t, qa)
     mine = pl.ds(pl.multiple_of(band * 48, 16), 48)
     own_first = sums_first[mine, :]
-    own_second = sums_second[mine, :].astype(BF16)
-    first[...] = own_first
-    joined[0:768, :] = fine_middle[...]
-    joined[768:816, :] = own_second[:, 0:128]
-    joined[816:864, :] = own_second[:, 128:256]
+    own_second = (sums_second[mine, :] * present).astype(BF16)
+    second[...] = own_second
     hi = own_first.astype(BF16)
     low = (own_first - hi.astype(F32)).astype(BF16)
-    f_here = here[band, 0:48, :]
-    total = mm_tn(f_here, hi) + mm_tn(f_here, low) + mm_tn(there[band, 0:48, :], own_second)
+    joined[0:768, :] = fine_first[...]
+    joined[768:816, :] = own_first[:, 0:128]
+    joined[816:864, :] = own_first[:, 128:256]
+    f_before = before[band, 0:48, :]
+    total = mm_tn(f_before, hi) + mm_tn(f_before, low) + mm_tn(own[band, 0:48, :], own_second)
     packed[:, 0:8, :] = total[:, 0:128].reshape(N_PLANE, 8, 128)
     packed[:, 8:16, :] = total[:, 128:256].reshape(N_PLANE, 8, 128)
     for chunk in range(N_PLANE):
@@ -218,23 +234,24 @@
         fine[4 * chunk : 4 * chunk + 4, :] = values[chunk, 16:20, :]
 
 
-def finish_body(first, joined, from_above, from_below, weight, coarse_first, coarse_weight, fine_out, coarse_out):
-    total = first[...] + joined[0:768, :].astype(F32)
+def finish_body(returned, middle, from_above, from_below, weight, coarse_second, coarse_weight, fine_out, coarse_out):
     w = weight[...]
+    total = returned[0:768, :] + middle[...].astype(F32)
     top = (total[0:384, :] + from_above[...].astype(F32)).astype(BF16)
     bottom = (total[384:768, :] + from_below[...].astype(F32)).astype(BF16)
     fine_out[0:384, :] = mm_nt(top, w).astype(BF16)
     fine_out[384:768, :] = mm_nt(bottom, w).astype(BF16)
     w = coarse_weight[...]
-    left = (coarse_first[:, 0:128] + joined[768:816, :].astype(F32)).astype(BF16)
-    right = (coarse_first[:, 128:256] + joined[816:864, :].astype(F32)).astype(BF16)
+    second = coarse_second[...].astype(F32)
+    left = (returned[768:816, :] + second[:, 0:128]).astype(BF16)
+    right = (returned[816:864, :] + second[:, 128:256]).astype(BF16)
     coarse_out[...] = (mm_nt(left, w[:, 0:128]) + mm_nt(right, w[:, 128:256])).astype(BF16)
 
 
 def shifted(value, frames, rows):
     pairs = [
-        (f * N_ROWS + r, (f + frames) * N_ROWS + r + rows)
-        for f in range(max(0, -frames), min(N_FRAMES, N_FRAMES - frames))
+        (f * N_ROWS + r, (f + frames) % N_FRAMES * N_ROWS + r + rows)
+        for f in range(N_FRAMES)
         for r in range(max(0, -rows), min(N_ROWS, N_ROWS - rows))
     ]
     return lax.ppermute(value, ALL, pairs)
@@ -243,61 +260,59 @@
 def local(coarse_features, fine_features, coarse_weight, fine_weight, grad_refined, grad_back):
     coarse_own = coarse_features.reshape(48, 256)
     fine_own = fine_features.reshape(768, 128)
-    refined = grad_refined.reshape(2, 768)
-    band = lax.axis_index(ROWS).astype(jnp.int32).reshape(1)
-    middle = shifted(fine_own, -1, 0)
-    above = shifted(fine_own[384:768], -1, 1)
-    below = shifted(fine_own[0:384], -1, -1)
-    outgoing = call(
+    above = shifted(fine_own[384:768], 0, 1)
+    below = shifted(fine_own[0:384], 0, -1)
+    outgoing, taken = call(
         prepare_body,
-        shape(N_ROWS, 64, 256),
+        (shape(N_ROWS, 64, 256), shape(816, 128)),
         [
-            pltpu.VMEM((16, 256), F32),
+            pltpu.VMEM((64, 256), F32),
             pltpu.VMEM((2, 768), F32),
             pltpu.VMEM((2, 48), F32),
-            pltpu.SemaphoreType.DMA((N_ROWS + 2,)),
+            pltpu.SemaphoreType.DMA((N_ROWS + 3,)),
         ],
-        n_in=3, flops=10**9, nbytes=10**6, kind=HBM, room=60,
-    )(coarse_own, refined, grad_back.reshape(2, 48))
-    here = lax.all_to_all(outgoing, ROWS, 0, 0, tiled=True)
-    there = shifted(here, -1, 0)
-    first, mid_out, up_out, down_out, fine_partial = call(
+        n_in=4, flops=10**9, nbytes=10**6, kind=HBM, room=60,
+    )(coarse_own, fine_own, grad_refined.reshape(2, 768), grad_back.reshape(2, 48))
+    taken = shifted(taken, 1, 0)
+    own = lax.all_to_all(outgoing, ROWS, 0, 0, tiled=True)
+    before = shifted(own, 1, 0)
+    fine_first, middle, up_out, down_out, fine_partial = call(
         fine_body,
-        (shape(8, 96, 128, dtype=F32), shape(768, 128), shape(384, 128), shape(384, 128), shape(128, 128, dtype=F32)),
+        (shape(768, 128, dtype=F32), shape(768, 128), shape(384, 128), shape(384, 128), shape(128, 128, dtype=F32)),
         [
+            pltpu.VMEM((8, 96, 128), F32),
             pltpu.VMEM((8, 96, 128), BF16),
             pltpu.VMEM((16, 128, 128), BF16),
             pltpu.VMEM((16, 128, 128), F32),
             pltpu.VMEM((8, 768), F32),
             pltpu.VMEM((12, 64, 128), F32),
         ],
-        n_in=6, flops=20 * 10**9, nbytes=4 * 10**6,
-    )(fine_own, middle, above, below, fine_weight, refined)
-    back_up = shifted(up_out, 1, -1)
-    back_down = shifted(down_out, 1, 1)
-    coarse_first, joined, send = call(
+        n_in=5, flops=20 * 10**9, nbytes=4 * 10**6,
+    )(taken, fine_own, above, below, fine_weight)
+    back_up = shifted(up_out, 0, -1)
+    back_down = shifted(down_out, 0, 1)
+    coarse_second, joined, send = call(
         coarse_body,
-        (shape(48, 256, dtype=F32), shape(864, 128), shape(N_PLANE, 20, 128)),
+        (shape(48, 256), shape(864, 128, dtype=F32), shape(N_PLANE, 20, 128)),
         [
             pltpu.VMEM((384, 256), F32),
             pltpu.VMEM((384, 256), F32),
             pltpu.VMEM((N_PLANE, 24, 128), F32),
         ],
-        n_smem=1, n_in=5, flops=3 * 10**9, nbytes=2 * 10**6,
-    )(band, here, there, coarse_weight, fine_partial, mid_out)
-    back_joined = shifted(joined, 1, 0)
+        n_in=5, flops=3 * 10**9, nbytes=2 * 10**6,
+    )(before, own, coarse_weight, fine_partial, fine_first)
+    returned = shifted(joined, -1, 0)
     parts = lax.all_to_all(send, PLANE, 0, 0, tiled=True)
     copies = call(sum_body, shape(N_Z, 20, 128), n_in=1, nbytes=10**6)(parts)
-    parts = lax.all_to_all(copies, "z", 0, 0, tiled=True)
-    parts, back_up, back_joined = lax.optimization_barrier((parts, back_up, back_joined))
+    parts = lax.all_to_all(copies, "z", 0, 0, axis_index_groups=[[(9 + i) % N_Z for i in range(N_Z)]], tiled=True)
     copies = call(sum_body, shape(N_PLANE, 20, 128), n_in=1, nbytes=10**6)(parts)
     parts = lax.all_to_all(copies, PLANE, 0, 0, tiled=True)
     coarse_total, fine_total = call(
         unpack_body, (shape(256, 256, dtype=F32), shape(128, 128, dtype=F32)), n_in=1, nbytes=10**6
     )(parts)
     fine_grad, coarse_grad = call(
-        finish_body, (shape(768, 128), shape(48, 256)), n_in=7, flops=10**8, nbytes=10**6
-    )(first.reshape(768, 128), back_joined, back_down, back_up, fine_weight, coarse_first, coarse_weight)
+        finish_body, (shape(768, 128), shape(48, 256)), n_in=7, flops=20 * 10**9, nbytes=10**6
+    )(returned, middle, back_down, back_up, fine_weight, coarse_second, coarse_weight)
     return (
         coarse_grad.reshape(coarse_features.shape),
         fine_grad.reshape(fine_features.shape),

time: 88.5 us -> 85.3 us (0.964)
  blocking collectives: 15.4 us -> 0 us
  starting transfers between devices: 45.6 us -> 55.9 us
  waiting for transfers between devices: 15.8 us -> 17.1 us
    all_to_all x2 -> x3, starting transfers between devices: 14.8 us -> 31.6 us  [the longest x1 12.8 us: local(): lax.all_to_all(copies, 'z', 0, 0, axis_index_groups=[[(9 + i) % N_Z for i...]
    all_to_all x1 -> x0, blocking collectives: 15.4 us -> none  [local(): parts = lax.all_to_all(send, PLANE, 0, 0, tiled=True)]
    ppermute x7, waiting for transfers between devices: 10.1 us -> 1.96 us  [shifted(): return lax.ppermute(value, ALL, pairs)]
    all_to_all x1, waiting for transfers between devices: 0.56 us -> 7.08 us  [local(): parts = lax.all_to_all(copies, PLANE, 0, 0, tiled=True)]
    ppermute x7, starting transfers between devices: 24.5 us -> 18.6 us  [shifted(): return lax.ppermute(value, ALL, pairs)]
    all_to_all x2 -> x3, waiting for transfers between devices: 5.11 us -> 8.07 us  [the longest x1 5.88 us: local(): parts = lax.all_to_all(send, PLANE, 0, 0, tiled=True)]
  transfers between devices with their start and end apart: 10 -> 11, of which waited for: 7 -> 5; matrix products, arithmetic and copies ran while one was open for 0% -> 0% of each run, Pallas kernels for 7% -> 7%
where the time goes in v5:
time: 85.3 us; the launch traced here: 84.7 us
  starting transfers between devices  55.9 us (66%)
  waiting for transfers between devices  17.1 us (20%)
  Pallas kernels  10.8 us (13%)
    ppermute x7, starting transfers between devices, shifted(): return lax.ppermute(value, ALL, pairs)  18.6 us
    all_to_all x1, starting transfers between devices, local(): lax.all_to_all(copies, 'z', 0, 0, axis_index_groups=[[(9 + i) % N_Z for i...  12.8 us
    all_to_all x1, starting transfers between devices, local(): parts = lax.all_to_all(send, PLANE, 0, 0, tiled=True)  12.8 us
    all_to_all x1, waiting for transfers between devices, local(): parts = lax.all_to_all(copies, PLANE, 0, 0, tiled=True)  7.08 us
    all_to_all x1, starting transfers between devices, local(): own = lax.all_to_all(outgoing, ROWS, 0, 0, tiled=True)  6.01 us
    all_to_all x1, waiting for transfers between devices, local(): parts = lax.all_to_all(send, PLANE, 0, 0, tiled=True)  5.88 us
    all_to_all x1, starting transfers between devices, local(): parts = lax.all_to_all(copies, PLANE, 0, 0, tiled=True)  5.78 us
    pallas_call x1, Pallas kernels, local(): call(fine_body, (shape(768, 128, dtype=F32), shape(768, 128), shape(384,...  3.43 us
  transfers between devices with their start and end apart: 11, of which 5 were waited for; matrix products, arithmetic and copies ran while one was open for 0% of the time, Pallas kernels for 7%

profile of v5, /device:TPU:1, one launch (start us, length us, event | category | flops | bytes accessed | tf_op | source)
XLA Modules:
  0.0 84.7 jit_solution(10867815899907881443)
XLA Ops:
  0.6 1.9 %shard_map.93 = (bf16[8,64,256]{2,1,0:T(8,128)(2,1)}, bf16[816,128]{1,0:T(8,128)(2,1)}) custom-call(bf16[48,256]{1,0:T(8,128)(2,1)} %bitcast.12, bf16[768,128]{1,0:T(8,128)(2,1)} %bitcast.8, f32[2,768]{1,0:T(2,128)} %bitcast.13, f32[2,48]{1,0:T(2,128)} %bitcast.14), custom_call_target="tpu_custom_call" | custom-call | flops 1000000000 | bytes 1000000 | tf_op jit(solution)/shard_map/pallas_call | solution.py:265
  2.5 0.0 copy-start
  2.6 6.0 %all-to-all-start = ((bf16[8,64,256]{2,1,0:T(8,128)(2,1)}), bf16[8,64,256]{2,1,0:T(8,128)(2,1)S(1)}, u32[]{:S(2)}, u32[]{:S(2)}) async-start(bf16[8,64,256]{2,1,0:T(8,128)(2,1)} %get-tuple-element.18), calls=%async_computation | async-start | bytes 524288 | tf_op jit(solution)/shard_map/all_to_all | solution.py:277
  8.6 5.4 %collective-permute-start.1 = (bf16[816,128]{1,0:T(8,128)(2,1)S(1)}, bf16[816,128]{1,0:T(8,128)(2,1)S(1)}, u32[]{:S(2)}, u32[]{:S(2)}) collective-permute-start(bf16[816,128]{1,0:T(8,128)(2,1)S(1)} %copy-done.3), channel_id=1, source_target_pairs={{0,8},{1,9},{2,10},{3,11},{4,12},{5,13},{6,14},{7,15},{8,16},{9,17... | collective-permute-start | bytes 626696 | tf_op jit(solution)/shard_map/ppermute | solution.py:257
  14.0 3.2 %collective-permute-start.2 = (bf16[384,128]{1,0:T(8,128)(2,1)S(1)}, bf16[384,128]{1,0:T(8,128)(2,1)S(1)}, u32[]{:S(2)}, u32[]{:S(2)}) collective-permute-start(bf16[384,128]{1,0:T(8,128)(2,1)S(1)} %bitcast.11), channel_id=1, source_target_pairs={{0,1},{1,2},{2,3},{3,4},{4,5},{5,6},{6,7},{8,9},{9,10},{10,11},{11... | collective-permute-start | bytes 294920 | tf_op jit(solution)/shard_map/ppermute | solution.py:257
  17.2 1.4 %collective-permute-start.3 = (bf16[384,128]{1,0:T(8,128)(2,1)S(1)}, bf16[384,128]{1,0:T(8,128)(2,1)S(1)}, u32[]{:S(2)}, u32[]{:S(2)}) collective-permute-start(bf16[384,128]{1,0:T(8,128)(2,1)S(1)} %bitcast.10), channel_id=1, source_target_pairs={{1,0},{2,1},{3,2},{4,3},{5,4},{6,5},{7,6},{9,8},{10,9},{11,10},{12... | collective-permute-start | bytes 294920 | tf_op jit(solution)/shard_map/ppermute | solution.py:257
  18.6 2.8 %collective-permute-start = (bf16[8,64,256]{2,1,0:T(8,128)(2,1)S(1)}, bf16[8,64,256]{2,1,0:T(8,128)(2,1)S(1)}, u32[]{:S(2)}, u32[]{:S(2)}) collective-permute-start(bf16[8,64,256]{2,1,0:T(8,128)(2,1)S(1)} %all-to-all-done.own), channel_id=1, source_target_pairs={{0,8},{1,9},{2,10},{3,11},{4,12},{5,13},{6,14},{7,15},{8,16},{9,17... | collective-permute-start | bytes 786440 | tf_op jit(solution)/shard_map/ppermute | solution.py:257
  21.4 1.9 %collective-permute-done.3.below = bf16[384,128]{1,0:T(8,128)(2,1)S(1)} collective-permute-done((bf16[384,128]{1,0:T(8,128)(2,1)S(1)}, bf16[384,128]{1,0:T(8,128)(2,1)S(1)}, u32[]{:S(2)}, u32[]{:S(2)}) %collective-permute-start.3) | collective-permute-done | bytes 98336 | tf_op jit(solution)/shard_map/ppermute | solution.py:257
  23.3 3.4 %shard_map.94 = (f32[768,128]{1,0:T(8,128)S(1)}, bf16[768,128]{1,0:T(8,128)(2,1)S(1)}, bf16[384,128]{1,0:T(8,128)(2,1)S(1)}, bf16[384,128]{1,0:T(8,128)(2,1)S(1)}, f32[128,128]{1,0:T(8,128)S(1)}) custom-call(bf16[816,128]{1,0:T(8,128)(2,1)S(1)} %collective-permute-done.1.taken, bf16[768,128]{1,0:T(8,128)(2,1)S(1)} %bitcast.9, ...), custom_call_target="tpu_custom_call" | custom-call | flops 20000000000 | bytes 4000000 | tf_op jit(solution)/shard_map/pallas_call | solution.py:279
  26.7 0.1 collective-permute-done.before
  26.8 2.4 %shard_map.95 = (bf16[48,256]{1,0:T(8,128)(2,1)S(1)}, f32[864,128]{1,0:T(8,128)S(1)}, bf16[32,20,128]{2,1,0:T(8,128)(2,1)}) custom-call(bf16[8,64,256]{2,1,0:T(8,128)(2,1)S(1)} %collective-permute-done.before, bf16[8,64,256]{2,1,0:T(8,128)(2,1)S(1)} %all-to-all-done.own, bf16[256,256]{1,0:T(8,128)(2,1)S(1)} %copy-done.1, ...), custom_call_target="tpu_custom_call" | custom-call | flops 3000000000 | bytes 2000000 | tf_op jit(solution)/shard_map/pallas_call | solution.py:294
  29.2 12.8 %all-to-all-start.1 = ((bf16[32,20,128]{2,1,0:T(8,128)(2,1)}), bf16[32,20,128]{2,1,0:T(8,128)(2,1)S(1)}, u32[]{:S(2)}, u32[]{:S(2)}) async-start(bf16[32,20,128]{2,1,0:T(8,128)(2,1)} %get-tuple-element.29), calls=%async_computation.1 | async-start | bytes 393216 | tf_op jit(solution)/shard_map/all_to_all | solution.py:305
  42.0 2.1 %collective-permute-start.4 = (f32[864,128]{1,0:T(8,128)S(1)}, f32[864,128]{1,0:T(8,128)S(1)}, u32[]{:S(2)}, u32[]{:S(2)}) collective-permute-start(f32[864,128]{1,0:T(8,128)S(1)} %get-tuple-element.22), channel_id=1, source_target_pairs={{0,504},{1,505},{2,506},{3,507},{4,508},{5,509},{6,510},{7,511},{8... | collective-permute-start | bytes 1327112 | tf_op jit(solution)/shard_map/ppermute | solution.py:257
  44.1 5.9 %all-to-all-done.1.parts = bf16[32,20,128]{2,1,0:T(8,128)(2,1)S(1)} async-done(((bf16[32,20,128]{2,1,0:T(8,128)(2,1)}), bf16[32,20,128]{2,1,0:T(8,128)(2,1)S(1)}, u32[]{:S(2)}, u32[]{:S(2)}) %all-to-all-start.1) | async-done | bytes 163872 | tf_op jit(solution)/shard_map/all_to_all | solution.py:305
  50.0 0.7 shard_map.97
  50.7 12.8 %all-to-all-start.2 = ((bf16[16,20,128]{2,1,0:T(8,128)(2,1)}), bf16[16,20,128]{2,1,0:T(8,128)(2,1)S(1)}, u32[]{:S(2)}, u32[]{:S(2)}) async-start(bf16[16,20,128]{2,1,0:T(8,128)(2,1)} %shard_map.97), calls=%async_computation.2 | async-start | bytes 196608 | tf_op jit(solution)/shard_map/all_to_all | solution.py:307
  63.5 2.4 %collective-permute-start.5 = (bf16[384,128]{1,0:T(8,128)(2,1)S(1)}, bf16[384,128]{1,0:T(8,128)(2,1)S(1)}, u32[]{:S(2)}, u32[]{:S(2)}) collective-permute-start(bf16[384,128]{1,0:T(8,128)(2,1)S(1)} %get-tuple-element.24), channel_id=1, source_target_pairs={{0,1},{1,2},{2,3},{3,4},{4,5},{5,6},{6,7},{8,9},{9,10},{10,11},{11... | collective-permute-start | bytes 294920 | tf_op jit(solution)/shard_map/ppermute | solution.py:257
  65.9 1.3 %collective-permute-start.6 = (bf16[384,128]{1,0:T(8,128)(2,1)S(1)}, bf16[384,128]{1,0:T(8,128)(2,1)S(1)}, u32[]{:S(2)}, u32[]{:S(2)}) collective-permute-start(bf16[384,128]{1,0:T(8,128)(2,1)S(1)} %get-tuple-element.25), channel_id=1, source_target_pairs={{1,0},{2,1},{3,2},{4,3},{5,4},{6,5},{7,6},{9,8},{10,9},{11,10},{12... | collective-permute-start | bytes 294920 | tf_op jit(solution)/shard_map/ppermute | solution.py:257
  67.2 2.2 %all-to-all-done.2.parts = bf16[16,20,128]{2,1,0:T(8,128)(2,1)S(1)} async-done(((bf16[16,20,128]{2,1,0:T(8,128)(2,1)}), bf16[16,20,128]{2,1,0:T(8,128)(2,1)S(1)}, u32[]{:S(2)}, u32[]{:S(2)}) %all-to-all-start.2) | async-done | bytes 81952 | tf_op jit(solution)/shard_map/all_to_all | solution.py:307
  69.4 0.7 shard_map.98
  70.1 5.8 %all-to-all-start.3 = ((bf16[32,20,128]{2,1,0:T(8,128)(2,1)}), bf16[32,20,128]{2,1,0:T(8,128)(2,1)S(1)}, u32[]{:S(2)}, u32[]{:S(2)}) async-start(bf16[32,20,128]{2,1,0:T(8,128)(2,1)} %shard_map.98), calls=%async_computation.3 | async-start | bytes 393216 | tf_op jit(solution)/shard_map/all_to_all | solution.py:309
  75.9 0.9 %shard_map.96 = (bf16[768,128]{1,0:T(8,128)(2,1)}, bf16[48,256]{1,0:T(8,128)(2,1)}) custom-call(f32[864,128]{1,0:T(8,128)S(1)} %collective-permute-done.4.returned, bf16[768,128]{1,0:T(8,128)(2,1)S(1)} %get-tuple-element.23.middle, bf16[384,128]{1,0:T(8,128)(2,1)S(1)} %collective-permute-done.5.from_above, ...), custom_call_target="tpu_custom_call" | custom-call | flops 20000000000 | bytes 1000000 | tf_op jit(solution)/shard_map/pallas_call | solution.py:313
  76.8 7.1 %all-to-all-done.3.parts = bf16[32,20,128]{2,1,0:T(8,128)(2,1)S(1)} async-done(((bf16[32,20,128]{2,1,0:T(8,128)(2,1)}), bf16[32,20,128]{2,1,0:T(8,128)(2,1)S(1)}, u32[]{:S(2)}, u32[]{:S(2)}) %all-to-all-start.3) | async-done | bytes 163872 | tf_op jit(solution)/shard_map/all_to_all | solution.py:309
  83.9 0.7 shard_map.99
  (14 shorter events, 0.1 us)
Async XLA Ops:
  2.5 6.0 %copy-start.3 = (bf16[816,128]{1,0:T(8,128)(2,1)S(1)}, bf16[816,128]{1,0:T(8,128)(2,1)}, u32[]{:S(2)}) copy-start(bf16[816,128]{1,0:T(8,128)(2,1)} %get-tuple-element.19) | copy-start | bytes 626692
  2.5 11.4 %copy-start = (bf16[1,8,96,128]{3,2,1,0:T(8,128)(2,1)S(1)}, bf16[1,8,96,128]{3,2,1,0:T(8,128)(2,1)}, u32[]{:S(2)}) copy-start(bf16[1,8,96,128]{3,2,1,0:T(8,128)(2,1)} %param.7) | copy-start | bytes 589828
  2.6 16.0 %all-to-all-start = ((bf16[8,64,256]{2,1,0:T(8,128)(2,1)}), bf16[8,64,256]{2,1,0:T(8,128)(2,1)S(1)}, u32[]{:S(2)}, u32[]{:S(2)}) async-start(bf16[8,64,256]{2,1,0:T(8,128)(2,1)} %get-tuple-element.18), calls=%async_computation | async-start | bytes 524288 | tf_op jit(solution)/shard_map/all_to_all | solution.py:277
  8.6 14.7 %copy-start.2 = (bf16[128,128]{1,0:T(8,128)(2,1)S(1)}, bf16[128,128]{1,0:T(8,128)(2,1)}, u32[]{:S(2)}) copy-start(bf16[128,128]{1,0:T(8,128)(2,1)} %weight.5) | copy-start | bytes 98308
  8.6 14.7 %collective-permute-start.1 = (bf16[816,128]{1,0:T(8,128)(2,1)S(1)}, bf16[816,128]{1,0:T(8,128)(2,1)S(1)}, u32[]{:S(2)}, u32[]{:S(2)}) collective-permute-start(bf16[816,128]{1,0:T(8,128)(2,1)S(1)} %copy-done.3), channel_id=1, source_target_pairs={{0,8},{1,9},{2,10},{3,11},{4,12},{5,13},{6,14},{7,15},{8,16},{9,17... | collective-permute-start | bytes 626696 | tf_op jit(solution)/shard_map/ppermute | solution.py:257
  14.0 7.4 %collective-permute-start.2 = (bf16[384,128]{1,0:T(8,128)(2,1)S(1)}, bf16[384,128]{1,0:T(8,128)(2,1)S(1)}, u32[]{:S(2)}, u32[]{:S(2)}) collective-permute-start(bf16[384,128]{1,0:T(8,128)(2,1)S(1)} %bitcast.11), channel_id=1, source_target_pairs={{0,1},{1,2},{2,3},{3,4},{4,5},{5,6},{6,7},{8,9},{9,10},{10,11},{11... | collective-permute-start | bytes 294920 | tf_op jit(solution)/shard_map/ppermute | solution.py:257
  17.2 9.7 %copy-start.1 = (bf16[256,256]{1,0:T(8,128)(2,1)S(1)}, bf16[256,256]{1,0:T(8,128)(2,1)}, u32[]{:S(2)}) copy-start(bf16[256,256]{1,0:T(8,128)(2,1)} %coarse_weight.1) | copy-start | bytes 393220
  17.2 6.1 %collective-permute-start.3 = (bf16[384,128]{1,0:T(8,128)(2,1)S(1)}, bf16[384,128]{1,0:T(8,128)(2,1)S(1)}, u32[]{:S(2)}, u32[]{:S(2)}) collective-permute-start(bf16[384,128]{1,0:T(8,128)(2,1)S(1)} %bitcast.10), channel_id=1, source_target_pairs={{1,0},{2,1},{3,2},{4,3},{5,4},{6,5},{7,6},{9,8},{10,9},{11,10},{12... | collective-permute-start | bytes 294920 | tf_op jit(solution)/shard_map/ppermute | solution.py:257
  18.6 8.2 %collective-permute-start = (bf16[8,64,256]{2,1,0:T(8,128)(2,1)S(1)}, bf16[8,64,256]{2,1,0:T(8,128)(2,1)S(1)}, u32[]{:S(2)}, u32[]{:S(2)}) collective-permute-start(bf16[8,64,256]{2,1,0:T(8,128)(2,1)S(1)} %all-to-all-done.own), channel_id=1, source_target_pairs={{0,8},{1,9},{2,10},{3,11},{4,12},{5,13},{6,14},{7,15},{8,16},{9,17... | collective-permute-start | bytes 786440 | tf_op jit(solution)/shard_map/ppermute | solution.py:257
  29.2 20.8 %all-to-all-start.1 = ((bf16[32,20,128]{2,1,0:T(8,128)(2,1)}), bf16[32,20,128]{2,1,0:T(8,128)(2,1)S(1)}, u32[]{:S(2)}, u32[]{:S(2)}) async-start(bf16[32,20,128]{2,1,0:T(8,128)(2,1)} %get-tuple-element.29), calls=%async_computation.1 | async-start | bytes 393216 | tf_op jit(solution)/shard_map/all_to_all | solution.py:305
  42.0 33.9 %collective-permute-start.4 = (f32[864,128]{1,0:T(8,128)S(1)}, f32[864,128]{1,0:T(8,128)S(1)}, u32[]{:S(2)}, u32[]{:S(2)}) collective-permute-start(f32[864,128]{1,0:T(8,128)S(1)} %get-tuple-element.22), channel_id=1, source_target_pairs={{0,504},{1,505},{2,506},{3,507},{4,508},{5,509},{6,510},{7,511},{8... | collective-permute-start | bytes 1327112 | tf_op jit(solution)/shard_map/ppermute | solution.py:257
  50.7 18.7 %all-to-all-start.2 = ((bf16[16,20,128]{2,1,0:T(8,128)(2,1)}), bf16[16,20,128]{2,1,0:T(8,128)(2,1)S(1)}, u32[]{:S(2)}, u32[]{:S(2)}) async-start(bf16[16,20,128]{2,1,0:T(8,128)(2,1)} %shard_map.97), calls=%async_computation.2 | async-start | bytes 196608 | tf_op jit(solution)/shard_map/all_to_all | solution.py:307
  63.5 12.4 %collective-permute-start.5 = (bf16[384,128]{1,0:T(8,128)(2,1)S(1)}, bf16[384,128]{1,0:T(8,128)(2,1)S(1)}, u32[]{:S(2)}, u32[]{:S(2)}) collective-permute-start(bf16[384,128]{1,0:T(8,128)(2,1)S(1)} %get-tuple-element.24), channel_id=1, source_target_pairs={{0,1},{1,2},{2,3},{3,4},{4,5},{5,6},{6,7},{8,9},{9,10},{10,11},{11... | collective-permute-start | bytes 294920 | tf_op jit(solution)/shard_map/ppermute | solution.py:257
  65.9 10.0 %collective-permute-start.6 = (bf16[384,128]{1,0:T(8,128)(2,1)S(1)}, bf16[384,128]{1,0:T(8,128)(2,1)S(1)}, u32[]{:S(2)}, u32[]{:S(2)}) collective-permute-start(bf16[384,128]{1,0:T(8,128)(2,1)S(1)} %get-tuple-element.25), channel_id=1, source_target_pairs={{1,0},{2,1},{3,2},{4,3},{5,4},{6,5},{7,6},{9,8},{10,9},{11,10},{12... | collective-permute-start | bytes 294920 | tf_op jit(solution)/shard_map/ppermute | solution.py:257
  70.1 13.8 %all-to-all-start.3 = ((bf16[32,20,128]{2,1,0:T(8,128)(2,1)}), bf16[32,20,128]{2,1,0:T(8,128)(2,1)S(1)}, u32[]{:S(2)}, u32[]{:S(2)}) async-start(bf16[32,20,128]{2,1,0:T(8,128)(2,1)} %shard_map.98), calls=%async_computation.3 | async-start | bytes 393216 | tf_op jit(solution)/shard_map/all_to_all | solution.py:309

commit v6 on v5

--- a/solution.py
+++ b/solution.py
@@ -63,14 +63,13 @@
     return jnp.minimum(frame, 1).astype(F32)
 
 
-def prepare_body(coarse_hbm, fine_hbm, refined_hbm, back_hbm, out, taken, cots, refined, back, sems):
+def prepare_body(coarse_hbm, fine_hbm, refined_hbm, back_hbm, taken, cots, coarse, refined, back, sems):
     copies = [
-        pltpu.make_async_copy(refined_hbm, refined, sems.at[N_ROWS]),
-        pltpu.make_async_copy(back_hbm, back, sems.at[N_ROWS + 1]),
-        pltpu.make_async_copy(fine_hbm, taken.at[pl.ds(0, 768), :], sems.at[N_ROWS + 2]),
+        pltpu.make_async_copy(refined_hbm, refined, sems.at[0]),
+        pltpu.make_async_copy(back_hbm, back, sems.at[1]),
+        pltpu.make_async_copy(coarse_hbm, coarse, sems.at[2]),
+        pltpu.make_async_copy(fine_hbm, taken.at[pl.ds(0, 768), :], sems.at[3]),
     ]
-    for band in range(N_ROWS):
-        copies.append(pltpu.make_async_copy(coarse_hbm, out.at[band, pl.ds(0, 48), :], sems.at[band]))
     for copy in copies:
         copy.start()
     cell = iota((768, 128), 0)
@@ -86,20 +85,28 @@
     for term in range(3):
         wide = terms[term].astype(F32)
         for k in range(6):
-            at = 16 + 16 * term + 2 * k
-            cots[at : at + 2, 0:128] = wide[:, 128 * k : 128 * k + 128]
-    cots[0:2, 0:128] = 4.0 * (mm(terms[0], pool) + (mm(terms[1], pool) + mm(terms[2], pool)))
-    cots[2:4, 0:48] = back[...]
-    hi, mid, rest = split3(cots[0:4, :])
-    cots[0:4, :] = hi.astype(F32)
-    cots[4:8, :] = mid.astype(F32)
-    cots[8:12, :] = rest.astype(F32)
-    packed = cots[0:16, :].astype(BF16)
-    taken[768:816, :] = cots[16:64, 0:128].astype(BF16)
+            at = 16 * term + 2 * k
+            cots[at : at + 2, :] = wide[:, 128 * k : 128 * k + 128]
+    cots[48:50, :] = 4.0 * (mm(terms[0], pool) + (mm(terms[1], pool) + mm(terms[2], pool)))
+    cots[50:52, 0:48] = back[...]
+    hi, mid, rest = split3(cots[48:52, :])
+    cots[48:52, :] = hi.astype(F32)
+    cots[52:56, :] = mid.astype(F32)
+    cots[56:60, :] = rest.astype(F32)
+    taken[864:928, :] = cots[...].astype(BF16)
+    copies[2].wait()
+    taken[768:816, :] = coarse[:, 0:128]
+    taken[816:864, :] = coarse[:, 128:256]
+    copies[3].wait()
+
+
+def pack_body(coarse, taken, out):
+    before = jnp.concatenate([taken[768:816, :], taken[816:864, :]], axis=1)
+    cots = jnp.concatenate([taken[912:928, :], jnp.zeros((16, 128), BF16)], axis=1)
     for band in range(N_ROWS):
-        out[band, 48:64, :] = packed
-    for copy in copies[2:]:
-        copy.wait()
+        out[band, 0:48, :] = coarse[...]
+        out[band, 48:96, :] = before
+        out[band, 96:112, :] = cots
 
 
 def fine_body(taken, own, above, below, weight, first_out, mid_out, up_out, down_out, partial,
@@ -115,7 +122,7 @@
     keys[12:16, 16:112, :] = (mm(below[...], w) * present).astype(BF16).reshape(4, 96, 128)
     key_grad[...] = jnp.zeros_like(key_grad)
     turned[...] = jnp.zeros_like(turned)
-    terms = taken[768:816, :].astype(F32)
+    terms = taken[864:912, :].astype(F32)
     refined = terms[0:16, :] + (terms[16:32, :] + terms[32:48, :])
     for k in range(6):
         turned[0:2, 128 * k : 128 * k + 128] = refined[2 * k : 2 * k + 2, :]
@@ -183,17 +190,17 @@
     return jnp.concatenate(lines, axis=0).astype(BF16)
 
 
-def coarse_body(before, own, weight, fine_partial, fine_first, second, joined, send,
+def coarse_body(bands, weight, fine_partial, fine_first, second, joined, send,
                 sums_first, sums_second, packed):
     band, present = lax.axis_index("x") * 2 + lax.axis_index("yl"), key_frame_present()
     w = weight[...]
-    qa = mm(before[:, 0:48, :].reshape(384, 256), w).astype(BF16)
-    qb = (mm(own[:, 0:48, :].reshape(384, 256), w) * present).astype(BF16)
+    qa = mm(bands[:, 48:96, :].reshape(384, 256), w).astype(BF16)
+    qb = (mm(bands[:, 0:48, :].reshape(384, 256), w) * present).astype(BF16)
     flat = jnp.zeros((16, 384), F32)
     ahead = iota((128, 384), 1) - iota((128, 384), 0)
     for source in range(N_ROWS):
         place = (ahead == 48 * source).astype(F32).astype(BF16)
-        flat = flat + mm(before[source, 48:64, 0:128], place)
+        flat = flat + mm(bands[source, 96:112, 0:128], place)
     cots = flat[0:4, :] + (flat[4:8, :] + flat[8:12, :])
     forward_t = match(mm_nt(qb, qa), cots[0:1, :], cots[1:2, :])
     backward_t = match(mm_nt(qa, qb), cots[2:3, :], cots[3:4, :])
@@ -208,8 +215,8 @@
     joined[0:768, :] = fine_first[...]
     joined[768:816, :] = own_first[:, 0:128]
     joined[816:864, :] = own_first[:, 128:256]
-    f_before = before[band, 0:48, :]
-    total = mm_tn(f_before, hi) + mm_tn(f_before, low) + mm_tn(own[band, 0:48, :], own_second)
+    f_before = bands[band, 48:96, :]
+    total = mm_tn(f_before, hi) + mm_tn(f_before, low) + mm_tn(bands[band, 0:48, :], own_second)
     packed[:, 0:8, :] = total[:, 0:128].reshape(N_PLANE, 8, 128)
     packed[:, 8:16, :] = total[:, 128:256].reshape(N_PLANE, 8, 128)
     for chunk in range(N_PLANE):
@@ -260,22 +267,24 @@
 def local(coarse_features, fine_features, coarse_weight, fine_weight, grad_refined, grad_back):
     coarse_own = coarse_features.reshape(48, 256)
     fine_own = fine_features.reshape(768, 128)
-    above = shifted(fine_own[384:768], 0, 1)
-    below = shifted(fine_own[0:384], 0, -1)
-    outgoing, taken = call(
+    taken = call(
         prepare_body,
-        (shape(N_ROWS, 64, 256), shape(816, 128)),
+        shape(928, 128),
         [
-            pltpu.VMEM((64, 256), F32),
+            pltpu.VMEM((64, 128), F32),
+            pltpu.VMEM((48, 256), BF16),
             pltpu.VMEM((2, 768), F32),
             pltpu.VMEM((2, 48), F32),
-            pltpu.SemaphoreType.DMA((N_ROWS + 3,)),
+            pltpu.SemaphoreType.DMA((4,)),
         ],
         n_in=4, flops=10**9, nbytes=10**6, kind=HBM, room=60,
     )(coarse_own, fine_own, grad_refined.reshape(2, 768), grad_back.reshape(2, 48))
+    taken, rims = lax.optimization_barrier((taken, fine_own))
     taken = shifted(taken, 1, 0)
-    own = lax.all_to_all(outgoing, ROWS, 0, 0, tiled=True)
-    before = shifted(own, 1, 0)
+    above = shifted(rims[384:768], 0, 1)
+    below = shifted(rims[0:384], 0, -1)
+    outgoing = call(pack_body, shape(N_ROWS, 112, 256), n_in=2, nbytes=10**6)(coarse_own, taken)
+    bands = lax.all_to_all(outgoing, ROWS, 0, 0, tiled=True)
     fine_first, middle, up_out, down_out, fine_partial = call(
         fine_body,
         (shape(768, 128, dtype=F32), shape(768, 128), shape(384, 128), shape(384, 128), shape(128, 128, dtype=F32)),
@@ -299,8 +308,8 @@
             pltpu.VMEM((384, 256), F32),
             pltpu.VMEM((N_PLANE, 24, 128), F32),
         ],
-        n_in=5, flops=3 * 10**9, nbytes=2 * 10**6,
-    )(before, own, coarse_weight, fine_partial, fine_first)
+        n_in=4, flops=3 * 10**9, nbytes=2 * 10**6,
+    )(bands, coarse_weight, fine_partial, fine_first)
     returned = shifted(joined, -1, 0)
     parts = lax.all_to_all(send, PLANE, 0, 0, tiled=True)
     copies = call(sum_body, shape(N_Z, 20, 128), n_in=1, nbytes=10**6)(parts)

time: 85.3 us -> 84.5 us (level)
  starting transfers between devices: 55.9 us -> 53.1 us
  waiting for transfers between devices: 17.1 us -> 18.4 us
    all_to_all x1, waiting for transfers between devices: 0.01 us -> 3.12 us  [local(): bands = lax.all_to_all(outgoing, ROWS, 0, 0, tiled=True)]
    ppermute x7 -> x6, waiting for transfers between devices: 1.96 us -> 0.17 us  [shifted(): return lax.ppermute(value, ALL, pairs)]
    ppermute x7 -> x6, starting transfers between devices: 18.6 us -> 17.4 us  [shifted(): return lax.ppermute(value, ALL, pairs)]
    all_to_all x1, starting transfers between devices: 6.01 us -> 5.03 us  [local(): bands = lax.all_to_all(outgoing, ROWS, 0, 0, tiled=True)]
    pallas_call x1 -> x2, Pallas kernels: 1.89 us -> 2.55 us  [the longest x1 1.74 us: local(): call(prepare_body, shape(928, 128), [pltpu.VMEM((64, 128), F32), pltpu.VM...]
  transfers between devices with their start and end apart: 11 -> 10, of which waited for: 5 -> 5; matrix products, arithmetic and copies ran while one was open for 0% -> 0% of each run, Pallas kernels for 7% -> 8%
where the time goes in v6:
time: 84.5 us; the launch traced here: 83.8 us
  starting transfers between devices  53.1 us (63%)
  waiting for transfers between devices  18.4 us (22%)
  Pallas kernels  11.4 us (13%)
    ppermute x6, starting transfers between devices, shifted(): return lax.ppermute(value, ALL, pairs)  17.4 us
    all_to_all x1, starting transfers between devices, local(): parts = lax.all_to_all(send, PLANE, 0, 0, tiled=True)  12.5 us
    all_to_all x1, starting transfers between devices, local(): lax.all_to_all(copies, 'z', 0, 0, axis_index_groups=[[(9 + i) % N_Z for i...  12.5 us
    all_to_all x1, waiting for transfers between devices, local(): parts = lax.all_to_all(copies, PLANE, 0, 0, tiled=True)  7.08 us
    all_to_all x1, waiting for transfers between devices, local(): parts = lax.all_to_all(send, PLANE, 0, 0, tiled=True)  5.88 us
    all_to_all x1, starting transfers between devices, local(): parts = lax.all_to_all(copies, PLANE, 0, 0, tiled=True)  5.78 us
    all_to_all x1, starting transfers between devices, local(): bands = lax.all_to_all(outgoing, ROWS, 0, 0, tiled=True)  5.03 us
    pallas_call x1, Pallas kernels, local(): call(fine_body, (shape(768, 128, dtype=F32), shape(768, 128), shape(384,...  3.43 us
  transfers between devices with their start and end apart: 10, of which 5 were waited for; matrix products, arithmetic and copies ran while one was open for 0% of the time, Pallas kernels for 8%

profile of v6, /device:TPU:1, one launch (start us, length us, event | category | flops | bytes accessed | tf_op | source)
XLA Modules:
  0.0 83.8 jit_solution(17157752022137866542)
XLA Ops:
  0.6 1.7 %shard_map.93 = bf16[928,128]{1,0:T(8,128)(2,1)} custom-call(bf16[48,256]{1,0:T(8,128)(2,1)} %bitcast.9, bf16[768,128]{1,0:T(8,128)(2,1)} %bitcast.6, f32[2,768]{1,0:T(2,128)} %bitcast.11, f32[2,48]{1,0:T(2,128)} %bitcast.12), custom_call_target="tpu_custom_call" | custom-call | flops 1000000000 | bytes 1000000 | tf_op jit(solution)/shard_map/pallas_call | solution.py:270
  2.4 0.0 copy-start.1
  2.4 6.2 %collective-permute-start = (bf16[928,128]{1,0:T(8,128)(2,1)}, bf16[928,128]{1,0:T(8,128)(2,1)S(1)}, u32[]{:S(2)}, u32[]{:S(2)}) collective-permute-start(bf16[928,128]{1,0:T(8,128)(2,1)} %shard_map.93), channel_id=1, source_target_pairs={{0,8},{1,9},{2,10},{3,11},{4,12},{5,13},{6,14},{7,15},{8,16},{9,17... | collective-permute-start | bytes 712712 | tf_op jit(solution)/shard_map/ppermute | solution.py:264
  8.7 1.3 %collective-permute-start.2 = (bf16[384,128]{1,0:T(8,128)(2,1)S(1)}, bf16[384,128]{1,0:T(8,128)(2,1)S(1)}, u32[]{:S(2)}, u32[]{:S(2)}) collective-permute-start(bf16[384,128]{1,0:T(8,128)(2,1)S(1)} %get-tuple-element.32), channel_id=1, source_target_pairs={{1,0},{2,1},{3,2},{4,3},{5,4},{6,5},{7,6},{9,8},{10,9},{11,10},{12... | collective-permute-start | bytes 294920 | tf_op jit(solution)/shard_map/ppermute | solution.py:264
  10.0 4.0 %collective-permute-start.1 = (bf16[384,128]{1,0:T(8,128)(2,1)S(1)}, bf16[384,128]{1,0:T(8,128)(2,1)S(1)}, u32[]{:S(2)}, u32[]{:S(2)}) collective-permute-start(bf16[384,128]{1,0:T(8,128)(2,1)S(1)} %get-tuple-element.33), channel_id=1, source_target_pairs={{0,1},{1,2},{2,3},{3,4},{4,5},{5,6},{6,7},{8,9},{9,10},{10,11},{11... | collective-permute-start | bytes 294920 | tf_op jit(solution)/shard_map/ppermute | solution.py:264
  14.0 0.2 collective-permute-done.taken
  14.1 0.8 shard_map.94
  14.9 5.0 %all-to-all-start = ((bf16[8,112,256]{2,1,0:T(8,128)(2,1)}), bf16[8,112,256]{2,1,0:T(8,128)(2,1)S(1)}, u32[]{:S(2)}, u32[]{:S(2)}) async-start(bf16[8,112,256]{2,1,0:T(8,128)(2,1)} %shard_map.94), calls=%async_computation | async-start | bytes 917504 | tf_op jit(solution)/shard_map/all_to_all | solution.py:287
  20.0 3.4 %shard_map.95 = (f32[768,128]{1,0:T(8,128)S(1)}, bf16[768,128]{1,0:T(8,128)(2,1)S(1)}, bf16[384,128]{1,0:T(8,128)(2,1)S(1)}, bf16[384,128]{1,0:T(8,128)(2,1)S(1)}, f32[128,128]{1,0:T(8,128)S(1)}) custom-call(bf16[928,128]{1,0:T(8,128)(2,1)S(1)} %collective-permute-done.taken, bf16[768,128]{1,0:T(8,128)(2,1)S(1)} %bitcast.8, ...), custom_call_target="tpu_custom_call" | custom-call | flops 20000000000 | bytes 4000000 | tf_op jit(solution)/shard_map/pallas_call | solution.py:288
  23.4 3.1 %all-to-all-done.bands = bf16[8,112,256]{2,1,0:T(8,128)(2,1)S(1)} async-done(((bf16[8,112,256]{2,1,0:T(8,128)(2,1)}), bf16[8,112,256]{2,1,0:T(8,128)(2,1)S(1)}, u32[]{:S(2)}, u32[]{:S(2)}) %all-to-all-start) | async-done | bytes 458784 | tf_op jit(solution)/shard_map/all_to_all | solution.py:287
  26.5 2.4 %shard_map.96 = (bf16[48,256]{1,0:T(8,128)(2,1)S(1)}, f32[864,128]{1,0:T(8,128)S(1)}, bf16[32,20,128]{2,1,0:T(8,128)(2,1)}) custom-call(bf16[8,112,256]{2,1,0:T(8,128)(2,1)S(1)} %all-to-all-done.bands, bf16[256,256]{1,0:T(8,128)(2,1)S(1)} %copy-done.2, f32[128,128]{1,0:T(8,128)S(1)} %get-tuple-element.20.fine_partial, ...), custom_call_target="tpu_custom_call" | custom-call | flops 3000000000 | bytes 2000000 | tf_op jit(solution)/shard_map/pallas_call | solution.py:303
  28.9 12.5 %all-to-all-start.1 = ((bf16[32,20,128]{2,1,0:T(8,128)(2,1)}), bf16[32,20,128]{2,1,0:T(8,128)(2,1)S(1)}, u32[]{:S(2)}, u32[]{:S(2)}) async-start(bf16[32,20,128]{2,1,0:T(8,128)(2,1)} %get-tuple-element.29), calls=%async_computation.1 | async-start | bytes 393216 | tf_op jit(solution)/shard_map/all_to_all | solution.py:314
  41.4 2.2 %collective-permute-start.3 = (f32[864,128]{1,0:T(8,128)S(1)}, f32[864,128]{1,0:T(8,128)S(1)}, u32[]{:S(2)}, u32[]{:S(2)}) collective-permute-start(f32[864,128]{1,0:T(8,128)S(1)} %get-tuple-element.22), channel_id=1, source_target_pairs={{0,504},{1,505},{2,506},{3,507},{4,508},{5,509},{6,510},{7,511},{8... | collective-permute-start | bytes 1327112 | tf_op jit(solution)/shard_map/ppermute | solution.py:264
  43.6 5.9 %all-to-all-done.1.parts = bf16[32,20,128]{2,1,0:T(8,128)(2,1)S(1)} async-done(((bf16[32,20,128]{2,1,0:T(8,128)(2,1)}), bf16[32,20,128]{2,1,0:T(8,128)(2,1)S(1)}, u32[]{:S(2)}, u32[]{:S(2)}) %all-to-all-start.1) | async-done | bytes 163872 | tf_op jit(solution)/shard_map/all_to_all | solution.py:314
  49.5 0.7 shard_map.98
  50.2 12.5 %all-to-all-start.2 = ((bf16[16,20,128]{2,1,0:T(8,128)(2,1)}), bf16[16,20,128]{2,1,0:T(8,128)(2,1)S(1)}, u32[]{:S(2)}, u32[]{:S(2)}) async-start(bf16[16,20,128]{2,1,0:T(8,128)(2,1)} %shard_map.98), calls=%async_computation.2 | async-start | bytes 196608 | tf_op jit(solution)/shard_map/all_to_all | solution.py:316
  62.6 2.4 %collective-permute-start.4 = (bf16[384,128]{1,0:T(8,128)(2,1)S(1)}, bf16[384,128]{1,0:T(8,128)(2,1)S(1)}, u32[]{:S(2)}, u32[]{:S(2)}) collective-permute-start(bf16[384,128]{1,0:T(8,128)(2,1)S(1)} %get-tuple-element.24), channel_id=1, source_target_pairs={{0,1},{1,2},{2,3},{3,4},{4,5},{5,6},{6,7},{8,9},{9,10},{10,11},{11... | collective-permute-start | bytes 294920 | tf_op jit(solution)/shard_map/ppermute | solution.py:264
  65.0 1.3 %collective-permute-start.5 = (bf16[384,128]{1,0:T(8,128)(2,1)S(1)}, bf16[384,128]{1,0:T(8,128)(2,1)S(1)}, u32[]{:S(2)}, u32[]{:S(2)}) collective-permute-start(bf16[384,128]{1,0:T(8,128)(2,1)S(1)} %get-tuple-element.25), channel_id=1, source_target_pairs={{1,0},{2,1},{3,2},{4,3},{5,4},{6,5},{7,6},{9,8},{10,9},{11,10},{12... | collective-permute-start | bytes 294920 | tf_op jit(solution)/shard_map/ppermute | solution.py:264
  66.3 2.2 %all-to-all-done.2.parts = bf16[16,20,128]{2,1,0:T(8,128)(2,1)S(1)} async-done(((bf16[16,20,128]{2,1,0:T(8,128)(2,1)}), bf16[16,20,128]{2,1,0:T(8,128)(2,1)S(1)}, u32[]{:S(2)}, u32[]{:S(2)}) %all-to-all-start.2) | async-done | bytes 81952 | tf_op jit(solution)/shard_map/all_to_all | solution.py:316
  68.5 0.7 shard_map.99
  69.2 5.8 %all-to-all-start.3 = ((bf16[32,20,128]{2,1,0:T(8,128)(2,1)}), bf16[32,20,128]{2,1,0:T(8,128)(2,1)S(1)}, u32[]{:S(2)}, u32[]{:S(2)}) async-start(bf16[32,20,128]{2,1,0:T(8,128)(2,1)} %shard_map.99), calls=%async_computation.3 | async-start | bytes 393216 | tf_op jit(solution)/shard_map/all_to_all | solution.py:318
  75.1 0.9 %shard_map.97 = (bf16[768,128]{1,0:T(8,128)(2,1)}, bf16[48,256]{1,0:T(8,128)(2,1)}) custom-call(f32[864,128]{1,0:T(8,128)S(1)} %collective-permute-done.3.returned, bf16[768,128]{1,0:T(8,128)(2,1)S(1)} %get-tuple-element.23.middle, bf16[384,128]{1,0:T(8,128)(2,1)S(1)} %collective-permute-done.4.from_above, ...), custom_call_target="tpu_custom_call" | custom-call | flops 20000000000 | bytes 1000000 | tf_op jit(solution)/shard_map/pallas_call | solution.py:322
  76.0 7.1 %all-to-all-done.3.parts = bf16[32,20,128]{2,1,0:T(8,128)(2,1)S(1)} async-done(((bf16[32,20,128]{2,1,0:T(8,128)(2,1)}), bf16[32,20,128]{2,1,0:T(8,128)(2,1)S(1)}, u32[]{:S(2)}, u32[]{:S(2)}) %all-to-all-start.3) | async-done | bytes 163872 | tf_op jit(solution)/shard_map/all_to_all | solution.py:318
  83.1 0.7 shard_map.100
  (13 shorter events, 0.0 us)
Async XLA Ops:
  0.6 8.0 %copy-start = (bf16[1,8,96,128]{3,2,1,0:T(8,128)(2,1)S(1)}, bf16[1,8,96,128]{3,2,1,0:T(8,128)(2,1)}, u32[]{:S(2)}) copy-start(bf16[1,8,96,128]{3,2,1,0:T(8,128)(2,1)} %param.7) | copy-start | bytes 589828
  2.4 11.7 %copy-start.1 = (bf16[1,2,24,256]{3,2,1,0:T(8,128)(2,1)S(1)}, bf16[1,2,24,256]{3,2,1,0:T(8,128)(2,1)}, u32[]{:S(2)}) copy-start(bf16[1,2,24,256]{3,2,1,0:T(8,128)(2,1)} %param.6) | copy-start | bytes 73732
  2.4 11.7 %collective-permute-start = (bf16[928,128]{1,0:T(8,128)(2,1)}, bf16[928,128]{1,0:T(8,128)(2,1)S(1)}, u32[]{:S(2)}, u32[]{:S(2)}) collective-permute-start(bf16[928,128]{1,0:T(8,128)(2,1)} %shard_map.93), channel_id=1, source_target_pairs={{0,8},{1,9},{2,10},{3,11},{4,12},{5,13},{6,14},{7,15},{8,16},{9,17... | collective-permute-start | bytes 712712 | tf_op jit(solution)/shard_map/ppermute | solution.py:264
  8.7 11.3 %collective-permute-start.2 = (bf16[384,128]{1,0:T(8,128)(2,1)S(1)}, bf16[384,128]{1,0:T(8,128)(2,1)S(1)}, u32[]{:S(2)}, u32[]{:S(2)}) collective-permute-start(bf16[384,128]{1,0:T(8,128)(2,1)S(1)} %get-tuple-element.32), channel_id=1, source_target_pairs={{1,0},{2,1},{3,2},{4,3},{5,4},{6,5},{7,6},{9,8},{10,9},{11,10},{12... | collective-permute-start | bytes 294920 | tf_op jit(solution)/shard_map/ppermute | solution.py:264
  10.0 10.0 %collective-permute-start.1 = (bf16[384,128]{1,0:T(8,128)(2,1)S(1)}, bf16[384,128]{1,0:T(8,128)(2,1)S(1)}, u32[]{:S(2)}, u32[]{:S(2)}) collective-permute-start(bf16[384,128]{1,0:T(8,128)(2,1)S(1)} %get-tuple-element.33), channel_id=1, source_target_pairs={{0,1},{1,2},{2,3},{3,4},{4,5},{5,6},{6,7},{8,9},{9,10},{10,11},{11... | collective-permute-start | bytes 294920 | tf_op jit(solution)/shard_map/ppermute | solution.py:264
  14.9 5.1 %copy-start.3 = (bf16[128,128]{1,0:T(8,128)(2,1)S(1)}, bf16[128,128]{1,0:T(8,128)(2,1)}, u32[]{:S(2)}) copy-start(bf16[128,128]{1,0:T(8,128)(2,1)} %weight.5) | copy-start | bytes 98308
  14.9 11.6 %all-to-all-start = ((bf16[8,112,256]{2,1,0:T(8,128)(2,1)}), bf16[8,112,256]{2,1,0:T(8,128)(2,1)S(1)}, u32[]{:S(2)}, u32[]{:S(2)}) async-start(bf16[8,112,256]{2,1,0:T(8,128)(2,1)} %shard_map.94), calls=%async_computation | async-start | bytes 917504 | tf_op jit(solution)/shard_map/all_to_all | solution.py:287
  19.9 6.6 %copy-start.2 = (bf16[256,256]{1,0:T(8,128)(2,1)S(1)}, bf16[256,256]{1,0:T(8,128)(2,1)}, u32[]{:S(2)}) copy-start(bf16[256,256]{1,0:T(8,128)(2,1)} %coarse_weight.1) | copy-start | bytes 393220
  28.9 20.6 %all-to-all-start.1 = ((bf16[32,20,128]{2,1,0:T(8,128)(2,1)}), bf16[32,20,128]{2,1,0:T(8,128)(2,1)S(1)}, u32[]{:S(2)}, u32[]{:S(2)}) async-start(bf16[32,20,128]{2,1,0:T(8,128)(2,1)} %get-tuple-element.29), calls=%async_computation.1 | async-start | bytes 393216 | tf_op jit(solution)/shard_map/all_to_all | solution.py:314
  41.4 33.7 %collective-permute-start.3 = (f32[864,128]{1,0:T(8,128)S(1)}, f32[864,128]{1,0:T(8,128)S(1)}, u32[]{:S(2)}, u32[]{:S(2)}) collective-permute-start(f32[864,128]{1,0:T(8,128)S(1)} %get-tuple-element.22), channel_id=1, source_target_pairs={{0,504},{1,505},{2,506},{3,507},{4,508},{5,509},{6,510},{7,511},{8... | collective-permute-start | bytes 1327112 | tf_op jit(solution)/shard_map/ppermute | solution.py:264
  50.2 18.3 %all-to-all-start.2 = ((bf16[16,20,128]{2,1,0:T(8,128)(2,1)}), bf16[16,20,128]{2,1,0:T(8,128)(2,1)S(1)}, u32[]{:S(2)}, u32[]{:S(2)}) async-start(bf16[16,20,128]{2,1,0:T(8,128)(2,1)} %shard_map.98), calls=%async_computation.2 | async-start | bytes 196608 | tf_op jit(solution)/shard_map/all_to_all | solution.py:316
  62.6 12.4 %collective-permute-start.4 = (bf16[384,128]{1,0:T(8,128)(2,1)S(1)}, bf16[384,128]{1,0:T(8,128)(2,1)S(1)}, u32[]{:S(2)}, u32[]{:S(2)}) collective-permute-start(bf16[384,128]{1,0:T(8,128)(2,1)S(1)} %get-tuple-element.24), channel_id=1, source_target_pairs={{0,1},{1,2},{2,3},{3,4},{4,5},{5,6},{6,7},{8,9},{9,10},{10,11},{11... | collective-permute-start | bytes 294920 | tf_op jit(solution)/shard_map/ppermute | solution.py:264
  65.0 10.0 %collective-permute-start.5 = (bf16[384,128]{1,0:T(8,128)(2,1)S(1)}, bf16[384,128]{1,0:T(8,128)(2,1)S(1)}, u32[]{:S(2)}, u32[]{:S(2)}) collective-permute-start(bf16[384,128]{1,0:T(8,128)(2,1)S(1)} %get-tuple-element.25), channel_id=1, source_target_pairs={{1,0},{2,1},{3,2},{4,3},{5,4},{6,5},{7,6},{9,8},{10,9},{11,10},{12... | collective-permute-start | bytes 294920 | tf_op jit(solution)/shard_map/ppermute | solution.py:264
  69.2 13.8 %all-to-all-start.3 = ((bf16[32,20,128]{2,1,0:T(8,128)(2,1)}), bf16[32,20,128]{2,1,0:T(8,128)(2,1)S(1)}, u32[]{:S(2)}, u32[]{:S(2)}) async-start(bf16[32,20,128]{2,1,0:T(8,128)(2,1)} %shard_map.99), calls=%async_computation.3 | async-start | bytes 393216 | tf_op jit(solution)/shard_map/all_to_all | solution.py:318

commit v7 on v6

--- a/solution.py
+++ b/solution.py
@@ -100,11 +100,13 @@
     copies[3].wait()
 
 
-def pack_body(coarse, taken, out):
-    before = jnp.concatenate([taken[768:816, :], taken[816:864, :]], axis=1)
+def pack_body(coarse, taken, weight, out):
+    w = weight[...]
+    own = (mm(coarse[...], w) * key_frame_present()).astype(BF16)
+    before = (mm(taken[768:816, :], w[0:128, :]) + mm(taken[816:864, :], w[128:256, :])).astype(BF16)
     cots = jnp.concatenate([taken[912:928, :], jnp.zeros((16, 128), BF16)], axis=1)
     for band in range(N_ROWS):
-        out[band, 0:48, :] = coarse[...]
+        out[band, 0:48, :] = own
         out[band, 48:96, :] = before
         out[band, 96:112, :] = cots
 
@@ -142,9 +144,9 @@
             pieces = [(4 * part + line) * 96 + 32 * column for line in range(4)]
             cot = jnp.transpose(jnp.concatenate([upright[at : at + 32, :] for at in pieces], axis=0), (1, 0))
             gx, gy = cot[0:1, :], cot[1:2, :]
-            s = mm_nt(k, q).reshape(12, 64, 128) * (scale * math.log2(math.e)) + window[...]
+            s = mm_nt(k, q).reshape(12, 64, 128) + window[...]
             top = jnp.max(jnp.max(s, axis=0), axis=0, keepdims=True)
-            e = jnp.exp2(s - top)
+            e = jnp.exp2((s - top) * (scale * math.log2(math.e)))
             by_x = jnp.sum(e, axis=0)
             inverse = 1.0 / jnp.sum(by_x, axis=0, keepdims=True)
             mean_x = jnp.sum(by_x * key_x, axis=0, keepdims=True) * inverse
@@ -173,8 +175,7 @@
 
 
 def match(scores, cot_x, cot_y):
-    s = scores * (math.log2(math.e) / 16.0)
-    e = jnp.exp2(s - jnp.max(s, axis=0, keepdims=True)).reshape(16, 24, 384)
+    e = jnp.exp2((scores - jnp.max(scores, axis=0, keepdims=True)) * (math.log2(math.e) / 16.0)).reshape(16, 24, 384)
     by_x = jnp.sum(e, axis=0)
     inverse = 1.0 / jnp.sum(by_x, axis=0, keepdims=True)
     key_x = iota((24, 384), 0).astype(F32)
@@ -190,12 +191,11 @@
     return jnp.concatenate(lines, axis=0).astype(BF16)
 
 
-def coarse_body(bands, weight, fine_partial, fine_first, second, joined, send,
+def coarse_body(bands, coarse, taken, fine_partial, fine_first, second, joined, send,
                 sums_first, sums_second, packed):
     band, present = lax.axis_index("x") * 2 + lax.axis_index("yl"), key_frame_present()
-    w = weight[...]
-    qa = mm(bands[:, 48:96, :].reshape(384, 256), w).astype(BF16)
-    qb = (mm(bands[:, 0:48, :].reshape(384, 256), w) * present).astype(BF16)
+    qa = bands[:, 48:96, :].reshape(384, 256)
+    qb = bands[:, 0:48, :].reshape(384, 256)
     flat = jnp.zeros((16, 384), F32)
     ahead = iota((128, 384), 1) - iota((128, 384), 0)
     for source in range(N_ROWS):
@@ -215,8 +215,8 @@
     joined[0:768, :] = fine_first[...]
     joined[768:816, :] = own_first[:, 0:128]
     joined[816:864, :] = own_first[:, 128:256]
-    f_before = bands[band, 48:96, :]
-    total = mm_tn(f_before, hi) + mm_tn(f_before, low) + mm_tn(bands[band, 0:48, :], own_second)
+    f_before = jnp.concatenate([taken[768:816, :], taken[816:864, :]], axis=1)
+    total = mm_tn(f_before, hi) + mm_tn(f_before, low) + mm_tn(coarse[...], own_second)
     packed[:, 0:8, :] = total[:, 0:128].reshape(N_PLANE, 8, 128)
     packed[:, 8:16, :] = total[:, 128:256].reshape(N_PLANE, 8, 128)
     for chunk in range(N_PLANE):
@@ -283,7 +283,7 @@
     taken = shifted(taken, 1, 0)
     above = shifted(rims[384:768], 0, 1)
     below = shifted(rims[0:384], 0, -1)
-    outgoing = call(pack_body, shape(N_ROWS, 112, 256), n_in=2, nbytes=10**6)(coarse_own, taken)
+    outgoing = call(pack_body, shape(N_ROWS, 112, 256), n_in=3, nbytes=10**6)(coarse_own, taken, coarse_weight)
     bands = lax.all_to_all(outgoing, ROWS, 0, 0, tiled=True)
     fine_first, middle, up_out, down_out, fine_partial = call(
         fine_body,
@@ -308,8 +308,8 @@
             pltpu.VMEM((384, 256), F32),
             pltpu.VMEM((N_PLANE, 24, 128), F32),
         ],
-        n_in=4, flops=3 * 10**9, nbytes=2 * 10**6,
-    )(bands, coarse_weight, fine_partial, fine_first)
+        n_in=5, flops=3 * 10**9, nbytes=2 * 10**6,
+    )(bands, coarse_own, taken, fine_partial, fine_first)
     returned = shifted(joined, -1, 0)
     parts = lax.all_to_all(send, PLANE, 0, 0, tiled=True)
     copies = call(sum_body, shape(N_Z, 20, 128), n_in=1, nbytes=10**6)(parts)

time: 84.5 us -> 84.5 us (level)
  no operation moved by 1% of the time
where the time goes in v7:
time: 84.5 us; the launch traced here: 83.9 us
  starting transfers between devices  53.3 us (63%)
  waiting for transfers between devices  18.4 us (22%)
  Pallas kernels  11.4 us (13%)
    ppermute x6, starting transfers between devices, shifted(): return lax.ppermute(value, ALL, pairs)  17.5 us
    all_to_all x1, starting transfers between devices, local(): parts = lax.all_to_all(send, PLANE, 0, 0, tiled=True)  12.5 us
    all_to_all x1, starting transfers between devices, local(): lax.all_to_all(copies, 'z', 0, 0, axis_index_groups=[[(9 + i) % N_Z for i...  12.5 us
    all_to_all x1, waiting for transfers between devices, local(): parts = lax.all_to_all(copies, PLANE, 0, 0, tiled=True)  7.08 us
    all_to_all x1, waiting for transfers between devices, local(): parts = lax.all_to_all(send, PLANE, 0, 0, tiled=True)  5.88 us
    all_to_all x1, starting transfers between devices, local(): parts = lax.all_to_all(copies, PLANE, 0, 0, tiled=True)  5.78 us
    all_to_all x1, starting transfers between devices, local(): bands = lax.all_to_all(outgoing, ROWS, 0, 0, tiled=True)  5.03 us
    pallas_call x1, Pallas kernels, local(): call(fine_body, (shape(768, 128, dtype=F32), shape(768, 128), shape(384,...  3.49 us
  transfers between devices with their start and end apart: 10, of which 5 were waited for; matrix products, arithmetic and copies ran while one was open for 0% of the time, Pallas kernels for 8%

profile of v7, /device:TPU:1, one launch (start us, length us, event | category | flops | bytes accessed | tf_op | source)
XLA Modules:
  0.0 83.9 jit_solution(5650191206149312728)
XLA Ops:
  0.6 1.7 %shard_map.93 = bf16[928,128]{1,0:T(8,128)(2,1)} custom-call(bf16[48,256]{1,0:T(8,128)(2,1)} %bitcast.9, bf16[768,128]{1,0:T(8,128)(2,1)} %bitcast.6, f32[2,768]{1,0:T(2,128)} %bitcast.12, f32[2,48]{1,0:T(2,128)} %bitcast.13), custom_call_target="tpu_custom_call" | custom-call | flops 1000000000 | bytes 1000000 | tf_op jit(solution)/shard_map/pallas_call | solution.py:270
  2.4 0.0 copy-start.1
  2.4 6.3 %collective-permute-start = (bf16[928,128]{1,0:T(8,128)(2,1)}, bf16[928,128]{1,0:T(8,128)(2,1)S(1)}, u32[]{:S(2)}, u32[]{:S(2)}) collective-permute-start(bf16[928,128]{1,0:T(8,128)(2,1)} %shard_map.93), channel_id=1, source_target_pairs={{0,8},{1,9},{2,10},{3,11},{4,12},{5,13},{6,14},{7,15},{8,16},{9,17... | collective-permute-start | bytes 712712 | tf_op jit(solution)/shard_map/ppermute | solution.py:264
  8.8 1.3 %collective-permute-start.2 = (bf16[384,128]{1,0:T(8,128)(2,1)S(1)}, bf16[384,128]{1,0:T(8,128)(2,1)S(1)}, u32[]{:S(2)}, u32[]{:S(2)}) collective-permute-start(bf16[384,128]{1,0:T(8,128)(2,1)S(1)} %get-tuple-element.32), channel_id=1, source_target_pairs={{1,0},{2,1},{3,2},{4,3},{5,4},{6,5},{7,6},{9,8},{10,9},{11,10},{12... | collective-permute-start | bytes 294920 | tf_op jit(solution)/shard_map/ppermute | solution.py:264
  10.1 4.0 %collective-permute-start.1 = (bf16[384,128]{1,0:T(8,128)(2,1)S(1)}, bf16[384,128]{1,0:T(8,128)(2,1)S(1)}, u32[]{:S(2)}, u32[]{:S(2)}) collective-permute-start(bf16[384,128]{1,0:T(8,128)(2,1)S(1)} %get-tuple-element.33), channel_id=1, source_target_pairs={{0,1},{1,2},{2,3},{3,4},{4,5},{5,6},{6,7},{8,9},{9,10},{10,11},{11... | collective-permute-start | bytes 294920 | tf_op jit(solution)/shard_map/ppermute | solution.py:264
  14.1 0.2 collective-permute-done.taken
  14.3 1.0 %shard_map.94 = bf16[8,112,256]{2,1,0:T(8,128)(2,1)} custom-call(bf16[48,256]{1,0:T(8,128)(2,1)S(1)} %bitcast.10, bf16[928,128]{1,0:T(8,128)(2,1)S(1)} %collective-permute-done.taken, bf16[256,256]{1,0:T(8,128)(2,1)S(1)} %copy-done.1), custom_call_target="tpu_custom_call" | custom-call | bytes 1000000 | tf_op jit(solution)/shard_map/pallas_call | solution.py:286
  15.2 5.0 %all-to-all-start = ((bf16[8,112,256]{2,1,0:T(8,128)(2,1)}), bf16[8,112,256]{2,1,0:T(8,128)(2,1)S(1)}, u32[]{:S(2)}, u32[]{:S(2)}) async-start(bf16[8,112,256]{2,1,0:T(8,128)(2,1)} %shard_map.94), calls=%async_computation | async-start | bytes 917504 | tf_op jit(solution)/shard_map/all_to_all | solution.py:287
  20.3 3.5 %shard_map.95 = (f32[768,128]{1,0:T(8,128)S(1)}, bf16[768,128]{1,0:T(8,128)(2,1)S(1)}, bf16[384,128]{1,0:T(8,128)(2,1)S(1)}, bf16[384,128]{1,0:T(8,128)(2,1)S(1)}, f32[128,128]{1,0:T(8,128)S(1)}) custom-call(bf16[928,128]{1,0:T(8,128)(2,1)S(1)} %collective-permute-done.taken, bf16[768,128]{1,0:T(8,128)(2,1)S(1)} %bitcast.8, ...), custom_call_target="tpu_custom_call" | custom-call | flops 20000000000 | bytes 4000000 | tf_op jit(solution)/shard_map/pallas_call | solution.py:288
  23.8 3.1 %all-to-all-done.bands = bf16[8,112,256]{2,1,0:T(8,128)(2,1)S(1)} async-done(((bf16[8,112,256]{2,1,0:T(8,128)(2,1)}), bf16[8,112,256]{2,1,0:T(8,128)(2,1)S(1)}, u32[]{:S(2)}, u32[]{:S(2)}) %all-to-all-start) | async-done | bytes 458784 | tf_op jit(solution)/shard_map/all_to_all | solution.py:287
  26.8 2.2 %shard_map.96 = (bf16[48,256]{1,0:T(8,128)(2,1)S(1)}, f32[864,128]{1,0:T(8,128)S(1)}, bf16[32,20,128]{2,1,0:T(8,128)(2,1)}) custom-call(bf16[8,112,256]{2,1,0:T(8,128)(2,1)S(1)} %all-to-all-done.bands, bf16[48,256]{1,0:T(8,128)(2,1)S(1)} %bitcast.11, bf16[928,128]{1,0:T(8,128)(2,1)S(1)} %collective-permute-done.taken, ...), custom_call_target="tpu_custom_call" | custom-call | flops 3000000000 | bytes 2000000 | tf_op jit(solution)/shard_map/pallas_call | solution.py:303
  29.0 12.5 %all-to-all-start.1 = ((bf16[32,20,128]{2,1,0:T(8,128)(2,1)}), bf16[32,20,128]{2,1,0:T(8,128)(2,1)S(1)}, u32[]{:S(2)}, u32[]{:S(2)}) async-start(bf16[32,20,128]{2,1,0:T(8,128)(2,1)} %get-tuple-element.29), calls=%async_computation.1 | async-start | bytes 393216 | tf_op jit(solution)/shard_map/all_to_all | solution.py:314
  41.5 2.2 %collective-permute-start.3 = (f32[864,128]{1,0:T(8,128)S(1)}, f32[864,128]{1,0:T(8,128)S(1)}, u32[]{:S(2)}, u32[]{:S(2)}) collective-permute-start(f32[864,128]{1,0:T(8,128)S(1)} %get-tuple-element.22), channel_id=1, source_target_pairs={{0,504},{1,505},{2,506},{3,507},{4,508},{5,509},{6,510},{7,511},{8... | collective-permute-start | bytes 1327112 | tf_op jit(solution)/shard_map/ppermute | solution.py:264
  43.7 5.9 %all-to-all-done.1.parts = bf16[32,20,128]{2,1,0:T(8,128)(2,1)S(1)} async-done(((bf16[32,20,128]{2,1,0:T(8,128)(2,1)}), bf16[32,20,128]{2,1,0:T(8,128)(2,1)S(1)}, u32[]{:S(2)}, u32[]{:S(2)}) %all-to-all-start.1) | async-done | bytes 163872 | tf_op jit(solution)/shard_map/all_to_all | solution.py:314
  49.6 0.7 shard_map.98
  50.3 12.5 %all-to-all-start.2 = ((bf16[16,20,128]{2,1,0:T(8,128)(2,1)}), bf16[16,20,128]{2,1,0:T(8,128)(2,1)S(1)}, u32[]{:S(2)}, u32[]{:S(2)}) async-start(bf16[16,20,128]{2,1,0:T(8,128)(2,1)} %shard_map.98), calls=%async_computation.2 | async-start | bytes 196608 | tf_op jit(solution)/shard_map/all_to_all | solution.py:316
  62.7 2.4 %collective-permute-start.4 = (bf16[384,128]{1,0:T(8,128)(2,1)S(1)}, bf16[384,128]{1,0:T(8,128)(2,1)S(1)}, u32[]{:S(2)}, u32[]{:S(2)}) collective-permute-start(bf16[384,128]{1,0:T(8,128)(2,1)S(1)} %get-tuple-element.24), channel_id=1, source_target_pairs={{0,1},{1,2},{2,3},{3,4},{4,5},{5,6},{6,7},{8,9},{9,10},{10,11},{11... | collective-permute-start | bytes 294920 | tf_op jit(solution)/shard_map/ppermute | solution.py:264
  65.1 1.3 %collective-permute-start.5 = (bf16[384,128]{1,0:T(8,128)(2,1)S(1)}, bf16[384,128]{1,0:T(8,128)(2,1)S(1)}, u32[]{:S(2)}, u32[]{:S(2)}) collective-permute-start(bf16[384,128]{1,0:T(8,128)(2,1)S(1)} %get-tuple-element.25), channel_id=1, source_target_pairs={{1,0},{2,1},{3,2},{4,3},{5,4},{6,5},{7,6},{9,8},{10,9},{11,10},{12... | collective-permute-start | bytes 294920 | tf_op jit(solution)/shard_map/ppermute | solution.py:264
  66.4 2.2 %all-to-all-done.2.parts = bf16[16,20,128]{2,1,0:T(8,128)(2,1)S(1)} async-done(((bf16[16,20,128]{2,1,0:T(8,128)(2,1)}), bf16[16,20,128]{2,1,0:T(8,128)(2,1)S(1)}, u32[]{:S(2)}, u32[]{:S(2)}) %all-to-all-start.2) | async-done | bytes 81952 | tf_op jit(solution)/shard_map/all_to_all | solution.py:316
  68.6 0.7 shard_map.99
  69.3 5.8 %all-to-all-start.3 = ((bf16[32,20,128]{2,1,0:T(8,128)(2,1)}), bf16[32,20,128]{2,1,0:T(8,128)(2,1)S(1)}, u32[]{:S(2)}, u32[]{:S(2)}) async-start(bf16[32,20,128]{2,1,0:T(8,128)(2,1)} %shard_map.99), calls=%async_computation.3 | async-start | bytes 393216 | tf_op jit(solution)/shard_map/all_to_all | solution.py:318
  75.2 0.9 %shard_map.97 = (bf16[768,128]{1,0:T(8,128)(2,1)}, bf16[48,256]{1,0:T(8,128)(2,1)}) custom-call(f32[864,128]{1,0:T(8,128)S(1)} %collective-permute-done.3.returned, bf16[768,128]{1,0:T(8,128)(2,1)S(1)} %get-tuple-element.23.middle, bf16[384,128]{1,0:T(8,128)(2,1)S(1)} %collective-permute-done.4.from_above, ...), custom_call_target="tpu_custom_call" | custom-call | flops 20000000000 | bytes 1000000 | tf_op jit(solution)/shard_map/pallas_call | solution.py:322
  76.1 7.1 %all-to-all-done.3.parts = bf16[32,20,128]{2,1,0:T(8,128)(2,1)S(1)} async-done(((bf16[32,20,128]{2,1,0:T(8,128)(2,1)}), bf16[32,20,128]{2,1,0:T(8,128)(2,1)S(1)}, u32[]{:S(2)}, u32[]{:S(2)}) %all-to-all-start.3) | async-done | bytes 163872 | tf_op jit(solution)/shard_map/all_to_all | solution.py:318
  83.1 0.7 shard_map.100
  (13 shorter events, 0.0 us)
Async XLA Ops:
  0.6 8.1 %copy-start = (bf16[1,8,96,128]{3,2,1,0:T(8,128)(2,1)S(1)}, bf16[1,8,96,128]{3,2,1,0:T(8,128)(2,1)}, u32[]{:S(2)}) copy-start(bf16[1,8,96,128]{3,2,1,0:T(8,128)(2,1)} %param.7) | copy-start | bytes 589828
  2.4 11.9 %copy-start.1 = (bf16[256,256]{1,0:T(8,128)(2,1)S(1)}, bf16[256,256]{1,0:T(8,128)(2,1)}, u32[]{:S(2)}) copy-start(bf16[256,256]{1,0:T(8,128)(2,1)} %coarse_weight.1) | copy-start | bytes 393220
  2.4 11.9 %copy-start.2 = (bf16[1,2,24,256]{3,2,1,0:T(8,128)(2,1)S(1)}, bf16[1,2,24,256]{3,2,1,0:T(8,128)(2,1)}, u32[]{:S(2)}) copy-start(bf16[1,2,24,256]{3,2,1,0:T(8,128)(2,1)} %param.6) | copy-start | bytes 73732
  2.4 11.8 %collective-permute-start = (bf16[928,128]{1,0:T(8,128)(2,1)}, bf16[928,128]{1,0:T(8,128)(2,1)S(1)}, u32[]{:S(2)}, u32[]{:S(2)}) collective-permute-start(bf16[928,128]{1,0:T(8,128)(2,1)} %shard_map.93), channel_id=1, source_target_pairs={{0,8},{1,9},{2,10},{3,11},{4,12},{5,13},{6,14},{7,15},{8,16},{9,17... | collective-permute-start | bytes 712712 | tf_op jit(solution)/shard_map/ppermute | solution.py:264
  8.8 11.5 %collective-permute-start.2 = (bf16[384,128]{1,0:T(8,128)(2,1)S(1)}, bf16[384,128]{1,0:T(8,128)(2,1)S(1)}, u32[]{:S(2)}, u32[]{:S(2)}) collective-permute-start(bf16[384,128]{1,0:T(8,128)(2,1)S(1)} %get-tuple-element.32), channel_id=1, source_target_pairs={{1,0},{2,1},{3,2},{4,3},{5,4},{6,5},{7,6},{9,8},{10,9},{11,10},{12... | collective-permute-start | bytes 294920 | tf_op jit(solution)/shard_map/ppermute | solution.py:264
  10.1 10.2 %collective-permute-start.1 = (bf16[384,128]{1,0:T(8,128)(2,1)S(1)}, bf16[384,128]{1,0:T(8,128)(2,1)S(1)}, u32[]{:S(2)}, u32[]{:S(2)}) collective-permute-start(bf16[384,128]{1,0:T(8,128)(2,1)S(1)} %get-tuple-element.33), channel_id=1, source_target_pairs={{0,1},{1,2},{2,3},{3,4},{4,5},{5,6},{6,7},{8,9},{9,10},{10,11},{11... | collective-permute-start | bytes 294920 | tf_op jit(solution)/shard_map/ppermute | solution.py:264
  15.2 5.1 %copy-start.3 = (bf16[128,128]{1,0:T(8,128)(2,1)S(1)}, bf16[128,128]{1,0:T(8,128)(2,1)}, u32[]{:S(2)}) copy-start(bf16[128,128]{1,0:T(8,128)(2,1)} %weight.5) | copy-start | bytes 98308
  15.2 11.6 %all-to-all-start = ((bf16[8,112,256]{2,1,0:T(8,128)(2,1)}), bf16[8,112,256]{2,1,0:T(8,128)(2,1)S(1)}, u32[]{:S(2)}, u32[]{:S(2)}) async-start(bf16[8,112,256]{2,1,0:T(8,128)(2,1)} %shard_map.94), calls=%async_computation | async-start | bytes 917504 | tf_op jit(solution)/shard_map/all_to_all | solution.py:287
  29.0 20.6 %all-to-all-start.1 = ((bf16[32,20,128]{2,1,0:T(8,128)(2,1)}), bf16[32,20,128]{2,1,0:T(8,128)(2,1)S(1)}, u32[]{:S(2)}, u32[]{:S(2)}) async-start(bf16[32,20,128]{2,1,0:T(8,128)(2,1)} %get-tuple-element.29), calls=%async_computation.1 | async-start | bytes 393216 | tf_op jit(solution)/shard_map/all_to_all | solution.py:314
  41.5 33.7 %collective-permute-start.3 = (f32[864,128]{1,0:T(8,128)S(1)}, f32[864,128]{1,0:T(8,128)S(1)}, u32[]{:S(2)}, u32[]{:S(2)}) collective-permute-start(f32[864,128]{1,0:T(8,128)S(1)} %get-tuple-element.22), channel_id=1, source_target_pairs={{0,504},{1,505},{2,506},{3,507},{4,508},{5,509},{6,510},{7,511},{8... | collective-permute-start | bytes 1327112 | tf_op jit(solution)/shard_map/ppermute | solution.py:264
  50.3 18.3 %all-to-all-start.2 = ((bf16[16,20,128]{2,1,0:T(8,128)(2,1)}), bf16[16,20,128]{2,1,0:T(8,128)(2,1)S(1)}, u32[]{:S(2)}, u32[]{:S(2)}) async-start(bf16[16,20,128]{2,1,0:T(8,128)(2,1)} %shard_map.98), calls=%async_computation.2 | async-start | bytes 196608 | tf_op jit(solution)/shard_map/all_to_all | solution.py:316
  62.7 12.4 %collective-permute-start.4 = (bf16[384,128]{1,0:T(8,128)(2,1)S(1)}, bf16[384,128]{1,0:T(8,128)(2,1)S(1)}, u32[]{:S(2)}, u32[]{:S(2)}) collective-permute-start(bf16[384,128]{1,0:T(8,128)(2,1)S(1)} %get-tuple-element.24), channel_id=1, source_target_pairs={{0,1},{1,2},{2,3},{3,4},{4,5},{5,6},{6,7},{8,9},{9,10},{10,11},{11... | collective-permute-start | bytes 294920 | tf_op jit(solution)/shard_map/ppermute | solution.py:264
  65.1 10.0 %collective-permute-start.5 = (bf16[384,128]{1,0:T(8,128)(2,1)S(1)}, bf16[384,128]{1,0:T(8,128)(2,1)S(1)}, u32[]{:S(2)}, u32[]{:S(2)}) collective-permute-start(bf16[384,128]{1,0:T(8,128)(2,1)S(1)} %get-tuple-element.25), channel_id=1, source_target_pairs={{1,0},{2,1},{3,2},{4,3},{5,4},{6,5},{7,6},{9,8},{10,9},{11,10},{12... | collective-permute-start | bytes 294920 | tf_op jit(solution)/shard_map/ppermute | solution.py:264
  69.3 13.8 %all-to-all-start.3 = ((bf16[32,20,128]{2,1,0:T(8,128)(2,1)}), bf16[32,20,128]{2,1,0:T(8,128)(2,1)S(1)}, u32[]{:S(2)}, u32[]{:S(2)}) async-start(bf16[32,20,128]{2,1,0:T(8,128)(2,1)} %shard_map.99), calls=%async_computation.3 | async-start | bytes 393216 | tf_op jit(solution)/shard_map/all_to_all | solution.py:318

commit v8 on v7

--- a/solution.py
+++ b/solution.py
@@ -279,7 +279,7 @@
         ],
         n_in=4, flops=10**9, nbytes=10**6, kind=HBM, room=60,
     )(coarse_own, fine_own, grad_refined.reshape(2, 768), grad_back.reshape(2, 48))
-    taken, rims = lax.optimization_barrier((taken, fine_own))
+    rims = fine_own
     taken = shifted(taken, 1, 0)
     above = shifted(rims[384:768], 0, 1)
     below = shifted(rims[0:384], 0, -1)
@@ -311,11 +311,11 @@
         n_in=5, flops=3 * 10**9, nbytes=2 * 10**6,
     )(bands, coarse_own, taken, fine_partial, fine_first)
     returned = shifted(joined, -1, 0)
-    parts = lax.all_to_all(send, PLANE, 0, 0, tiled=True)
+    parts = lax.all_to_all(send, PLANE, 0, 0, axis_index_groups=[[(20 + i) % N_PLANE for i in range(N_PLANE)]], tiled=True)
     copies = call(sum_body, shape(N_Z, 20, 128), n_in=1, nbytes=10**6)(parts)
     parts = lax.all_to_all(copies, "z", 0, 0, axis_index_groups=[[(9 + i) % N_Z for i in range(N_Z)]], tiled=True)
     copies = call(sum_body, shape(N_PLANE, 20, 128), n_in=1, nbytes=10**6)(parts)
-    parts = lax.all_to_all(copies, PLANE, 0, 0, tiled=True)
+    parts = lax.all_to_all(copies, PLANE, 0, 0, axis_index_groups=[[(20 + i) % N_PLANE for i in range(N_PLANE)]], tiled=True)
     coarse_total, fine_total = call(
         unpack_body, (shape(256, 256, dtype=F32), shape(128, 128, dtype=F32)), n_in=1, nbytes=10**6
     )(parts)

time: 84.5 us -> 82.3 us (0.974)
  waiting for transfers between devices: 18.4 us -> 8.01 us
  starting transfers between devices: 53.3 us -> 61.4 us
    all_to_all x2, waiting for transfers between devices: 13 us -> 3.73 us  [the longest x1 2.44 us: local(): lax.all_to_all(copies, PLANE, 0, 0, axis_index_groups=[[(20 + i) % N_PLAN...]
    all_to_all x2, starting transfers between devices: 18.2 us -> 26.6 us  [the longest x1 16.2 us: local(): lax.all_to_all(send, PLANE, 0, 0, axis_index_groups=[[(20 + i) % N_PLANE...]
    all_to_all x1, starting transfers between devices: 5.03 us -> 6.65 us  [local(): bands = lax.all_to_all(outgoing, ROWS, 0, 0, tiled=True)]
    all_to_all x1, waiting for transfers between devices: 2.19 us -> 1.1 us  [local(): lax.all_to_all(copies, 'z', 0, 0, axis_index_groups=[[(9 + i) % N_Z for i...]
    ppermute x6, starting transfers between devices: 17.5 us -> 16.5 us  [shifted(): return lax.ppermute(value, ALL, pairs)]
where the time goes in v8:
time: 82.3 us; the launch traced here: 81.6 us
  starting transfers between devices  61.4 us (75%)
  Pallas kernels  11.4 us (14%)
  waiting for transfers between devices  8.01 us (10%)
    ppermute x6, starting transfers between devices, shifted(): return lax.ppermute(value, ALL, pairs)  16.5 us
    all_to_all x1, starting transfers between devices, local(): lax.all_to_all(send, PLANE, 0, 0, axis_index_groups=[[(20 + i) % N_PLANE...  16.2 us
    all_to_all x1, starting transfers between devices, local(): lax.all_to_all(copies, 'z', 0, 0, axis_index_groups=[[(9 + i) % N_Z for i...  11.7 us
    all_to_all x1, starting transfers between devices, local(): lax.all_to_all(copies, PLANE, 0, 0, axis_index_groups=[[(20 + i) % N_PLAN...  10.4 us
    all_to_all x1, starting transfers between devices, local(): bands = lax.all_to_all(outgoing, ROWS, 0, 0, tiled=True)  6.65 us
    pallas_call x1, Pallas kernels, local(): call(fine_body, (shape(768, 128, dtype=F32), shape(768, 128), shape(384,...  3.49 us
    all_to_all x1, waiting for transfers between devices, local(): bands = lax.all_to_all(outgoing, ROWS, 0, 0, tiled=True)  3.07 us
    all_to_all x1, waiting for transfers between devices, local(): lax.all_to_all(copies, PLANE, 0, 0, axis_index_groups=[[(20 + i) % N_PLAN...  2.44 us
  transfers between devices with their start and end apart: 10, of which 5 were waited for; matrix products, arithmetic and copies ran while one was open for 0% of the time, Pallas kernels for 8%

profile of v8, /device:TPU:1, one launch (start us, length us, event | category | flops | bytes accessed | tf_op | source)
XLA Modules:
  0.0 81.6 jit_solution(1354635101800578475)
XLA Ops:
  0.6 1.7 %shard_map.93 = bf16[928,128]{1,0:T(8,128)(2,1)} custom-call(bf16[48,256]{1,0:T(8,128)(2,1)} %bitcast.10, bf16[768,128]{1,0:T(8,128)(2,1)} %bitcast.8, f32[2,768]{1,0:T(2,128)} %bitcast.15, f32[2,48]{1,0:T(2,128)} %bitcast.16), custom_call_target="tpu_custom_call" | custom-call | flops 1000000000 | bytes 1000000 | tf_op jit(solution)/shard_map/pallas_call | solution.py:270
  2.4 0.0 copy-start.1
  2.4 6.3 %collective-permute-start = (bf16[928,128]{1,0:T(8,128)(2,1)}, bf16[928,128]{1,0:T(8,128)(2,1)S(1)}, u32[]{:S(2)}, u32[]{:S(2)}) collective-permute-start(bf16[928,128]{1,0:T(8,128)(2,1)} %shard_map.93), channel_id=1, source_target_pairs={{0,8},{1,9},{2,10},{3,11},{4,12},{5,13},{6,14},{7,15},{8,16},{9,17... | collective-permute-start | bytes 712712 | tf_op jit(solution)/shard_map/ppermute | solution.py:264
  8.8 2.3 %collective-permute-start.1 = (bf16[384,128]{1,0:T(8,128)(2,1)S(1)}, bf16[384,128]{1,0:T(8,128)(2,1)S(1)}, u32[]{:S(2)}, u32[]{:S(2)}) collective-permute-start(bf16[384,128]{1,0:T(8,128)(2,1)S(1)} %bitcast.14), channel_id=1, source_target_pairs={{0,1},{1,2},{2,3},{3,4},{4,5},{5,6},{6,7},{8,9},{9,10},{10,11},{11... | collective-permute-start | bytes 294920 | tf_op jit(solution)/shard_map/ppermute | solution.py:264
  11.1 1.3 %collective-permute-start.2 = (bf16[384,128]{1,0:T(8,128)(2,1)S(1)}, bf16[384,128]{1,0:T(8,128)(2,1)S(1)}, u32[]{:S(2)}, u32[]{:S(2)}) collective-permute-start(bf16[384,128]{1,0:T(8,128)(2,1)S(1)} %bitcast.13), channel_id=1, source_target_pairs={{1,0},{2,1},{3,2},{4,3},{5,4},{6,5},{7,6},{9,8},{10,9},{11,10},{12... | collective-permute-start | bytes 294920 | tf_op jit(solution)/shard_map/ppermute | solution.py:264
  12.4 0.1 collective-permute-done.taken
  12.5 1.0 %shard_map.94 = bf16[8,112,256]{2,1,0:T(8,128)(2,1)} custom-call(bf16[48,256]{1,0:T(8,128)(2,1)S(1)} %bitcast.11, bf16[928,128]{1,0:T(8,128)(2,1)S(1)} %collective-permute-done.taken, bf16[256,256]{1,0:T(8,128)(2,1)S(1)} %copy-done.1), custom_call_target="tpu_custom_call" | custom-call | bytes 1000000 | tf_op jit(solution)/shard_map/pallas_call | solution.py:286
  13.5 6.7 %all-to-all-start = ((bf16[8,112,256]{2,1,0:T(8,128)(2,1)}), bf16[8,112,256]{2,1,0:T(8,128)(2,1)S(1)}, u32[]{:S(2)}, u32[]{:S(2)}) async-start(bf16[8,112,256]{2,1,0:T(8,128)(2,1)} %shard_map.94), calls=%async_computation | async-start | bytes 917504 | tf_op jit(solution)/shard_map/all_to_all | solution.py:287
  20.2 3.5 %shard_map.95 = (f32[768,128]{1,0:T(8,128)S(1)}, bf16[768,128]{1,0:T(8,128)(2,1)S(1)}, bf16[384,128]{1,0:T(8,128)(2,1)S(1)}, bf16[384,128]{1,0:T(8,128)(2,1)S(1)}, f32[128,128]{1,0:T(8,128)S(1)}) custom-call(bf16[928,128]{1,0:T(8,128)(2,1)S(1)} %collective-permute-done.taken, bf16[768,128]{1,0:T(8,128)(2,1)S(1)} %bitcast.9, ...), custom_call_target="tpu_custom_call" | custom-call | flops 20000000000 | bytes 4000000 | tf_op jit(solution)/shard_map/pallas_call | solution.py:288
  23.7 3.1 %all-to-all-done.bands = bf16[8,112,256]{2,1,0:T(8,128)(2,1)S(1)} async-done(((bf16[8,112,256]{2,1,0:T(8,128)(2,1)}), bf16[8,112,256]{2,1,0:T(8,128)(2,1)S(1)}, u32[]{:S(2)}, u32[]{:S(2)}) %all-to-all-start) | async-done | bytes 458784 | tf_op jit(solution)/shard_map/all_to_all | solution.py:287
  26.7 2.2 %shard_map.96 = (bf16[48,256]{1,0:T(8,128)(2,1)S(1)}, f32[864,128]{1,0:T(8,128)S(1)}, bf16[32,20,128]{2,1,0:T(8,128)(2,1)}) custom-call(bf16[8,112,256]{2,1,0:T(8,128)(2,1)S(1)} %all-to-all-done.bands, bf16[48,256]{1,0:T(8,128)(2,1)S(1)} %bitcast.12, bf16[928,128]{1,0:T(8,128)(2,1)S(1)} %collective-permute-done.taken, ...), custom_call_target="tpu_custom_call" | custom-call | flops 3000000000 | bytes 2000000 | tf_op jit(solution)/shard_map/pallas_call | solution.py:303
  28.9 16.2 %all-to-all-start.1 = ((bf16[32,20,128]{2,1,0:T(8,128)(2,1)}), bf16[32,20,128]{2,1,0:T(8,128)(2,1)S(1)}, u32[]{:S(2)}, u32[]{:S(2)}) async-start(bf16[32,20,128]{2,1,0:T(8,128)(2,1)} %get-tuple-element.25), calls=%async_computation.1 | async-start | bytes 393216 | tf_op jit(solution)/shard_map/all_to_all | solution.py:314
  45.1 2.3 %collective-permute-start.3 = (f32[864,128]{1,0:T(8,128)S(1)}, f32[864,128]{1,0:T(8,128)S(1)}, u32[]{:S(2)}, u32[]{:S(2)}) collective-permute-start(f32[864,128]{1,0:T(8,128)S(1)} %get-tuple-element.18), channel_id=1, source_target_pairs={{0,504},{1,505},{2,506},{3,507},{4,508},{5,509},{6,510},{7,511},{8... | collective-permute-start | bytes 1327112 | tf_op jit(solution)/shard_map/ppermute | solution.py:264
  47.4 1.3 %all-to-all-done.1.parts = bf16[32,20,128]{2,1,0:T(8,128)(2,1)S(1)} async-done(((bf16[32,20,128]{2,1,0:T(8,128)(2,1)}), bf16[32,20,128]{2,1,0:T(8,128)(2,1)S(1)}, u32[]{:S(2)}, u32[]{:S(2)}) %all-to-all-start.1) | async-done | bytes 163872 | tf_op jit(solution)/shard_map/all_to_all | solution.py:314
  48.7 0.7 shard_map.98
  49.3 11.7 %all-to-all-start.2 = ((bf16[16,20,128]{2,1,0:T(8,128)(2,1)}), bf16[16,20,128]{2,1,0:T(8,128)(2,1)S(1)}, u32[]{:S(2)}, u32[]{:S(2)}) async-start(bf16[16,20,128]{2,1,0:T(8,128)(2,1)} %shard_map.98), calls=%async_computation.2 | async-start | bytes 196608 | tf_op jit(solution)/shard_map/all_to_all | solution.py:316
  61.0 3.0 %collective-permute-start.4 = (bf16[384,128]{1,0:T(8,128)(2,1)S(1)}, bf16[384,128]{1,0:T(8,128)(2,1)S(1)}, u32[]{:S(2)}, u32[]{:S(2)}) collective-permute-start(bf16[384,128]{1,0:T(8,128)(2,1)S(1)} %get-tuple-element.20), channel_id=1, source_target_pairs={{0,1},{1,2},{2,3},{3,4},{4,5},{5,6},{6,7},{8,9},{9,10},{10,11},{11... | collective-permute-start | bytes 294920 | tf_op jit(solution)/shard_map/ppermute | solution.py:264
  64.0 1.3 %collective-permute-start.5 = (bf16[384,128]{1,0:T(8,128)(2,1)S(1)}, bf16[384,128]{1,0:T(8,128)(2,1)S(1)}, u32[]{:S(2)}, u32[]{:S(2)}) collective-permute-start(bf16[384,128]{1,0:T(8,128)(2,1)S(1)} %get-tuple-element.21), channel_id=1, source_target_pairs={{1,0},{2,1},{3,2},{4,3},{5,4},{6,5},{7,6},{9,8},{10,9},{11,10},{12... | collective-permute-start | bytes 294920 | tf_op jit(solution)/shard_map/ppermute | solution.py:264
  65.3 1.1 %all-to-all-done.2.parts = bf16[16,20,128]{2,1,0:T(8,128)(2,1)S(1)} async-done(((bf16[16,20,128]{2,1,0:T(8,128)(2,1)}), bf16[16,20,128]{2,1,0:T(8,128)(2,1)S(1)}, u32[]{:S(2)}, u32[]{:S(2)}) %all-to-all-start.2) | async-done | bytes 81952 | tf_op jit(solution)/shard_map/all_to_all | solution.py:316
  66.4 0.7 shard_map.99
  67.1 10.4 %all-to-all-start.3 = ((bf16[32,20,128]{2,1,0:T(8,128)(2,1)}), bf16[32,20,128]{2,1,0:T(8,128)(2,1)S(1)}, u32[]{:S(2)}, u32[]{:S(2)}) async-start(bf16[32,20,128]{2,1,0:T(8,128)(2,1)} %shard_map.99), calls=%async_computation.3 | async-start | bytes 393216 | tf_op jit(solution)/shard_map/all_to_all | solution.py:318
  77.5 0.9 %shard_map.97 = (bf16[768,128]{1,0:T(8,128)(2,1)}, bf16[48,256]{1,0:T(8,128)(2,1)}) custom-call(f32[864,128]{1,0:T(8,128)S(1)} %collective-permute-done.3.returned, bf16[768,128]{1,0:T(8,128)(2,1)S(1)} %get-tuple-element.19.middle, bf16[384,128]{1,0:T(8,128)(2,1)S(1)} %collective-permute-done.4.from_above, ...), custom_call_target="tpu_custom_call" | custom-call | flops 20000000000 | bytes 1000000 | tf_op jit(solution)/shard_map/pallas_call | solution.py:322
  78.5 2.4 %all-to-all-done.3.parts = bf16[32,20,128]{2,1,0:T(8,128)(2,1)S(1)} async-done(((bf16[32,20,128]{2,1,0:T(8,128)(2,1)}), bf16[32,20,128]{2,1,0:T(8,128)(2,1)S(1)}, u32[]{:S(2)}, u32[]{:S(2)}) %all-to-all-start.3) | async-done | bytes 163872 | tf_op jit(solution)/shard_map/all_to_all | solution.py:318
  80.9 0.7 shard_map.100
  (13 shorter events, 0.0 us)
Async XLA Ops:
  0.6 8.1 %copy-start = (bf16[1,8,96,128]{3,2,1,0:T(8,128)(2,1)S(1)}, bf16[1,8,96,128]{3,2,1,0:T(8,128)(2,1)}, u32[]{:S(2)}) copy-start(bf16[1,8,96,128]{3,2,1,0:T(8,128)(2,1)} %param.7) | copy-start | bytes 589828
  2.4 10.1 %copy-start.1 = (bf16[256,256]{1,0:T(8,128)(2,1)S(1)}, bf16[256,256]{1,0:T(8,128)(2,1)}, u32[]{:S(2)}) copy-start(bf16[256,256]{1,0:T(8,128)(2,1)} %coarse_weight.1) | copy-start | bytes 393220
  2.4 10.1 %collective-permute-start = (bf16[928,128]{1,0:T(8,128)(2,1)}, bf16[928,128]{1,0:T(8,128)(2,1)S(1)}, u32[]{:S(2)}, u32[]{:S(2)}) collective-permute-start(bf16[928,128]{1,0:T(8,128)(2,1)} %shard_map.93), channel_id=1, source_target_pairs={{0,8},{1,9},{2,10},{3,11},{4,12},{5,13},{6,14},{7,15},{8,16},{9,17... | collective-permute-start | bytes 712712 | tf_op jit(solution)/shard_map/ppermute | solution.py:264
  8.8 3.8 %copy-start.2 = (bf16[1,2,24,256]{3,2,1,0:T(8,128)(2,1)S(1)}, bf16[1,2,24,256]{3,2,1,0:T(8,128)(2,1)}, u32[]{:S(2)}) copy-start(bf16[1,2,24,256]{3,2,1,0:T(8,128)(2,1)} %param.6) | copy-start | bytes 73732
  8.8 11.3 %collective-permute-start.1 = (bf16[384,128]{1,0:T(8,128)(2,1)S(1)}, bf16[384,128]{1,0:T(8,128)(2,1)S(1)}, u32[]{:S(2)}, u32[]{:S(2)}) collective-permute-start(bf16[384,128]{1,0:T(8,128)(2,1)S(1)} %bitcast.14), channel_id=1, source_target_pairs={{0,1},{1,2},{2,3},{3,4},{4,5},{5,6},{6,7},{8,9},{9,10},{10,11},{11... | collective-permute-start | bytes 294920 | tf_op jit(solution)/shard_map/ppermute | solution.py:264
  11.1 9.0 %collective-permute-start.2 = (bf16[384,128]{1,0:T(8,128)(2,1)S(1)}, bf16[384,128]{1,0:T(8,128)(2,1)S(1)}, u32[]{:S(2)}, u32[]{:S(2)}) collective-permute-start(bf16[384,128]{1,0:T(8,128)(2,1)S(1)} %bitcast.13), channel_id=1, source_target_pairs={{1,0},{2,1},{3,2},{4,3},{5,4},{6,5},{7,6},{9,8},{10,9},{11,10},{12... | collective-permute-start | bytes 294920 | tf_op jit(solution)/shard_map/ppermute | solution.py:264
  13.5 6.7 %copy-start.3 = (bf16[128,128]{1,0:T(8,128)(2,1)S(1)}, bf16[128,128]{1,0:T(8,128)(2,1)}, u32[]{:S(2)}) copy-start(bf16[128,128]{1,0:T(8,128)(2,1)} %weight.5) | copy-start | bytes 98308
  13.5 13.2 %all-to-all-start = ((bf16[8,112,256]{2,1,0:T(8,128)(2,1)}), bf16[8,112,256]{2,1,0:T(8,128)(2,1)S(1)}, u32[]{:S(2)}, u32[]{:S(2)}) async-start(bf16[8,112,256]{2,1,0:T(8,128)(2,1)} %shard_map.94), calls=%async_computation | async-start | bytes 917504 | tf_op jit(solution)/shard_map/all_to_all | solution.py:287
  28.9 19.8 %all-to-all-start.1 = ((bf16[32,20,128]{2,1,0:T(8,128)(2,1)}), bf16[32,20,128]{2,1,0:T(8,128)(2,1)S(1)}, u32[]{:S(2)}, u32[]{:S(2)}) async-start(bf16[32,20,128]{2,1,0:T(8,128)(2,1)} %get-tuple-element.25), calls=%async_computation.1 | async-start | bytes 393216 | tf_op jit(solution)/shard_map/all_to_all | solution.py:314
  45.1 32.4 %collective-permute-start.3 = (f32[864,128]{1,0:T(8,128)S(1)}, f32[864,128]{1,0:T(8,128)S(1)}, u32[]{:S(2)}, u32[]{:S(2)}) collective-permute-start(f32[864,128]{1,0:T(8,128)S(1)} %get-tuple-element.18), channel_id=1, source_target_pairs={{0,504},{1,505},{2,506},{3,507},{4,508},{5,509},{6,510},{7,511},{8... | collective-permute-start | bytes 1327112 | tf_op jit(solution)/shard_map/ppermute | solution.py:264
  49.3 17.0 %all-to-all-start.2 = ((bf16[16,20,128]{2,1,0:T(8,128)(2,1)}), bf16[16,20,128]{2,1,0:T(8,128)(2,1)S(1)}, u32[]{:S(2)}, u32[]{:S(2)}) async-start(bf16[16,20,128]{2,1,0:T(8,128)(2,1)} %shard_map.98), calls=%async_computation.2 | async-start | bytes 196608 | tf_op jit(solution)/shard_map/all_to_all | solution.py:316
  61.0 16.5 %collective-permute-start.4 = (bf16[384,128]{1,0:T(8,128)(2,1)S(1)}, bf16[384,128]{1,0:T(8,128)(2,1)S(1)}, u32[]{:S(2)}, u32[]{:S(2)}) collective-permute-start(bf16[384,128]{1,0:T(8,128)(2,1)S(1)} %get-tuple-element.20), channel_id=1, source_target_pairs={{0,1},{1,2},{2,3},{3,4},{4,5},{5,6},{6,7},{8,9},{9,10},{10,11},{11... | collective-permute-start | bytes 294920 | tf_op jit(solution)/shard_map/ppermute | solution.py:264
  64.0 13.5 %collective-permute-start.5 = (bf16[384,128]{1,0:T(8,128)(2,1)S(1)}, bf16[384,128]{1,0:T(8,128)(2,1)S(1)}, u32[]{:S(2)}, u32[]{:S(2)}) collective-permute-start(bf16[384,128]{1,0:T(8,128)(2,1)S(1)} %get-tuple-element.21), channel_id=1, source_target_pairs={{1,0},{2,1},{3,2},{4,3},{5,4},{6,5},{7,6},{9,8},{10,9},{11,10},{12... | collective-permute-start | bytes 294920 | tf_op jit(solution)/shard_map/ppermute | solution.py:264
  67.1 13.8 %all-to-all-start.3 = ((bf16[32,20,128]{2,1,0:T(8,128)(2,1)}), bf16[32,20,128]{2,1,0:T(8,128)(2,1)S(1)}, u32[]{:S(2)}, u32[]{:S(2)}) async-start(bf16[32,20,128]{2,1,0:T(8,128)(2,1)} %shard_map.99), calls=%async_computation.3 | async-start | bytes 393216 | tf_op jit(solution)/shard_map/all_to_all | solution.py:318

commit v9 on v8

--- a/solution.py
+++ b/solution.py
@@ -311,11 +311,11 @@
         n_in=5, flops=3 * 10**9, nbytes=2 * 10**6,
     )(bands, coarse_own, taken, fine_partial, fine_first)
     returned = shifted(joined, -1, 0)
-    parts = lax.all_to_all(send, PLANE, 0, 0, axis_index_groups=[[(20 + i) % N_PLANE for i in range(N_PLANE)]], tiled=True)
+    parts = lax.all_to_all(send, PLANE, 0, 0, axis_index_groups=[[(28 + i) % N_PLANE for i in range(N_PLANE)]], tiled=True)
     copies = call(sum_body, shape(N_Z, 20, 128), n_in=1, nbytes=10**6)(parts)
     parts = lax.all_to_all(copies, "z", 0, 0, axis_index_groups=[[(9 + i) % N_Z for i in range(N_Z)]], tiled=True)
     copies = call(sum_body, shape(N_PLANE, 20, 128), n_in=1, nbytes=10**6)(parts)
-    parts = lax.all_to_all(copies, PLANE, 0, 0, axis_index_groups=[[(20 + i) % N_PLANE for i in range(N_PLANE)]], tiled=True)
+    parts = lax.all_to_all(copies, PLANE, 0, 0, axis_index_groups=[[(28 + i) % N_PLANE for i in range(N_PLANE)]], tiled=True)
     coarse_total, fine_total = call(
         unpack_body, (shape(256, 256, dtype=F32), shape(128, 128, dtype=F32)), n_in=1, nbytes=10**6
     )(parts)

time: 82.3 us -> 81.4 us (0.989)
  starting transfers between devices: 61.4 us -> 60.2 us
    all_to_all x2, starting transfers between devices: 26.6 us -> 25.5 us  [the longest x1 15.9 us: local(): lax.all_to_all(send, PLANE, 0, 0, axis_index_groups=[[(28 + i) % N_PLANE...]
where the time goes in v9:
time: 81.4 us; the launch traced here: 80.7 us
  starting transfers between devices  60.2 us (74%)
  Pallas kernels  11.4 us (14%)
  waiting for transfers between devices  8.26 us (10%)
    ppermute x6, starting transfers between devices, shifted(): return lax.ppermute(value, ALL, pairs)  16.4 us
    all_to_all x1, starting transfers between devices, local(): lax.all_to_all(send, PLANE, 0, 0, axis_index_groups=[[(28 + i) % N_PLANE...  15.9 us
    all_to_all x1, starting transfers between devices, local(): lax.all_to_all(copies, 'z', 0, 0, axis_index_groups=[[(9 + i) % N_Z for i...  11.7 us
    all_to_all x1, starting transfers between devices, local(): lax.all_to_all(copies, PLANE, 0, 0, axis_index_groups=[[(28 + i) % N_PLAN...  9.59 us
    all_to_all x1, starting transfers between devices, local(): bands = lax.all_to_all(outgoing, ROWS, 0, 0, tiled=True)  6.65 us
    pallas_call x1, Pallas kernels, local(): call(fine_body, (shape(768, 128, dtype=F32), shape(768, 128), shape(384,...  3.49 us
    all_to_all x1, waiting for transfers between devices, local(): bands = lax.all_to_all(outgoing, ROWS, 0, 0, tiled=True)  3.07 us
    all_to_all x1, waiting for transfers between devices, local(): lax.all_to_all(copies, PLANE, 0, 0, axis_index_groups=[[(28 + i) % N_PLAN...  2.63 us
  transfers between devices with their start and end apart: 10, of which 5 were waited for; matrix products, arithmetic and copies ran while one was open for 0% of the time, Pallas kernels for 8%

profile of v9, /device:TPU:1, one launch (start us, length us, event | category | flops | bytes accessed | tf_op | source)
XLA Modules:
  0.0 80.7 jit_solution(5701508613120167409)
XLA Ops:
  0.6 1.7 %shard_map.93 = bf16[928,128]{1,0:T(8,128)(2,1)} custom-call(bf16[48,256]{1,0:T(8,128)(2,1)} %bitcast.10, bf16[768,128]{1,0:T(8,128)(2,1)} %bitcast.8, f32[2,768]{1,0:T(2,128)} %bitcast.15, f32[2,48]{1,0:T(2,128)} %bitcast.16), custom_call_target="tpu_custom_call" | custom-call | flops 1000000000 | bytes 1000000 | tf_op jit(solution)/shard_map/pallas_call | solution.py:270
  2.4 0.0 copy-start.1
  2.4 6.3 %collective-permute-start = (bf16[928,128]{1,0:T(8,128)(2,1)}, bf16[928,128]{1,0:T(8,128)(2,1)S(1)}, u32[]{:S(2)}, u32[]{:S(2)}) collective-permute-start(bf16[928,128]{1,0:T(8,128)(2,1)} %shard_map.93), channel_id=1, source_target_pairs={{0,8},{1,9},{2,10},{3,11},{4,12},{5,13},{6,14},{7,15},{8,16},{9,17... | collective-permute-start | bytes 712712 | tf_op jit(solution)/shard_map/ppermute | solution.py:264
  8.8 2.3 %collective-permute-start.1 = (bf16[384,128]{1,0:T(8,128)(2,1)S(1)}, bf16[384,128]{1,0:T(8,128)(2,1)S(1)}, u32[]{:S(2)}, u32[]{:S(2)}) collective-permute-start(bf16[384,128]{1,0:T(8,128)(2,1)S(1)} %bitcast.14), channel_id=1, source_target_pairs={{0,1},{1,2},{2,3},{3,4},{4,5},{5,6},{6,7},{8,9},{9,10},{10,11},{11... | collective-permute-start | bytes 294920 | tf_op jit(solution)/shard_map/ppermute | solution.py:264
  11.1 1.3 %collective-permute-start.2 = (bf16[384,128]{1,0:T(8,128)(2,1)S(1)}, bf16[384,128]{1,0:T(8,128)(2,1)S(1)}, u32[]{:S(2)}, u32[]{:S(2)}) collective-permute-start(bf16[384,128]{1,0:T(8,128)(2,1)S(1)} %bitcast.13), channel_id=1, source_target_pairs={{1,0},{2,1},{3,2},{4,3},{5,4},{6,5},{7,6},{9,8},{10,9},{11,10},{12... | collective-permute-start | bytes 294920 | tf_op jit(solution)/shard_map/ppermute | solution.py:264
  12.4 0.1 collective-permute-done.taken
  12.5 1.0 %shard_map.94 = bf16[8,112,256]{2,1,0:T(8,128)(2,1)} custom-call(bf16[48,256]{1,0:T(8,128)(2,1)S(1)} %bitcast.11, bf16[928,128]{1,0:T(8,128)(2,1)S(1)} %collective-permute-done.taken, bf16[256,256]{1,0:T(8,128)(2,1)S(1)} %copy-done.1), custom_call_target="tpu_custom_call" | custom-call | bytes 1000000 | tf_op jit(solution)/shard_map/pallas_call | solution.py:286
  13.5 6.7 %all-to-all-start = ((bf16[8,112,256]{2,1,0:T(8,128)(2,1)}), bf16[8,112,256]{2,1,0:T(8,128)(2,1)S(1)}, u32[]{:S(2)}, u32[]{:S(2)}) async-start(bf16[8,112,256]{2,1,0:T(8,128)(2,1)} %shard_map.94), calls=%async_computation | async-start | bytes 917504 | tf_op jit(solution)/shard_map/all_to_all | solution.py:287
  20.2 3.5 %shard_map.95 = (f32[768,128]{1,0:T(8,128)S(1)}, bf16[768,128]{1,0:T(8,128)(2,1)S(1)}, bf16[384,128]{1,0:T(8,128)(2,1)S(1)}, bf16[384,128]{1,0:T(8,128)(2,1)S(1)}, f32[128,128]{1,0:T(8,128)S(1)}) custom-call(bf16[928,128]{1,0:T(8,128)(2,1)S(1)} %collective-permute-done.taken, bf16[768,128]{1,0:T(8,128)(2,1)S(1)} %bitcast.9, ...), custom_call_target="tpu_custom_call" | custom-call | flops 20000000000 | bytes 4000000 | tf_op jit(solution)/shard_map/pallas_call | solution.py:288
  23.7 3.1 %all-to-all-done.bands = bf16[8,112,256]{2,1,0:T(8,128)(2,1)S(1)} async-done(((bf16[8,112,256]{2,1,0:T(8,128)(2,1)}), bf16[8,112,256]{2,1,0:T(8,128)(2,1)S(1)}, u32[]{:S(2)}, u32[]{:S(2)}) %all-to-all-start) | async-done | bytes 458784 | tf_op jit(solution)/shard_map/all_to_all | solution.py:287
  26.7 2.2 %shard_map.96 = (bf16[48,256]{1,0:T(8,128)(2,1)S(1)}, f32[864,128]{1,0:T(8,128)S(1)}, bf16[32,20,128]{2,1,0:T(8,128)(2,1)}) custom-call(bf16[8,112,256]{2,1,0:T(8,128)(2,1)S(1)} %all-to-all-done.bands, bf16[48,256]{1,0:T(8,128)(2,1)S(1)} %bitcast.12, bf16[928,128]{1,0:T(8,128)(2,1)S(1)} %collective-permute-done.taken, ...), custom_call_target="tpu_custom_call" | custom-call | flops 3000000000 | bytes 2000000 | tf_op jit(solution)/shard_map/pallas_call | solution.py:303
  28.9 15.9 %all-to-all-start.1 = ((bf16[32,20,128]{2,1,0:T(8,128)(2,1)}), bf16[32,20,128]{2,1,0:T(8,128)(2,1)S(1)}, u32[]{:S(2)}, u32[]{:S(2)}) async-start(bf16[32,20,128]{2,1,0:T(8,128)(2,1)} %get-tuple-element.25), calls=%async_computation.1 | async-start | bytes 393216 | tf_op jit(solution)/shard_map/all_to_all | solution.py:314
  44.8 2.3 %collective-permute-start.3 = (f32[864,128]{1,0:T(8,128)S(1)}, f32[864,128]{1,0:T(8,128)S(1)}, u32[]{:S(2)}, u32[]{:S(2)}) collective-permute-start(f32[864,128]{1,0:T(8,128)S(1)} %get-tuple-element.18), channel_id=1, source_target_pairs={{0,504},{1,505},{2,506},{3,507},{4,508},{5,509},{6,510},{7,511},{8... | collective-permute-start | bytes 1327112 | tf_op jit(solution)/shard_map/ppermute | solution.py:264
  47.1 1.3 %all-to-all-done.1.parts = bf16[32,20,128]{2,1,0:T(8,128)(2,1)S(1)} async-done(((bf16[32,20,128]{2,1,0:T(8,128)(2,1)}), bf16[32,20,128]{2,1,0:T(8,128)(2,1)S(1)}, u32[]{:S(2)}, u32[]{:S(2)}) %all-to-all-start.1) | async-done | bytes 163872 | tf_op jit(solution)/shard_map/all_to_all | solution.py:314
  48.4 0.7 shard_map.98
  49.1 11.7 %all-to-all-start.2 = ((bf16[16,20,128]{2,1,0:T(8,128)(2,1)}), bf16[16,20,128]{2,1,0:T(8,128)(2,1)S(1)}, u32[]{:S(2)}, u32[]{:S(2)}) async-start(bf16[16,20,128]{2,1,0:T(8,128)(2,1)} %shard_map.98), calls=%async_computation.2 | async-start | bytes 196608 | tf_op jit(solution)/shard_map/all_to_all | solution.py:316
  60.7 2.9 %collective-permute-start.4 = (bf16[384,128]{1,0:T(8,128)(2,1)S(1)}, bf16[384,128]{1,0:T(8,128)(2,1)S(1)}, u32[]{:S(2)}, u32[]{:S(2)}) collective-permute-start(bf16[384,128]{1,0:T(8,128)(2,1)S(1)} %get-tuple-element.20), channel_id=1, source_target_pairs={{0,1},{1,2},{2,3},{3,4},{4,5},{5,6},{6,7},{8,9},{9,10},{10,11},{11... | collective-permute-start | bytes 294920 | tf_op jit(solution)/shard_map/ppermute | solution.py:264
  63.7 1.3 %collective-permute-start.5 = (bf16[384,128]{1,0:T(8,128)(2,1)S(1)}, bf16[384,128]{1,0:T(8,128)(2,1)S(1)}, u32[]{:S(2)}, u32[]{:S(2)}) collective-permute-start(bf16[384,128]{1,0:T(8,128)(2,1)S(1)} %get-tuple-element.21), channel_id=1, source_target_pairs={{1,0},{2,1},{3,2},{4,3},{5,4},{6,5},{7,6},{9,8},{10,9},{11,10},{12... | collective-permute-start | bytes 294920 | tf_op jit(solution)/shard_map/ppermute | solution.py:264
  65.0 1.1 %all-to-all-done.2.parts = bf16[16,20,128]{2,1,0:T(8,128)(2,1)S(1)} async-done(((bf16[16,20,128]{2,1,0:T(8,128)(2,1)}), bf16[16,20,128]{2,1,0:T(8,128)(2,1)S(1)}, u32[]{:S(2)}, u32[]{:S(2)}) %all-to-all-start.2) | async-done | bytes 81952 | tf_op jit(solution)/shard_map/all_to_all | solution.py:316
  66.1 0.7 shard_map.99
  66.8 9.6 %all-to-all-start.3 = ((bf16[32,20,128]{2,1,0:T(8,128)(2,1)}), bf16[32,20,128]{2,1,0:T(8,128)(2,1)S(1)}, u32[]{:S(2)}, u32[]{:S(2)}) async-start(bf16[32,20,128]{2,1,0:T(8,128)(2,1)} %shard_map.99), calls=%async_computation.3 | async-start | bytes 393216 | tf_op jit(solution)/shard_map/all_to_all | solution.py:318
  76.5 0.9 %shard_map.97 = (bf16[768,128]{1,0:T(8,128)(2,1)}, bf16[48,256]{1,0:T(8,128)(2,1)}) custom-call(f32[864,128]{1,0:T(8,128)S(1)} %collective-permute-done.3.returned, bf16[768,128]{1,0:T(8,128)(2,1)S(1)} %get-tuple-element.19.middle, bf16[384,128]{1,0:T(8,128)(2,1)S(1)} %collective-permute-done.4.from_above, ...), custom_call_target="tpu_custom_call" | custom-call | flops 20000000000 | bytes 1000000 | tf_op jit(solution)/shard_map/pallas_call | solution.py:322
  77.4 2.6 %all-to-all-done.3.parts = bf16[32,20,128]{2,1,0:T(8,128)(2,1)S(1)} async-done(((bf16[32,20,128]{2,1,0:T(8,128)(2,1)}), bf16[32,20,128]{2,1,0:T(8,128)(2,1)S(1)}, u32[]{:S(2)}, u32[]{:S(2)}) %all-to-all-start.3) | async-done | bytes 163872 | tf_op jit(solution)/shard_map/all_to_all | solution.py:318
  80.0 0.7 shard_map.100
  (13 shorter events, 0.0 us)
Async XLA Ops:
  0.6 8.1 %copy-start = (bf16[1,8,96,128]{3,2,1,0:T(8,128)(2,1)S(1)}, bf16[1,8,96,128]{3,2,1,0:T(8,128)(2,1)}, u32[]{:S(2)}) copy-start(bf16[1,8,96,128]{3,2,1,0:T(8,128)(2,1)} %param.7) | copy-start | bytes 589828
  2.4 10.1 %copy-start.1 = (bf16[256,256]{1,0:T(8,128)(2,1)S(1)}, bf16[256,256]{1,0:T(8,128)(2,1)}, u32[]{:S(2)}) copy-start(bf16[256,256]{1,0:T(8,128)(2,1)} %coarse_weight.1) | copy-start | bytes 393220
  2.4 10.1 %collective-permute-start = (bf16[928,128]{1,0:T(8,128)(2,1)}, bf16[928,128]{1,0:T(8,128)(2,1)S(1)}, u32[]{:S(2)}, u32[]{:S(2)}) collective-permute-start(bf16[928,128]{1,0:T(8,128)(2,1)} %shard_map.93), channel_id=1, source_target_pairs={{0,8},{1,9},{2,10},{3,11},{4,12},{5,13},{6,14},{7,15},{8,16},{9,17... | collective-permute-start | bytes 712712 | tf_op jit(solution)/shard_map/ppermute | solution.py:264
  8.8 3.8 %copy-start.2 = (bf16[1,2,24,256]{3,2,1,0:T(8,128)(2,1)S(1)}, bf16[1,2,24,256]{3,2,1,0:T(8,128)(2,1)}, u32[]{:S(2)}) copy-start(bf16[1,2,24,256]{3,2,1,0:T(8,128)(2,1)} %param.6) | copy-start | bytes 73732
  8.8 11.3 %collective-permute-start.1 = (bf16[384,128]{1,0:T(8,128)(2,1)S(1)}, bf16[384,128]{1,0:T(8,128)(2,1)S(1)}, u32[]{:S(2)}, u32[]{:S(2)}) collective-permute-start(bf16[384,128]{1,0:T(8,128)(2,1)S(1)} %bitcast.14), channel_id=1, source_target_pairs={{0,1},{1,2},{2,3},{3,4},{4,5},{5,6},{6,7},{8,9},{9,10},{10,11},{11... | collective-permute-start | bytes 294920 | tf_op jit(solution)/shard_map/ppermute | solution.py:264
  11.1 9.0 %collective-permute-start.2 = (bf16[384,128]{1,0:T(8,128)(2,1)S(1)}, bf16[384,128]{1,0:T(8,128)(2,1)S(1)}, u32[]{:S(2)}, u32[]{:S(2)}) collective-permute-start(bf16[384,128]{1,0:T(8,128)(2,1)S(1)} %bitcast.13), channel_id=1, source_target_pairs={{1,0},{2,1},{3,2},{4,3},{5,4},{6,5},{7,6},{9,8},{10,9},{11,10},{12... | collective-permute-start | bytes 294920 | tf_op jit(solution)/shard_map/ppermute | solution.py:264
  13.5 6.7 %copy-start.3 = (bf16[128,128]{1,0:T(8,128)(2,1)S(1)}, bf16[128,128]{1,0:T(8,128)(2,1)}, u32[]{:S(2)}) copy-start(bf16[128,128]{1,0:T(8,128)(2,1)} %weight.5) | copy-start | bytes 98308
  13.5 13.2 %all-to-all-start = ((bf16[8,112,256]{2,1,0:T(8,128)(2,1)}), bf16[8,112,256]{2,1,0:T(8,128)(2,1)S(1)}, u32[]{:S(2)}, u32[]{:S(2)}) async-start(bf16[8,112,256]{2,1,0:T(8,128)(2,1)} %shard_map.94), calls=%async_computation | async-start | bytes 917504 | tf_op jit(solution)/shard_map/all_to_all | solution.py:287
  28.9 19.5 %all-to-all-start.1 = ((bf16[32,20,128]{2,1,0:T(8,128)(2,1)}), bf16[32,20,128]{2,1,0:T(8,128)(2,1)S(1)}, u32[]{:S(2)}, u32[]{:S(2)}) async-start(bf16[32,20,128]{2,1,0:T(8,128)(2,1)} %get-tuple-element.25), calls=%async_computation.1 | async-start | bytes 393216 | tf_op jit(solution)/shard_map/all_to_all | solution.py:314
  44.8 31.7 %collective-permute-start.3 = (f32[864,128]{1,0:T(8,128)S(1)}, f32[864,128]{1,0:T(8,128)S(1)}, u32[]{:S(2)}, u32[]{:S(2)}) collective-permute-start(f32[864,128]{1,0:T(8,128)S(1)} %get-tuple-element.18), channel_id=1, source_target_pairs={{0,504},{1,505},{2,506},{3,507},{4,508},{5,509},{6,510},{7,511},{8... | collective-permute-start | bytes 1327112 | tf_op jit(solution)/shard_map/ppermute | solution.py:264
  49.1 17.0 %all-to-all-start.2 = ((bf16[16,20,128]{2,1,0:T(8,128)(2,1)}), bf16[16,20,128]{2,1,0:T(8,128)(2,1)S(1)}, u32[]{:S(2)}, u32[]{:S(2)}) async-start(bf16[16,20,128]{2,1,0:T(8,128)(2,1)} %shard_map.98), calls=%async_computation.2 | async-start | bytes 196608 | tf_op jit(solution)/shard_map/all_to_all | solution.py:316
  60.7 15.7 %collective-permute-start.4 = (bf16[384,128]{1,0:T(8,128)(2,1)S(1)}, bf16[384,128]{1,0:T(8,128)(2,1)S(1)}, u32[]{:S(2)}, u32[]{:S(2)}) collective-permute-start(bf16[384,128]{1,0:T(8,128)(2,1)S(1)} %get-tuple-element.20), channel_id=1, source_target_pairs={{0,1},{1,2},{2,3},{3,4},{4,5},{5,6},{6,7},{8,9},{9,10},{10,11},{11... | collective-permute-start | bytes 294920 | tf_op jit(solution)/shard_map/ppermute | solution.py:264
  63.7 12.8 %collective-permute-start.5 = (bf16[384,128]{1,0:T(8,128)(2,1)S(1)}, bf16[384,128]{1,0:T(8,128)(2,1)S(1)}, u32[]{:S(2)}, u32[]{:S(2)}) collective-permute-start(bf16[384,128]{1,0:T(8,128)(2,1)S(1)} %get-tuple-element.21), channel_id=1, source_target_pairs={{1,0},{2,1},{3,2},{4,3},{5,4},{6,5},{7,6},{9,8},{10,9},{11,10},{12... | collective-permute-start | bytes 294920 | tf_op jit(solution)/shard_map/ppermute | solution.py:264
  66.8 13.2 %all-to-all-start.3 = ((bf16[32,20,128]{2,1,0:T(8,128)(2,1)}), bf16[32,20,128]{2,1,0:T(8,128)(2,1)S(1)}, u32[]{:S(2)}, u32[]{:S(2)}) async-start(bf16[32,20,128]{2,1,0:T(8,128)(2,1)} %shard_map.99), calls=%async_computation.3 | async-start | bytes 393216 | tf_op jit(solution)/shard_map/all_to_all | solution.py:318
